TPU v7x, 32 devices: a whole 2x2x4 slice. The times are simulated.
32 devices in a mesh: groups: 2 (over y), seq: 8 (over z, x), head: 2 (over core).
Axes of the slice: x: 2, y: 2, z: 4, core: 2. Of those that a mesh axis runs over, the one named last changes fastest.
Arguments:
- queries: bfloat16 [256, 3072], P(('groups', 'seq'), 'head'), parts along dimension 0, may hold values from -300 to 300, as said below
- latent: bfloat16 [512, 256], P(None, ('groups', 'seq')), parts along dimension 1, may hold values from -6 to 6
- key_basis: bfloat16 [512, 3072], P(None, 'head'), may hold values from -0.25 to 0.25
- value_basis: bfloat16 [512, 3072], P(None, 'head'), may hold values from -0.25 to 0.25
- out_weight: bfloat16 [3072, 3072], P('seq', 'head'), may hold values from -0.625 to 0.625
Outputs:
- attended: bfloat16 [256, 3072], P(('groups', 'seq'), 'head'), parts along dimension 0
There are 2 independent parts, one for each index of `groups`. A program takes and returns all parts, laid end to end along the dimension named above; an argument that names none is the same for every part. Nothing has to cross between parts.
Inputs may be any that keep to these rules, and one draw needn't show every extreme that they name: `queries`: real-valued entries.
All inputs are finite; a program needn't handle non-finite values.
Results may differ from a plain program's by a relative error of at most 0.0099.
Values may be sent and summed in bfloat16 or wider, within the bound.
No kernel may reach another device: no remote copies, remote signals or barrier semaphores. Data moves between devices by JAX's collectives and lax.ppermute only.
A program may use at most 64 MiB of HBM per device.

v0:
```python
import math

import jax
import jax.numpy as jnp
from jax import lax
from jax.sharding import PartitionSpec as P

HEAD_DIM = 128


def attend(queries, latent, key_basis, value_basis):
    tok_rows = queries.shape[0]
    head_count = key_basis.shape[1] // HEAD_DIM
    rank_count = key_basis.shape[0]
    score_scale = 1.0 / math.sqrt(HEAD_DIM)
    query_heads = queries.reshape(tok_rows, head_count, HEAD_DIM).transpose(1, 0, 2)
    key_maps = key_basis.reshape(rank_count, head_count, HEAD_DIM).transpose(1, 0, 2)
    value_maps = value_basis.reshape(rank_count, head_count, HEAD_DIM).transpose(1, 0, 2)

    def one_head(operands):
        query_one, key_map, value_map = operands
        key_rows = lax.dot_general(
            latent, key_map, (((0,), (0,)), ((), ())), preferred_element_type=jnp.float32
        ).astype(jnp.bfloat16)
        value_rows = lax.dot_general(
            latent, value_map, (((0,), (0,)), ((), ())), preferred_element_type=jnp.float32
        ).astype(jnp.bfloat16)
        scores = (
            lax.dot_general(
                query_one, key_rows, (((1,), (1,)), ((), ())), preferred_element_type=jnp.float32
            )
            * score_scale
        )
        row_max = jnp.max(scores, axis=1, keepdims=True)
        weights = jnp.exp(scores - row_max)
        row_total = jnp.sum(weights, axis=1, keepdims=True)
        head_mixed = (
            jnp.dot(weights.astype(jnp.bfloat16), value_rows, preferred_element_type=jnp.float32)
            / row_total
        )
        return head_mixed.astype(jnp.bfloat16)

    mixed = lax.map(one_head, (query_heads, key_maps, value_maps))
    return mixed.transpose(1, 0, 2).reshape(tok_rows, head_count * HEAD_DIM)


def shards(queries, latent, key_basis, value_basis, out_weight):
    gathered = lax.all_gather(latent, "seq", axis=1, tiled=True)
    attended_heads = attend(queries, gathered, key_basis, value_basis)
    partial_value = lax.dot_general(
        attended_heads,
        lax.all_gather(out_weight, "seq", axis=0, tiled=True),
        (((1,), (1,)), ((), ())),
        preferred_element_type=jnp.float32,
    )
    attended = lax.psum_scatter(partial_value, "head", scatter_dimension=1, tiled=True).astype(
        jnp.bfloat16
    )
    return attended


def solution(mesh):
    placed = (
        P(("groups", "seq"), "head"),
        P(None, ("groups", "seq")),
        P(None, "head"),
        P(None, "head"),
        P("seq", "head"),
    )
    return jax.shard_map(
        shards, mesh=mesh, in_specs=placed, out_specs=P(("groups", "seq"), "head"), check_vma=False
    )
```

profile of v0, /device:TPU:1, one launch (start us, length us, event | category | flops | bytes accessed | tf_op | source)
XLA Modules:
  0.0 171.9 jit_solution(4047523913537241126)
XLA Ops:
  6.5 0.0 all-gather.2.cloned.1.call-start
  6.5 0.7 all-gather.2.cloned.1.call-update
  7.3 0.0 reduce-scatter.2.cloned.1.call-start
  7.3 1.7 copy.14
  9.0 0.0 copy-start.1
  9.0 0.0 copy-start
  9.1 1.7 %copy.15 = bf16[512,1536]{0,1:T(8,128)(2,1)S(1)} copy(bf16[512,1536]{1,0:T(8,128)(2,1)} %param.10) | data formatting | bytes 3145728 | tf_op args[3]
  10.8 0.0 copy-done.1
  10.8 26.4 %all_gather.6 = bf16[512,128]{0,1:T(8,128)(2,1)S(1)} all-gather(bf16[512,16]{0,1:T(8,128)(2,1)S(1)} %copy-done.1), channel_id=1, replica_groups=mesh['groups'=2,'seq'=8,'head'=2] {'seq'}, dimensions={1}, use_global_device_ids=true | all-gather | bytes 147456 | tf_op jit(solution)/shard_map/all_gather | solution.py:48
  37.2 0.1 copy.18
  37.3 0.0 copy-done
  37.3 0.1 reshape.14
  37.4 10.8 %while.10 = (s32[]{:T(128)}, bf16[12,16,128]{2,1,0:T(8,128)(2,1)S(1)}, bf16[12,16,128]{2,1,0:T(8,128)(2,1)S(1)}, bf16[12,512,128]{1,2,0:T(8,128)(2,1)S(1)}, bf16...) while((s32[]{:T(128)}, bf16[12,16,128]{2,1,0:T(8,128)(2,1)S(1)}, ...), condition=%wide.region_3.4_spmd, body=%wide.region_0.3_spmd.sunk | while | flops 34652128 | bytes 560397 | solution.py:43
  37.4 0.4 fusion.48
  37.8 0.2 fusion.49
  38.0 0.3 fusion.50
  38.3 0.4 fusion.48
  38.7 0.2 fusion.49
  38.9 0.3 fusion.50
  39.2 0.4 fusion.48
  39.6 0.2 fusion.49
  39.8 0.3 fusion.50
  40.1 0.4 fusion.48
  40.5 0.2 fusion.49
  40.7 0.3 fusion.50
  41.0 0.4 fusion.48
  41.4 0.2 fusion.49
  41.6 0.3 fusion.50
  41.9 0.4 fusion.48
  42.3 0.2 fusion.49
  42.5 0.3 fusion.50
  42.8 0.4 fusion.48
  43.2 0.2 fusion.49
  43.4 0.3 fusion.50
  43.7 0.4 fusion.48
  44.1 0.2 fusion.49
  44.3 0.3 fusion.50
  44.6 0.4 fusion.48
  45.0 0.2 fusion.49
  45.2 0.3 fusion.50
  45.5 0.4 fusion.48
  45.9 0.2 fusion.49
  46.1 0.3 fusion.50
  46.4 0.4 fusion.48
  46.8 0.2 fusion.49
  47.0 0.3 fusion.50
  47.3 0.4 fusion.48
  47.7 0.2 fusion.49
  47.9 0.3 fusion.50
  48.2 101.7 %all-gather.2.cloned.1.call-done = bf16[3072,1536]{1,0:T(8,128)(2,1)} async-done(((bf16[384,1536]{1,0:T(8,128)(2,1)}), bf16[3072,1536]{1,0:T(8,128)(2,1)}) %all-gather.2.cloned.1.call-update) | async-done | bytes 9437200 | tf_op jit(solution)/shard_map/all_gather | solution.py:52
  150.0 6.9 %fusion.25 = f32[16,3072]{1,0:T(8,128)} fusion(bf16[3072,1536]{1,0:T(8,128)(2,1)} %all-gather.2.cloned.1.call-done, bf16[12,16,128]{2,1,0:T(8,128)(2,1)S(1)} %get-tuple-element.37), kind=kOutput, calls=%fused_computation.21 | convolution fusion | flops 150994944 | bytes 9682944 | tf_op jit(solution)/shard_map/dot_general | solution.py:50
  156.9 0.0 reduce-scatter.2.cloned.1.call-update
  156.9 6.7 %reduce-scatter.2.cloned.1.call-done = f32[16,1536]{1,0:T(8,128)} async-done(((f32[16,3072]{1,0:T(8,128)}), f32[16,1536]{1,0:T(8,128)}) %reduce-scatter.2.cloned.1.call-update) | async-done | bytes 98320 | tf_op jit(solution)/shard_map/reduce_scatter | solution.py:56
  163.6 1.5 convert_element_type.17
  (2 shorter events, 0.0 us)
Async XLA Ops:
  6.5 143.4 %all-gather.2.cloned.1.call-start = ((), (), s32[]{:S(2)}) async-start(), calls=%async_computation.1 | async-start | bytes 10616832 | tf_op jit(solution)/shard_map/all_gather | solution.py:52
  7.3 156.3 %reduce-scatter.2.cloned.1.call-start = ((), (), s32[]{:S(2)}) async-start(), calls=%async_computation.2 | async-start | bytes 294912 | tf_op jit(solution)/shard_map/reduce_scatter | solution.py:56
  9.0 1.8 %copy-start.1 = (bf16[512,16]{0,1:T(8,128)(2,1)S(1)}, bf16[512,16]{0,1:T(8,128)(2,1)}, u32[]{:S(2)}) copy-start(bf16[512,16]{0,1:T(8,128)(2,1)} %param.8) | copy-start | bytes 49156
  9.0 28.3 %copy-start = (bf16[16,1536]{1,0:T(8,128)(2,1)S(1)}, bf16[16,1536]{1,0:T(8,128)(2,1)}, u32[]{:S(2)}) copy-start(bf16[16,1536]{1,0:T(8,128)(2,1)} %param.7) | copy-start | bytes 147460
Sparse Core Ops, SparseCore 0:
  9.5 140.3 all-gather.1
  157.0 6.4 reduce-scatter.1
where the time goes:
time: 172 us
  waiting for transfers between devices  109 us (63%)
  blocking collectives  26.4 us (15%)
  matrix products  15.4 us (9%)
  between operations  13.5 us (8%)
  other arithmetic  3.78 us (2%)
  local copies, waits for them, and re-layouts  3.65 us (2%)
    all_gather x1, waiting for transfers between devices, shards(): lax.all_gather(out_weight, 'seq', axis=0, tiled=True)  102 us
    all_gather x1, blocking collectives, shards(): gathered = lax.all_gather(latent, 'seq', axis=1, tiled=True)  26.4 us
    dot_general x1, matrix products, shards(): lax.dot_general(attended_heads, lax.all_gather(out_weight, 'seq', axis=0,...  6.91 us
    reduce_scatter x1, waiting for transfers between devices, shards(): lax.psum_scatter(partial_value, 'head', scatter_dimension=1, tiled=True)  6.66 us
    dot_general x12, matrix products, one_head(): lax.dot_general(query_one, key_rows, (((1,), (1,)), ((), ())), preferred_...  4.84 us
    dot_general x12, matrix products, one_head(): jnp.dot(weights.astype(jnp.bfloat16), value_rows, preferred_element_type=...  3.64 us
    unnamed x6, local copies, waits for them, and re-layouts  3.46 us
  transfers between devices with their start and end apart: 2, of which 2 were waited for; matrix products, arithmetic and copies ran while one was open for 8% of the time, Pallas kernels for 0%

commit v1 on v0

--- a/solution.py
+++ b/solution.py
@@ -1,11 +1,118 @@
+import functools
 import math
 
 import jax
 import jax.numpy as jnp
 from jax import lax
+from jax.experimental import pallas as pl
+from jax.experimental.pallas import tpu as pltpu
 from jax.sharding import PartitionSpec as P
 
 HEAD_DIM = 128
+MOST_DIRECT = 16
+NT = (((1,), (1,)), ((), ()))
+
+
+def mix_kernel(count, *refs):
+    blocks = refs[:count]
+    key_basis, value_basis, out_weight, keep, send, mixed, partial_sum = refs[count:]
+    width = key_basis.shape[1]
+    queries = jnp.concatenate([b[:, :width] for b in blocks], axis=0)
+    latent = jnp.concatenate([b[:, width:] for b in blocks], axis=0)
+    scale = 1.0 / math.sqrt(HEAD_DIM)
+    for first in range(0, width, HEAD_DIM):
+        cols = slice(first, first + HEAD_DIM)
+        keys = jnp.dot(latent, key_basis[:, cols], preferred_element_type=jnp.float32)
+        values = jnp.dot(latent, value_basis[:, cols], preferred_element_type=jnp.float32)
+        scores = (
+            lax.dot_general(
+                queries[:, cols], keys.astype(jnp.bfloat16), NT, preferred_element_type=jnp.float32
+            )
+            * scale
+        )
+        weights = jnp.exp(scores - jnp.max(scores, axis=1, keepdims=True))
+        totals = jnp.sum(weights, axis=1, keepdims=True)
+        head = jnp.dot(
+            weights.astype(jnp.bfloat16),
+            values.astype(jnp.bfloat16),
+            preferred_element_type=jnp.float32,
+        )
+        mixed[:, cols] = (head / totals).astype(jnp.bfloat16)
+    partial_sum[...] = lax.dot_general(
+        mixed[...], out_weight[...], NT, preferred_element_type=jnp.float32
+    )
+    rows = keep.shape[0]
+    core = lax.axis_index("head")
+    keep[...] = partial_sum[pl.ds(pl.multiple_of(core * rows, rows), rows), :]
+    send[...] = partial_sum[pl.ds(pl.multiple_of((1 - core) * rows, rows), rows), :]
+
+
+def mix(blocks, key_basis, value_basis, out_weight):
+    rows = sum(b.shape[0] for b in blocks)
+    width, features = key_basis.shape[1], out_weight.shape[0]
+    half = jax.ShapeDtypeStruct((rows // 2, features), jnp.float32)
+    vmem = pl.BlockSpec(memory_space=pltpu.VMEM)
+    rank = key_basis.shape[0]
+    return pl.pallas_call(
+        functools.partial(mix_kernel, len(blocks)),
+        out_shape=(half, half),
+        in_specs=[vmem] * (len(blocks) + 3),
+        out_specs=(vmem, vmem),
+        scratch_shapes=[
+            pltpu.VMEM((rows, width), jnp.bfloat16),
+            pltpu.VMEM((rows, features), jnp.float32),
+        ],
+        cost_estimate=pl.CostEstimate(
+            flops=2 * rows * width * (2 * rank + 2 * rows + features),
+            bytes_accessed=2 * width * (2 * rank + features),
+            transcendentals=rows * rows * (width // HEAD_DIM),
+        ),
+        compiler_params=pltpu.CompilerParams(vmem_limit_bytes=32 * 1024 * 1024),
+        name="mix",
+    )(*blocks, key_basis, value_basis, out_weight)
+
+
+def place_kernel(half, *refs):
+    parts, out = refs[:-1], refs[-1]
+    features = parts[0].shape[1]
+    mine = lax.rem(lax.axis_index("seq"), half)
+    for step, part in enumerate(parts):
+        column = jnp.bitwise_xor(mine, step) * features
+        out[:, pl.ds(pl.multiple_of(column, features), features)] = part[...]
+
+
+def place(parts, half):
+    rows, features = parts[0].shape
+    vmem = pl.BlockSpec(memory_space=pltpu.VMEM)
+    return pl.pallas_call(
+        functools.partial(place_kernel, half),
+        out_shape=jax.ShapeDtypeStruct((rows, features * half), parts[0].dtype),
+        in_specs=[vmem] * len(parts),
+        out_specs=vmem,
+        name="place",
+    )(*parts)
+
+
+def direct(count, queries, latent, key_basis, value_basis, out_weight):
+    rows, half = queries.shape[0], count // 2
+    own = jnp.concatenate([queries, latent.T], axis=1)
+    blocks = {0: own}
+    for flip in reversed(range(1, count)):
+        blocks[flip] = lax.ppermute(own, "seq", [(i, i ^ flip) for i in range(count)])
+    keep, send = mix([blocks[k] for k in range(count)], key_basis, value_basis, out_weight)
+    other = lax.ppermute(send, "head", [(0, 1), (1, 0)])
+    total = (keep + other).astype(jnp.bfloat16)
+    parts = [None] * half
+    for step in reversed(range(half)):
+        pairs = [
+            (2 * s + h, 2 * (s ^ (step + h * half)) + s // half)
+            for s in range(count)
+            for h in range(2)
+        ]
+        parts[step] = lax.ppermute(
+            total[step * rows : (step + 1) * rows], ("seq", "head"), pairs
+        )
+    return place(parts, half)
 
 
 def attend(queries, latent, key_basis, value_basis):
@@ -26,9 +133,7 @@
             latent, value_map, (((0,), (0,)), ((), ())), preferred_element_type=jnp.float32
         ).astype(jnp.bfloat16)
         scores = (
-            lax.dot_general(
-                query_one, key_rows, (((1,), (1,)), ((), ())), preferred_element_type=jnp.float32
-            )
+            lax.dot_general(query_one, key_rows, NT, preferred_element_type=jnp.float32)
             * score_scale
         )
         row_max = jnp.max(scores, axis=1, keepdims=True)
@@ -44,19 +149,14 @@
     return mixed.transpose(1, 0, 2).reshape(tok_rows, head_count * HEAD_DIM)
 
 
-def shards(queries, latent, key_basis, value_basis, out_weight):
-    gathered = lax.all_gather(latent, "seq", axis=1, tiled=True)
-    attended_heads = attend(queries, gathered, key_basis, value_basis)
-    partial_value = lax.dot_general(
-        attended_heads,
-        lax.all_gather(out_weight, "seq", axis=0, tiled=True),
-        (((1,), (1,)), ((), ())),
-        preferred_element_type=jnp.float32,
-    )
-    attended = lax.psum_scatter(partial_value, "head", scatter_dimension=1, tiled=True).astype(
+def gathered(queries, latent, key_basis, value_basis, out_weight):
+    latent = lax.all_gather(latent, "seq", axis=1, tiled=True)
+    mixed = attend(queries, latent, key_basis, value_basis)
+    weight = lax.all_gather(out_weight, "seq", axis=0, tiled=True)
+    partial_value = lax.dot_general(mixed, weight, NT, preferred_element_type=jnp.float32)
+    return lax.psum_scatter(partial_value, "head", scatter_dimension=1, tiled=True).astype(
         jnp.bfloat16
     )
-    return attended
 
 
 def solution(mesh):
@@ -67,6 +167,9 @@
         P(None, "head"),
         P("seq", "head"),
     )
+    count = mesh.shape["seq"]
+    pairwise = 2 <= count <= MOST_DIRECT and count & (count - 1) == 0 and mesh.shape["head"] == 2
+    shards = functools.partial(direct, count) if pairwise else gathered
     return jax.shard_map(
         shards, mesh=mesh, in_specs=placed, out_specs=P(("groups", "seq"), "head"), check_vma=False
     )

time: 172 us -> 41.8 us (0.24)
  waiting for transfers between devices: 109 us -> 9.7 us
  blocking collectives: 26.4 us -> 0 us
  starting transfers between devices: 0.04 us -> 19.7 us
  matrix products: 15.4 us -> 0 us
  between operations: 13.5 us -> 0.08 us
  Pallas kernels: 0 us -> 6.45 us
  other arithmetic: 3.78 us -> 0.83 us
    all_gather x1 -> x0, waiting for transfers between devices: 102 us -> none  [shards(): lax.all_gather(out_weight, 'seq', axis=0, tiled=True)]
    all_gather x1 -> x0, blocking collectives: 26.4 us -> none  [shards(): gathered = lax.all_gather(latent, 'seq', axis=1, tiled=True)]
    ppermute x0 -> x12, starting transfers between devices: none -> 19.7 us  [the longest x7 10.1 us: direct(): lax.ppermute(own, 'seq', [(i, i ^ flip) for i in range(count)])]
    dot_general x25 -> x0, matrix products: 15.4 us -> none  [the longest x1 6.91 us: shards(): lax.dot_general(attended_heads, lax.all_gather(out_weight, 'seq', axis=0,...]
    ppermute x0 -> x12, waiting for transfers between devices: none -> 9.7 us  [the longest x7 6.04 us: direct(): lax.ppermute(own, 'seq', [(i, i ^ flip) for i in range(count)])]
    reduce_scatter x1 -> x0, waiting for transfers between devices: 6.66 us -> none  [shards(): lax.psum_scatter(partial_value, 'head', scatter_dimension=1, tiled=True)]
    pallas_call x0 -> x2, Pallas kernels: none -> 6.45 us  [the longest x1 5.07 us: mix(): pl.pallas_call(functools.partial(mix_kernel, len(blocks)), out_shape=(hal...]
    reduce_sum x12 -> x0, other arithmetic: 2.26 us -> none  [one_head(): row_total = jnp.sum(weights, axis=1, keepdims=True)]
  transfers between devices with their start and end apart: 2 -> 12, of which waited for: 2 -> 7; matrix products, arithmetic and copies ran while one was open for 8% -> 0% of each run, Pallas kernels for 0% -> 0%
where the time goes in v1:
time: 41.8 us; the launch traced here: 41.5 us
  starting transfers between devices  19.7 us (47%)
  waiting for transfers between devices  9.7 us (23%)
  Pallas kernels  6.45 us (15%)
  local copies, waits for them, and re-layouts  4.69 us (11%)
  other arithmetic  0.83 us (2%)
    ppermute x7, starting transfers between devices, direct(): lax.ppermute(own, 'seq', [(i, i ^ flip) for i in range(count)])  10.1 us
    ppermute x4, starting transfers between devices, direct(): lax.ppermute(total[step * rows:(step + 1) * rows], ('seq', 'head'), pairs)  8.05 us
    ppermute x7, waiting for transfers between devices, direct(): lax.ppermute(own, 'seq', [(i, i ^ flip) for i in range(count)])  6.04 us
    pallas_call x1, Pallas kernels, mix(): pl.pallas_call(functools.partial(mix_kernel, len(blocks)), out_shape=(hal...  5.07 us
    unnamed x14, local copies, waits for them, and re-layouts  4.68 us
    ppermute x4, waiting for transfers between devices, direct(): lax.ppermute(total[step * rows:(step + 1) * rows], ('seq', 'head'), pairs)  2.72 us
    ppermute x1, starting transfers between devices, direct(): other = lax.ppermute(send, 'head', [(0, 1), (1, 0)])  1.61 us
    pallas_call x1, Pallas kernels, place(): pl.pallas_call(functools.partial(place_kernel, half), out_shape=jax.Shape...  1.38 us
  transfers between devices with their start and end apart: 12, of which 7 were waited for; matrix products, arithmetic and copies ran while one was open for 0% of the time, Pallas kernels for 0%

profile of v1, /device:TPU:1, one launch (start us, length us, event | category | flops | bytes accessed | tf_op | source)
XLA Modules:
  0.0 41.5 jit_solution(15454824785289941147)
XLA Ops:
  0.0 0.8 %pad_maximum_fusion.refs_0_ = bf16[16,2048]{1,0:T(8,128)(2,1)S(1)} fusion(bf16[16,512]{1,0:T(8,128)(2,1)} %bitcast.1, bf16[16,1536]{1,0:T(8,128)(2,1)} %param.5), kind=kLoop, calls=%fused_computation.1 | loop fusion | flops 131072 | bytes 131072 | tf_op jit(solution)/shard_map/concatenate | solution.py:98
  0.8 5.1 %collective-permute-start.6 = (bf16[16,2048]{1,0:T(8,128)(2,1)S(1)}, bf16[16,2048]{1,0:T(8,128)(2,1)S(1)}, u32[]{:S(2)}, u32[]{:S(2)}) collective-permute-start(bf16[16,2048]{1,0:T(8,128)(2,1)S(1)} %pad_maximum_fusion.refs_0_), channel_id=1, source_target_pairs={{0,14},{2,12},{4,10},{6,8},{8,6},{10,4},{12,2},{14,0},{1,15},{3,13... | collective-permute-start | bytes 196616 | tf_op jit(solution)/shard_map/ppermute | solution.py:101
  5.9 0.0 collective-permute-start.5
  5.9 0.4 %collective-permute-start.4 = (bf16[16,2048]{1,0:T(8,128)(2,1)S(1)}, bf16[16,2048]{1,0:T(8,128)(2,1)S(1)}, u32[]{:S(2)}, u32[]{:S(2)}) collective-permute-start(bf16[16,2048]{1,0:T(8,128)(2,1)S(1)} %pad_maximum_fusion.refs_0_), channel_id=1, source_target_pairs={{0,10},{2,8},{4,14},{6,12},{8,2},{10,0},{12,6},{14,4},{1,11},{3,9}... | collective-permute-start | bytes 196616 | tf_op jit(solution)/shard_map/ppermute | solution.py:101
  6.3 2.0 %collective-permute-start.3 = (bf16[16,2048]{1,0:T(8,128)(2,1)S(1)}, bf16[16,2048]{1,0:T(8,128)(2,1)S(1)}, u32[]{:S(2)}, u32[]{:S(2)}) collective-permute-start(bf16[16,2048]{1,0:T(8,128)(2,1)S(1)} %pad_maximum_fusion.refs_0_), channel_id=1, source_target_pairs={{0,8},{2,10},{4,12},{6,14},{8,0},{10,2},{12,4},{14,6},{1,9},{3,11}... | collective-permute-start | bytes 196616 | tf_op jit(solution)/shard_map/ppermute | solution.py:101
  8.3 2.0 %collective-permute-start.2 = (bf16[16,2048]{1,0:T(8,128)(2,1)S(1)}, bf16[16,2048]{1,0:T(8,128)(2,1)S(1)}, u32[]{:S(2)}, u32[]{:S(2)}) collective-permute-start(bf16[16,2048]{1,0:T(8,128)(2,1)S(1)} %pad_maximum_fusion.refs_0_), channel_id=1, source_target_pairs={{0,6},{2,4},{4,2},{6,0},{8,14},{10,12},{12,10},{14,8},{1,7},{3,5},... | collective-permute-start | bytes 196616 | tf_op jit(solution)/shard_map/ppermute | solution.py:101
  10.4 0.0 collective-permute-done.6.refs_7_
  10.4 0.3 collective-permute-start.1
  10.6 0.3 collective-permute-done.5.refs_6_
  10.9 0.3 collective-permute-start
  11.2 4.2 %collective-permute-done.4.refs_5_ = bf16[16,2048]{1,0:T(8,128)(2,1)S(1)} collective-permute-done((bf16[16,2048]{1,0:T(8,128)(2,1)S(1)}, bf16[16,2048]{1,0:T(8,128)(2,1)S(1)}, u32[]{:S(2)}, u32[]{:S(2)}) %collective-permute-start.4) | collective-permute-done | bytes 65568 | tf_op jit(solution)/shard_map/ppermute | solution.py:101
  15.4 1.5 %collective-permute-done.3.refs_4_ = bf16[16,2048]{1,0:T(8,128)(2,1)S(1)} collective-permute-done((bf16[16,2048]{1,0:T(8,128)(2,1)S(1)}, bf16[16,2048]{1,0:T(8,128)(2,1)S(1)}, u32[]{:S(2)}, u32[]{:S(2)}) %collective-permute-start.3) | collective-permute-done | bytes 65568 | tf_op jit(solution)/shard_map/ppermute | solution.py:101
  16.9 0.0 collective-permute-done.2.refs_3_
  16.9 0.0 collective-permute-done.1.refs_2_
  16.9 0.0 collective-permute-done.refs_1_
  16.9 0.0 copy-start
  16.9 1.4 %copy-done = bf16[512,1536]{1,0:T(8,128)(2,1)S(1)} copy-done((bf16[512,1536]{1,0:T(8,128)(2,1)S(1)}, bf16[512,1536]{1,0:T(8,128)(2,1)}, u32[]{:S(2)}) %copy-start) | copy-done | bytes 1572888
  18.3 0.0 copy-start.1
  18.3 1.4 %copy-done.1 = bf16[512,1536]{1,0:T(8,128)(2,1)S(1)} copy-done((bf16[512,1536]{1,0:T(8,128)(2,1)S(1)}, bf16[512,1536]{1,0:T(8,128)(2,1)}, u32[]{:S(2)}) %copy-start.1) | copy-done | bytes 1572888
  19.8 0.0 copy-start.2
  19.8 1.3 %copy-done.2 = bf16[384,1536]{1,0:T(8,128)(2,1)S(1)} copy-done((bf16[384,1536]{1,0:T(8,128)(2,1)S(1)}, bf16[384,1536]{1,0:T(8,128)(2,1)}, u32[]{:S(2)}) %copy-start.2) | copy-done | bytes 1179672
  21.0 5.1 %mix.1 = (f32[64,384]{1,0:T(8,128)S(1)}, f32[64,384]{1,0:T(8,128)S(1)}) custom-call(bf16[16,2048]{1,0:T(8,128)(2,1)S(1)} %pad_maximum_fusion.refs_0_, bf16[16,2048]{1,0:T(8,128)(2,1)S(1)} %collective-permute-done.refs_1_, bf16[16,2048]{1,0:T(8,128)(2,1)S(1)} %collective-permute-done.1.refs_2_, bf16[16,2048]{1,0:T(8,128)(2,1)S(1)} %collective-permute-done.2.refs_3_, ...), custom_call_target="tpu_custom_call" | custom-call | flops 654311424 | bytes 4325376 | tf_op jit(solution)/shard_map/mix/pallas_call | solution.py:56
  26.1 1.6 %collective-permute-start.7 = (f32[64,384]{1,0:T(8,128)S(1)}, f32[64,384]{1,0:T(8,128)S(1)}, u32[]{:S(2)}, u32[]{:S(2)}) collective-permute-start(f32[64,384]{1,0:T(8,128)S(1)} %get-tuple-element.8), channel_id=1, source_target_pairs={{0,1},{1,0},{2,3},{3,2},{4,5},{5,4},{6,7},{7,6},{8,9},{9,8},{10,11... | collective-permute-start | bytes 294920 | tf_op jit(solution)/shard_map/ppermute | solution.py:103
  27.7 0.9 %collective-permute-done.7 = f32[64,384]{1,0:T(8,128)S(1)} collective-permute-done((f32[64,384]{1,0:T(8,128)S(1)}, f32[64,384]{1,0:T(8,128)S(1)}, u32[]{:S(2)}, u32[]{:S(2)}) %collective-permute-start.7) | collective-permute-done | bytes 98336 | tf_op jit(solution)/shard_map/ppermute | solution.py:103
  28.7 3.9 %collective-permute-start.11 = (bf16[16,384]{1,0:T(8,128)(2,1)S(1)}, bf16[16,384]{1,0:T(8,128)(2,1)S(1)}, u32[]{:S(2)}, u32[]{:S(2)}) collective-permute-start(bf16[16,384]{1,0:T(8,128)(2,1)S(1)} %get-tuple-element.9), channel_id=1, source_target_pairs={{0,6},{1,14},{2,4},{3,12},{4,2},{5,10},{6,0},{7,8},{8,15},{9,7},{1... | collective-permute-start | bytes 36872 | tf_op jit(solution)/shard_map/ppermute | solution.py:112
  32.5 0.6 %collective-permute-start.10 = (bf16[16,384]{1,0:T(8,128)(2,1)S(1)}, bf16[16,384]{1,0:T(8,128)(2,1)S(1)}, u32[]{:S(2)}, u32[]{:S(2)}) collective-permute-start(bf16[16,384]{1,0:T(8,128)(2,1)S(1)} %get-tuple-element.10), channel_id=1, source_target_pairs={{0,4},{1,12},{2,6},{3,14},{4,0},{5,8},{6,2},{7,10},{8,13},{9,5},{1... | collective-permute-start | bytes 36872 | tf_op jit(solution)/shard_map/ppermute | solution.py:112
  33.1 0.4 collective-permute-start.9
  33.5 3.3 %collective-permute-start.8 = (bf16[16,384]{1,0:T(8,128)(2,1)S(1)}, bf16[16,384]{1,0:T(8,128)(2,1)S(1)}, u32[]{:S(2)}, u32[]{:S(2)}) collective-permute-start(bf16[16,384]{1,0:T(8,128)(2,1)S(1)} %get-tuple-element.12), channel_id=1, source_target_pairs={{0,0},{1,8},{2,2},{3,10},{4,4},{5,12},{6,6},{7,14},{8,9},{9,1},{10... | collective-permute-start | bytes 36872 | tf_op jit(solution)/shard_map/ppermute | solution.py:112
  36.7 0.0 collective-permute-done.11.refs_3_
  36.8 0.0 copy-start.3
  36.8 0.1 collective-permute-done.10.refs_2_
  36.9 0.0 copy-start.4
  36.9 0.6 %collective-permute-done.9.refs_1_ = bf16[16,384]{1,0:T(8,128)(2,1)S(1)} collective-permute-done((bf16[16,384]{1,0:T(8,128)(2,1)S(1)}, bf16[16,384]{1,0:T(8,128)(2,1)S(1)}, u32[]{:S(2)}, u32[]{:S(2)}) %collective-permute-start.9) | collective-permute-done | bytes 12320 | tf_op jit(solution)/shard_map/ppermute | solution.py:112
  37.5 0.0 copy-start.5
  37.5 2.0 %collective-permute-done.8.refs_0_ = bf16[16,384]{1,0:T(8,128)(2,1)S(1)} collective-permute-done((bf16[16,384]{1,0:T(8,128)(2,1)S(1)}, bf16[16,384]{1,0:T(8,128)(2,1)S(1)}, u32[]{:S(2)}, u32[]{:S(2)}) %collective-permute-start.8) | collective-permute-done | bytes 12320 | tf_op jit(solution)/shard_map/ppermute | solution.py:112
  39.5 0.0 copy-done.3
  39.5 0.0 copy-done.4
  39.5 0.0 copy-done.5
  39.5 0.0 copy-start.6
  39.5 0.6 %copy-done.6 = bf16[16,384]{1,0:T(8,128)(2,1)} copy-done((bf16[16,384]{1,0:T(8,128)(2,1)}, bf16[16,384]{1,0:T(8,128)(2,1)S(1)}, u32[]{:S(2)}) %copy-start.6) | copy-done | bytes 12312
  40.1 1.4 %place.1 = bf16[16,1536]{1,0:T(8,128)(2,1)} custom-call(bf16[16,384]{1,0:T(8,128)(2,1)} %copy-done.6, bf16[16,384]{1,0:T(8,128)(2,1)} %copy-done.5, bf16[16,384]{1,0:T(8,128)(2,1)} %copy-done.4, bf16[16,384]{1,0:T(8,128)(2,1)} %copy-done.3), custom_call_target="tpu_custom_call" | custom-call | tf_op jit(solution)/shard_map/place/pallas_call | solution.py:87
  (2 shorter events, 0.0 us)
Async XLA Ops:
  0.8 9.5 %collective-permute-start.6 = (bf16[16,2048]{1,0:T(8,128)(2,1)S(1)}, bf16[16,2048]{1,0:T(8,128)(2,1)S(1)}, u32[]{:S(2)}, u32[]{:S(2)}) collective-permute-start(bf16[16,2048]{1,0:T(8,128)(2,1)S(1)} %pad_maximum_fusion.refs_0_), channel_id=1, source_target_pairs={{0,14},{2,12},{4,10},{6,8},{8,6},{10,4},{12,2},{14,0},{1,15},{3,13... | collective-permute-start | bytes 196616 | tf_op jit(solution)/shard_map/ppermute | solution.py:101
  5.9 5.0 %collective-permute-start.5 = (bf16[16,2048]{1,0:T(8,128)(2,1)S(1)}, bf16[16,2048]{1,0:T(8,128)(2,1)S(1)}, u32[]{:S(2)}, u32[]{:S(2)}) collective-permute-start(bf16[16,2048]{1,0:T(8,128)(2,1)S(1)} %pad_maximum_fusion.refs_0_), channel_id=1, source_target_pairs={{0,12},{2,14},{4,8},{6,10},{8,4},{10,6},{12,0},{14,2},{1,13},{3,15... | collective-permute-start | bytes 196616 | tf_op jit(solution)/shard_map/ppermute | solution.py:101
  5.9 9.5 %collective-permute-start.4 = (bf16[16,2048]{1,0:T(8,128)(2,1)S(1)}, bf16[16,2048]{1,0:T(8,128)(2,1)S(1)}, u32[]{:S(2)}, u32[]{:S(2)}) collective-permute-start(bf16[16,2048]{1,0:T(8,128)(2,1)S(1)} %pad_maximum_fusion.refs_0_), channel_id=1, source_target_pairs={{0,10},{2,8},{4,14},{6,12},{8,2},{10,0},{12,6},{14,4},{1,11},{3,9}... | collective-permute-start | bytes 196616 | tf_op jit(solution)/shard_map/ppermute | solution.py:101
  6.3 10.6 %collective-permute-start.3 = (bf16[16,2048]{1,0:T(8,128)(2,1)S(1)}, bf16[16,2048]{1,0:T(8,128)(2,1)S(1)}, u32[]{:S(2)}, u32[]{:S(2)}) collective-permute-start(bf16[16,2048]{1,0:T(8,128)(2,1)S(1)} %pad_maximum_fusion.refs_0_), channel_id=1, source_target_pairs={{0,8},{2,10},{4,12},{6,14},{8,0},{10,2},{12,4},{14,6},{1,9},{3,11}... | collective-permute-start | bytes 196616 | tf_op jit(solution)/shard_map/ppermute | solution.py:101
  8.3 8.6 %collective-permute-start.2 = (bf16[16,2048]{1,0:T(8,128)(2,1)S(1)}, bf16[16,2048]{1,0:T(8,128)(2,1)S(1)}, u32[]{:S(2)}, u32[]{:S(2)}) collective-permute-start(bf16[16,2048]{1,0:T(8,128)(2,1)S(1)} %pad_maximum_fusion.refs_0_), channel_id=1, source_target_pairs={{0,6},{2,4},{4,2},{6,0},{8,14},{10,12},{12,10},{14,8},{1,7},{3,5},... | collective-permute-start | bytes 196616 | tf_op jit(solution)/shard_map/ppermute | solution.py:101
  10.4 6.6 %collective-permute-start.1 = (bf16[16,2048]{1,0:T(8,128)(2,1)S(1)}, bf16[16,2048]{1,0:T(8,128)(2,1)S(1)}, u32[]{:S(2)}, u32[]{:S(2)}) collective-permute-start(bf16[16,2048]{1,0:T(8,128)(2,1)S(1)} %pad_maximum_fusion.refs_0_), channel_id=1, source_target_pairs={{0,4},{2,6},{4,0},{6,2},{8,12},{10,14},{12,8},{14,10},{1,5},{3,7},... | collective-permute-start | bytes 196616 | tf_op jit(solution)/shard_map/ppermute | solution.py:101
  10.9 6.0 %collective-permute-start = (bf16[16,2048]{1,0:T(8,128)(2,1)S(1)}, bf16[16,2048]{1,0:T(8,128)(2,1)S(1)}, u32[]{:S(2)}, u32[]{:S(2)}) collective-permute-start(bf16[16,2048]{1,0:T(8,128)(2,1)S(1)} %pad_maximum_fusion.refs_0_), channel_id=1, source_target_pairs={{0,2},{2,0},{4,6},{6,4},{8,10},{10,8},{12,14},{14,12},{1,3},{3,1},... | collective-permute-start | bytes 196616 | tf_op jit(solution)/shard_map/ppermute | solution.py:101
  16.9 1.4 %copy-start = (bf16[512,1536]{1,0:T(8,128)(2,1)S(1)}, bf16[512,1536]{1,0:T(8,128)(2,1)}, u32[]{:S(2)}) copy-start(bf16[512,1536]{1,0:T(8,128)(2,1)} %refs_8_.1) | copy-start | bytes 4718596
  18.3 1.4 %copy-start.1 = (bf16[512,1536]{1,0:T(8,128)(2,1)S(1)}, bf16[512,1536]{1,0:T(8,128)(2,1)}, u32[]{:S(2)}) copy-start(bf16[512,1536]{1,0:T(8,128)(2,1)} %refs_9_.1) | copy-start | bytes 4718596
  19.8 1.3 %copy-start.2 = (bf16[384,1536]{1,0:T(8,128)(2,1)S(1)}, bf16[384,1536]{1,0:T(8,128)(2,1)}, u32[]{:S(2)}) copy-start(bf16[384,1536]{1,0:T(8,128)(2,1)} %refs_10_.1) | copy-start | bytes 3538948
  26.1 2.6 %collective-permute-start.7 = (f32[64,384]{1,0:T(8,128)S(1)}, f32[64,384]{1,0:T(8,128)S(1)}, u32[]{:S(2)}, u32[]{:S(2)}) collective-permute-start(f32[64,384]{1,0:T(8,128)S(1)} %get-tuple-element.8), channel_id=1, source_target_pairs={{0,1},{1,0},{2,3},{3,2},{4,5},{5,4},{6,7},{7,6},{8,9},{9,8},{10,11... | collective-permute-start | bytes 294920 | tf_op jit(solution)/shard_map/ppermute | solution.py:103
  28.7 8.1 %collective-permute-start.11 = (bf16[16,384]{1,0:T(8,128)(2,1)S(1)}, bf16[16,384]{1,0:T(8,128)(2,1)S(1)}, u32[]{:S(2)}, u32[]{:S(2)}) collective-permute-start(bf16[16,384]{1,0:T(8,128)(2,1)S(1)} %get-tuple-element.9), channel_id=1, source_target_pairs={{0,6},{1,14},{2,4},{3,12},{4,2},{5,10},{6,0},{7,8},{8,15},{9,7},{1... | collective-permute-start | bytes 36872 | tf_op jit(solution)/shard_map/ppermute | solution.py:112
  32.5 4.3 %collective-permute-start.10 = (bf16[16,384]{1,0:T(8,128)(2,1)S(1)}, bf16[16,384]{1,0:T(8,128)(2,1)S(1)}, u32[]{:S(2)}, u32[]{:S(2)}) collective-permute-start(bf16[16,384]{1,0:T(8,128)(2,1)S(1)} %get-tuple-element.10), channel_id=1, source_target_pairs={{0,4},{1,12},{2,6},{3,14},{4,0},{5,8},{6,2},{7,10},{8,13},{9,5},{1... | collective-permute-start | bytes 36872 | tf_op jit(solution)/shard_map/ppermute | solution.py:112
  33.1 4.3 %collective-permute-start.9 = (bf16[16,384]{1,0:T(8,128)(2,1)S(1)}, bf16[16,384]{1,0:T(8,128)(2,1)S(1)}, u32[]{:S(2)}, u32[]{:S(2)}) collective-permute-start(bf16[16,384]{1,0:T(8,128)(2,1)S(1)} %get-tuple-element.11), channel_id=1, source_target_pairs={{0,2},{1,10},{2,0},{3,8},{4,6},{5,14},{6,4},{7,12},{8,11},{9,3},{1... | collective-permute-start | bytes 36872 | tf_op jit(solution)/shard_map/ppermute | solution.py:112
  33.5 6.0 %collective-permute-start.8 = (bf16[16,384]{1,0:T(8,128)(2,1)S(1)}, bf16[16,384]{1,0:T(8,128)(2,1)S(1)}, u32[]{:S(2)}, u32[]{:S(2)}) collective-permute-start(bf16[16,384]{1,0:T(8,128)(2,1)S(1)} %get-tuple-element.12), channel_id=1, source_target_pairs={{0,0},{1,8},{2,2},{3,10},{4,4},{5,12},{6,6},{7,14},{8,9},{9,1},{10... | collective-permute-start | bytes 36872 | tf_op jit(solution)/shard_map/ppermute | solution.py:112
  36.8 2.7 %copy-start.3 = (bf16[16,384]{1,0:T(8,128)(2,1)}, bf16[16,384]{1,0:T(8,128)(2,1)S(1)}, u32[]{:S(2)}) copy-start(bf16[16,384]{1,0:T(8,128)(2,1)S(1)} %collective-permute-done.11.refs_3_) | copy-start | bytes 36868
  36.9 2.6 %copy-start.4 = (bf16[16,384]{1,0:T(8,128)(2,1)}, bf16[16,384]{1,0:T(8,128)(2,1)S(1)}, u32[]{:S(2)}) copy-start(bf16[16,384]{1,0:T(8,128)(2,1)S(1)} %collective-permute-done.10.refs_2_) | copy-start | bytes 36868
  37.5 2.0 %copy-start.5 = (bf16[16,384]{1,0:T(8,128)(2,1)}, bf16[16,384]{1,0:T(8,128)(2,1)S(1)}, u32[]{:S(2)}) copy-start(bf16[16,384]{1,0:T(8,128)(2,1)S(1)} %collective-permute-done.9.refs_1_) | copy-start | bytes 36868
  39.5 0.6 %copy-start.6 = (bf16[16,384]{1,0:T(8,128)(2,1)}, bf16[16,384]{1,0:T(8,128)(2,1)S(1)}, u32[]{:S(2)}) copy-start(bf16[16,384]{1,0:T(8,128)(2,1)S(1)} %collective-permute-done.8.refs_0_) | copy-start | bytes 36868

commit v2 on v1

--- a/solution.py
+++ b/solution.py
@@ -13,61 +13,88 @@
 NT = (((1,), (1,)), ((), ()))
 
 
-def mix_kernel(count, *refs):
+def hold_kernel(*refs):
+    count = (len(refs) - 1) // 2
+    copies = [
+        pltpu.make_async_copy(source, kept, refs[-1].at[i])
+        for i, (source, kept) in enumerate(zip(refs[:count], refs[count:-1]))
+    ]
+    for copy in copies:
+        copy.start()
+    for copy in copies:
+        copy.wait()
+
+
+def hold(*weights):
+    vmem = pl.BlockSpec(memory_space=pltpu.VMEM)
+    return pl.pallas_call(
+        hold_kernel,
+        out_shape=[jax.ShapeDtypeStruct(w.shape, w.dtype) for w in weights],
+        in_specs=[pl.BlockSpec(memory_space=pltpu.HBM)] * len(weights),
+        out_specs=[vmem] * len(weights),
+        scratch_shapes=[pltpu.SemaphoreType.DMA((len(weights),))],
+        cost_estimate=pl.CostEstimate(
+            flops=0, bytes_accessed=sum(4 * w.size for w in weights), transcendentals=0
+        ),
+        compiler_params=pltpu.CompilerParams(vmem_limit_bytes=1024 * 1024),
+        name="hold",
+    )(*(pltpu.with_memory_space_constraint(w, pltpu.HBM) for w in weights))
+
+
+def mix_kernel(count, half, *refs):
     blocks = refs[:count]
-    key_basis, value_basis, out_weight, keep, send, mixed, partial_sum = refs[count:]
+    key_basis, value_basis, out_weight, keep, send, partial_sum = refs[count:]
     width = key_basis.shape[1]
     queries = jnp.concatenate([b[:, :width] for b in blocks], axis=0)
     latent = jnp.concatenate([b[:, width:] for b in blocks], axis=0)
     scale = 1.0 / math.sqrt(HEAD_DIM)
-    for first in range(0, width, HEAD_DIM):
-        cols = slice(first, first + HEAD_DIM)
-        keys = jnp.dot(latent, key_basis[:, cols], preferred_element_type=jnp.float32)
-        values = jnp.dot(latent, value_basis[:, cols], preferred_element_type=jnp.float32)
-        scores = (
-            lax.dot_general(
-                queries[:, cols], keys.astype(jnp.bfloat16), NT, preferred_element_type=jnp.float32
-            )
-            * scale
-        )
-        weights = jnp.exp(scores - jnp.max(scores, axis=1, keepdims=True))
-        totals = jnp.sum(weights, axis=1, keepdims=True)
-        head = jnp.dot(
-            weights.astype(jnp.bfloat16),
-            values.astype(jnp.bfloat16),
-            preferred_element_type=jnp.float32,
-        )
-        mixed[:, cols] = (head / totals).astype(jnp.bfloat16)
+    heads = [slice(first, first + HEAD_DIM) for first in range(0, width, HEAD_DIM)]
+    keys = jnp.dot(latent, key_basis[...], preferred_element_type=jnp.float32).astype(jnp.bfloat16)
+    values = jnp.dot(latent, value_basis[...], preferred_element_type=jnp.float32).astype(
+        jnp.bfloat16
+    )
+    scores = [
+        lax.dot_general(queries[:, c], keys[:, c], NT, preferred_element_type=jnp.float32) * scale
+        for c in heads
+    ]
+    weights = [jnp.exp(s - jnp.max(s, axis=1, keepdims=True)) for s in scores]
+    totals = [jnp.sum(w, axis=1, keepdims=True) for w in weights]
+    sums = [
+        jnp.dot(w.astype(jnp.bfloat16), values[:, c], preferred_element_type=jnp.float32)
+        for w, c in zip(weights, heads)
+    ]
+    mixed = jnp.concatenate([(s / t).astype(jnp.bfloat16) for s, t in zip(sums, totals)], axis=1)
     partial_sum[...] = lax.dot_general(
-        mixed[...], out_weight[...], NT, preferred_element_type=jnp.float32
+        mixed, out_weight[...], NT, preferred_element_type=jnp.float32
     )
     rows = keep.shape[0]
-    core = lax.axis_index("head")
-    keep[...] = partial_sum[pl.ds(pl.multiple_of(core * rows, rows), rows), :]
-    send[...] = partial_sum[pl.ds(pl.multiple_of((1 - core) * rows, rows), rows), :]
-
-
-def mix(blocks, key_basis, value_basis, out_weight):
+    far = own_half(half)
+    keep[...] = partial_sum[pl.ds(pl.multiple_of(far * rows, rows), rows), :]
+    send[...] = partial_sum[pl.ds(pl.multiple_of((1 - far) * rows, rows), rows), :]
+
+
+def own_half(half):
+    taker = lax.axis_index("seq") // half
+    return 1 - jnp.bitwise_xor(taker, lax.axis_index("head"))
+
+
+def mix(half, blocks, key_basis, value_basis, out_weight):
     rows = sum(b.shape[0] for b in blocks)
     width, features = key_basis.shape[1], out_weight.shape[0]
-    half = jax.ShapeDtypeStruct((rows // 2, features), jnp.float32)
+    rank = key_basis.shape[0]
     vmem = pl.BlockSpec(memory_space=pltpu.VMEM)
-    rank = key_basis.shape[0]
     return pl.pallas_call(
-        functools.partial(mix_kernel, len(blocks)),
-        out_shape=(half, half),
+        functools.partial(mix_kernel, len(blocks), half),
+        out_shape=[jax.ShapeDtypeStruct((rows // 2, features), jnp.float32)] * 2,
         in_specs=[vmem] * (len(blocks) + 3),
-        out_specs=(vmem, vmem),
-        scratch_shapes=[
-            pltpu.VMEM((rows, width), jnp.bfloat16),
-            pltpu.VMEM((rows, features), jnp.float32),
-        ],
+        out_specs=[vmem] * 2,
+        scratch_shapes=[pltpu.VMEM((rows, features), jnp.float32)],
         cost_estimate=pl.CostEstimate(
             flops=2 * rows * width * (2 * rank + 2 * rows + features),
             bytes_accessed=2 * width * (2 * rank + features),
             transcendentals=rows * rows * (width // HEAD_DIM),
         ),
-        compiler_params=pltpu.CompilerParams(vmem_limit_bytes=32 * 1024 * 1024),
+        compiler_params=pltpu.CompilerParams(vmem_limit_bytes=16 * 1024 * 1024),
         name="mix",
     )(*blocks, key_basis, value_basis, out_weight)
 
@@ -89,30 +116,41 @@
         out_shape=jax.ShapeDtypeStruct((rows, features * half), parts[0].dtype),
         in_specs=[vmem] * len(parts),
         out_specs=vmem,
+        compiler_params=pltpu.CompilerParams(vmem_limit_bytes=1024 * 1024),
         name="place",
     )(*parts)
+
+
+def back(count, step):
+    half = count // 2
+    pairs = []
+    for s in range(count):
+        taker = s // half
+        pairs.append((2 * s + taker, 2 * (s ^ (step + half)) + taker))
+        pairs.append((2 * s + 1 - taker, 2 * (s ^ step) + taker))
+    return pairs
 
 
 def direct(count, queries, latent, key_basis, value_basis, out_weight):
     rows, half = queries.shape[0], count // 2
     own = jnp.concatenate([queries, latent.T], axis=1)
     blocks = {0: own}
-    for flip in reversed(range(1, count)):
+    for flip in flips(count):
         blocks[flip] = lax.ppermute(own, "seq", [(i, i ^ flip) for i in range(count)])
-    keep, send = mix([blocks[k] for k in range(count)], key_basis, value_basis, out_weight)
+    weights = hold(key_basis, value_basis, out_weight)
+    keep, send = mix(half, [blocks[k] for k in range(count)], *weights)
     other = lax.ppermute(send, "head", [(0, 1), (1, 0)])
     total = (keep + other).astype(jnp.bfloat16)
     parts = [None] * half
     for step in reversed(range(half)):
-        pairs = [
-            (2 * s + h, 2 * (s ^ (step + h * half)) + s // half)
-            for s in range(count)
-            for h in range(2)
-        ]
         parts[step] = lax.ppermute(
-            total[step * rows : (step + 1) * rows], ("seq", "head"), pairs
+            total[step * rows : (step + 1) * rows], ("seq", "head"), back(count, step)
         )
     return place(parts, half)
+
+
+def flips(count):
+    return (4, 5, 7, 6, 3, 1, 2) if count == 8 else tuple(reversed(range(1, count)))
 
 
 def attend(queries, latent, key_basis, value_basis):

time: 41.8 us -> 31.1 us (0.74)
  local copies, waits for them, and re-layouts: 4.69 us -> 0.01 us
  Pallas kernels: 6.45 us -> 4.27 us
  starting transfers between devices: 19.7 us -> 17.6 us
  waiting for transfers between devices: 9.7 us -> 8.17 us
    unnamed x14 -> x0, local copies, waits for them, and re-layouts: 4.68 us -> none
    ppermute x7, waiting for transfers between devices: 6.04 us -> 3.79 us  [direct(): lax.ppermute(own, 'seq', [(i, i ^ flip) for i in range(count)])]
    ppermute x4, starting transfers between devices: 8.05 us -> 5.91 us  [direct(): lax.ppermute(total[step * rows:(step + 1) * rows], ('seq', 'head'), back(...]
    pallas_call x1 -> x2, Pallas kernels: 5.07 us -> 3.64 us  [the longest x1 2.24 us: hold(): pl.pallas_call(hold_kernel, out_shape=[jax.ShapeDtypeStruct(w.shape, w.dt...]
    pallas_call x1, Pallas kernels: 1.38 us -> 0.63 us  [place(): pl.pallas_call(functools.partial(place_kernel, half), out_shape=jax.Shape...]
    ppermute x4, waiting for transfers between devices: 2.72 us -> 3.44 us  [direct(): lax.ppermute(total[step * rows:(step + 1) * rows], ('seq', 'head'), back(...]
  transfers between devices with their start and end apart: 12 -> 12, of which waited for: 7 -> 6; matrix products, arithmetic and copies ran while one was open for 0% -> 0% of each run, Pallas kernels for 0% -> 7%
where the time goes in v2:
time: 31.1 us; the launch traced here: 30.9 us
  starting transfers between devices  17.6 us (57%)
  waiting for transfers between devices  8.17 us (26%)
  Pallas kernels  4.27 us (14%)
  other arithmetic  0.83 us (3%)
    ppermute x7, starting transfers between devices, direct(): lax.ppermute(own, 'seq', [(i, i ^ flip) for i in range(count)])  10.1 us
    ppermute x4, starting transfers between devices, direct(): lax.ppermute(total[step * rows:(step + 1) * rows], ('seq', 'head'), back(...  5.91 us
    ppermute x7, waiting for transfers between devices, direct(): lax.ppermute(own, 'seq', [(i, i ^ flip) for i in range(count)])  3.79 us
    ppermute x4, waiting for transfers between devices, direct(): lax.ppermute(total[step * rows:(step + 1) * rows], ('seq', 'head'), back(...  3.44 us
    pallas_call x1, Pallas kernels, hold(): pl.pallas_call(hold_kernel, out_shape=[jax.ShapeDtypeStruct(w.shape, w.dt...  2.24 us
    ppermute x1, starting transfers between devices, direct(): other = lax.ppermute(send, 'head', [(0, 1), (1, 0)])  1.62 us
    pallas_call x1, Pallas kernels, mix(): pl.pallas_call(functools.partial(mix_kernel, len(blocks), half), out_shap...  1.4 us
    ppermute x1, waiting for transfers between devices, direct(): other = lax.ppermute(send, 'head', [(0, 1), (1, 0)])  0.94 us
  transfers between devices with their start and end apart: 12, of which 6 were waited for; matrix products, arithmetic and copies ran while one was open for 0% of the time, Pallas kernels for 7%

profile of v2, /device:TPU:1, one launch (start us, length us, event | category | flops | bytes accessed | tf_op | source)
XLA Modules:
  0.0 30.9 jit_solution(12943965229987365876)
XLA Ops:
  0.0 0.8 %pad_maximum_fusion.refs_0_ = bf16[16,2048]{1,0:T(8,128)(2,1)S(1)} fusion(bf16[16,512]{1,0:T(8,128)(2,1)} %bitcast.1, bf16[16,1536]{1,0:T(8,128)(2,1)} %param.5), kind=kLoop, calls=%fused_computation.1 | loop fusion | flops 131072 | bytes 131072 | tf_op jit(solution)/shard_map/concatenate | solution.py:136
  0.8 5.1 %collective-permute-start.6 = (bf16[16,2048]{1,0:T(8,128)(2,1)S(1)}, bf16[16,2048]{1,0:T(8,128)(2,1)S(1)}, u32[]{:S(2)}, u32[]{:S(2)}) collective-permute-start(bf16[16,2048]{1,0:T(8,128)(2,1)S(1)} %pad_maximum_fusion.refs_0_), channel_id=1, source_target_pairs={{0,14},{2,12},{4,10},{6,8},{8,6},{10,4},{12,2},{14,0},{1,15},{3,13... | collective-permute-start | bytes 196616 | tf_op jit(solution)/shard_map/ppermute | solution.py:139
  5.9 0.0 collective-permute-start.5
  5.9 0.4 %collective-permute-start.4 = (bf16[16,2048]{1,0:T(8,128)(2,1)S(1)}, bf16[16,2048]{1,0:T(8,128)(2,1)S(1)}, u32[]{:S(2)}, u32[]{:S(2)}) collective-permute-start(bf16[16,2048]{1,0:T(8,128)(2,1)S(1)} %pad_maximum_fusion.refs_0_), channel_id=1, source_target_pairs={{0,10},{2,8},{4,14},{6,12},{8,2},{10,0},{12,6},{14,4},{1,11},{3,9}... | collective-permute-start | bytes 196616 | tf_op jit(solution)/shard_map/ppermute | solution.py:139
  6.3 2.0 %collective-permute-start.3 = (bf16[16,2048]{1,0:T(8,128)(2,1)S(1)}, bf16[16,2048]{1,0:T(8,128)(2,1)S(1)}, u32[]{:S(2)}, u32[]{:S(2)}) collective-permute-start(bf16[16,2048]{1,0:T(8,128)(2,1)S(1)} %pad_maximum_fusion.refs_0_), channel_id=1, source_target_pairs={{0,8},{2,10},{4,12},{6,14},{8,0},{10,2},{12,4},{14,6},{1,9},{3,11}... | collective-permute-start | bytes 196616 | tf_op jit(solution)/shard_map/ppermute | solution.py:139
  8.3 2.0 %collective-permute-start.2 = (bf16[16,2048]{1,0:T(8,128)(2,1)S(1)}, bf16[16,2048]{1,0:T(8,128)(2,1)S(1)}, u32[]{:S(2)}, u32[]{:S(2)}) collective-permute-start(bf16[16,2048]{1,0:T(8,128)(2,1)S(1)} %pad_maximum_fusion.refs_0_), channel_id=1, source_target_pairs={{0,6},{2,4},{4,2},{6,0},{8,14},{10,12},{12,10},{14,8},{1,7},{3,5},... | collective-permute-start | bytes 196616 | tf_op jit(solution)/shard_map/ppermute | solution.py:139
  10.4 0.0 collective-permute-done.6.refs_7_
  10.4 0.3 collective-permute-start.1
  10.6 0.3 collective-permute-done.5.refs_6_
  10.9 0.3 collective-permute-start
  11.2 2.2 %hold.1 = (bf16[512,1536]{1,0:T(8,128)(2,1)S(1)}, bf16[512,1536]{1,0:T(8,128)(2,1)S(1)}, bf16[384,1536]{1,0:T(8,128)(2,1)S(1)}) custom-call(bf16[512,1536]{1,0:T(8,128)(2,1)} %refs_0_.1, bf16[512,1536]{1,0:T(8,128)(2,1)} %refs_1_.1, bf16[384,1536]{1,0:T(8,128)(2,1)} %refs_2_.1), custom_call_target="tpu_custom_call" | custom-call | bytes 8650752 | tf_op jit(solution)/shard_map/hold/pallas_call | solution.py:30
  13.4 2.0 %collective-permute-done.4.refs_5_ = bf16[16,2048]{1,0:T(8,128)(2,1)S(1)} collective-permute-done((bf16[16,2048]{1,0:T(8,128)(2,1)S(1)}, bf16[16,2048]{1,0:T(8,128)(2,1)S(1)}, u32[]{:S(2)}, u32[]{:S(2)}) %collective-permute-start.4) | collective-permute-done | bytes 65568 | tf_op jit(solution)/shard_map/ppermute | solution.py:139
  15.4 1.5 %collective-permute-done.3.refs_4_ = bf16[16,2048]{1,0:T(8,128)(2,1)S(1)} collective-permute-done((bf16[16,2048]{1,0:T(8,128)(2,1)S(1)}, bf16[16,2048]{1,0:T(8,128)(2,1)S(1)}, u32[]{:S(2)}, u32[]{:S(2)}) %collective-permute-start.3) | collective-permute-done | bytes 65568 | tf_op jit(solution)/shard_map/ppermute | solution.py:139
  16.9 0.0 collective-permute-done.2.refs_3_
  16.9 0.0 collective-permute-done.1.refs_2_
  16.9 0.0 collective-permute-done.refs_1_
  16.9 1.4 %mix.1 = (f32[64,384]{1,0:T(8,128)S(1)}, f32[64,384]{1,0:T(8,128)S(1)}) custom-call(bf16[16,2048]{1,0:T(8,128)(2,1)S(1)} %pad_maximum_fusion.refs_0_, bf16[16,2048]{1,0:T(8,128)(2,1)S(1)} %collective-permute-done.refs_1_, bf16[16,2048]{1,0:T(8,128)(2,1)S(1)} %collective-permute-done.1.refs_2_, bf16[16,2048]{1,0:T(8,128)(2,1)S(1)} %collective-permute-done.2.refs_3_, ...), custom_call_target="tpu_custom_call" | custom-call | flops 654311424 | bytes 4325376 | tf_op jit(solution)/shard_map/mix/pallas_call | solution.py:86
  18.3 1.6 %collective-permute-start.7 = (f32[64,384]{1,0:T(8,128)S(1)}, f32[64,384]{1,0:T(8,128)S(1)}, u32[]{:S(2)}, u32[]{:S(2)}) collective-permute-start(f32[64,384]{1,0:T(8,128)S(1)} %get-tuple-element.14), channel_id=1, source_target_pairs={{0,1},{1,0},{2,3},{3,2},{4,5},{5,4},{6,7},{7,6},{8,9},{9,8},{10,11... | collective-permute-start | bytes 294920 | tf_op jit(solution)/shard_map/ppermute | solution.py:142
  20.0 0.9 %collective-permute-done.7 = f32[64,384]{1,0:T(8,128)S(1)} collective-permute-done((f32[64,384]{1,0:T(8,128)S(1)}, f32[64,384]{1,0:T(8,128)S(1)}, u32[]{:S(2)}, u32[]{:S(2)}) %collective-permute-start.7) | collective-permute-done | bytes 98336 | tf_op jit(solution)/shard_map/ppermute | solution.py:142
  20.9 1.1 %collective-permute-start.11 = (bf16[16,384]{1,0:T(8,128)(2,1)S(1)}, bf16[16,384]{1,0:T(8,128)(2,1)S(1)}, u32[]{:S(2)}, u32[]{:S(2)}) collective-permute-start(bf16[16,384]{1,0:T(8,128)(2,1)S(1)} %get-tuple-element.15), channel_id=1, source_target_pairs={{0,14},{1,6},{2,12},{3,4},{4,10},{5,2},{6,8},{7,0},{9,7},{8,15},{1... | collective-permute-start | bytes 36872 | tf_op jit(solution)/shard_map/ppermute | solution.py:146
  22.1 2.6 %collective-permute-start.10 = (bf16[16,384]{1,0:T(8,128)(2,1)S(1)}, bf16[16,384]{1,0:T(8,128)(2,1)S(1)}, u32[]{:S(2)}, u32[]{:S(2)}) collective-permute-start(bf16[16,384]{1,0:T(8,128)(2,1)S(1)} %get-tuple-element.16), channel_id=1, source_target_pairs={{0,12},{1,4},{2,14},{3,6},{4,8},{5,0},{6,10},{7,2},{9,5},{8,13},{1... | collective-permute-start | bytes 36872 | tf_op jit(solution)/shard_map/ppermute | solution.py:146
  24.7 2.1 %collective-permute-start.9 = (bf16[16,384]{1,0:T(8,128)(2,1)S(1)}, bf16[16,384]{1,0:T(8,128)(2,1)S(1)}, u32[]{:S(2)}, u32[]{:S(2)}) collective-permute-start(bf16[16,384]{1,0:T(8,128)(2,1)S(1)} %get-tuple-element.17), channel_id=1, source_target_pairs={{0,10},{1,2},{2,8},{3,0},{4,14},{5,6},{6,12},{7,4},{9,3},{8,11},{1... | collective-permute-start | bytes 36872 | tf_op jit(solution)/shard_map/ppermute | solution.py:146
  26.9 0.0 collective-permute-start.8
  26.9 0.0 collective-permute-done.11.refs_3_
  26.9 0.0 collective-permute-done.10.refs_2_
  26.9 2.2 %collective-permute-done.9.refs_1_ = bf16[16,384]{1,0:T(8,128)(2,1)S(1)} collective-permute-done((bf16[16,384]{1,0:T(8,128)(2,1)S(1)}, bf16[16,384]{1,0:T(8,128)(2,1)S(1)}, u32[]{:S(2)}, u32[]{:S(2)}) %collective-permute-start.9) | collective-permute-done | bytes 12320 | tf_op jit(solution)/shard_map/ppermute | solution.py:146
  29.0 1.2 %collective-permute-done.8.refs_0_ = bf16[16,384]{1,0:T(8,128)(2,1)S(1)} collective-permute-done((bf16[16,384]{1,0:T(8,128)(2,1)S(1)}, bf16[16,384]{1,0:T(8,128)(2,1)S(1)}, u32[]{:S(2)}, u32[]{:S(2)}) %collective-permute-start.8) | collective-permute-done | bytes 12320 | tf_op jit(solution)/shard_map/ppermute | solution.py:146
  30.3 0.6 %place.1 = bf16[16,1536]{1,0:T(8,128)(2,1)} custom-call(bf16[16,384]{1,0:T(8,128)(2,1)S(1)} %collective-permute-done.8.refs_0_, bf16[16,384]{1,0:T(8,128)(2,1)S(1)} %collective-permute-done.9.refs_1_, bf16[16,384]{1,0:T(8,128)(2,1)S(1)} %collective-permute-done.10.refs_2_, bf16[16,384]{1,0:T(8,128)(2,1)S(1)} %collective-permute-done.11.refs_3_), custom_call_target="tpu_custom_call" | custom-call | tf_op jit(solution)/shard_map/place/pallas_call | solution.py:114
  (2 shorter events, 0.0 us)
Async XLA Ops:
  0.8 9.5 %collective-permute-start.6 = (bf16[16,2048]{1,0:T(8,128)(2,1)S(1)}, bf16[16,2048]{1,0:T(8,128)(2,1)S(1)}, u32[]{:S(2)}, u32[]{:S(2)}) collective-permute-start(bf16[16,2048]{1,0:T(8,128)(2,1)S(1)} %pad_maximum_fusion.refs_0_), channel_id=1, source_target_pairs={{0,14},{2,12},{4,10},{6,8},{8,6},{10,4},{12,2},{14,0},{1,15},{3,13... | collective-permute-start | bytes 196616 | tf_op jit(solution)/shard_map/ppermute | solution.py:139
  5.9 5.0 %collective-permute-start.5 = (bf16[16,2048]{1,0:T(8,128)(2,1)S(1)}, bf16[16,2048]{1,0:T(8,128)(2,1)S(1)}, u32[]{:S(2)}, u32[]{:S(2)}) collective-permute-start(bf16[16,2048]{1,0:T(8,128)(2,1)S(1)} %pad_maximum_fusion.refs_0_), channel_id=1, source_target_pairs={{0,12},{2,14},{4,8},{6,10},{8,4},{10,6},{12,0},{14,2},{1,13},{3,15... | collective-permute-start | bytes 196616 | tf_op jit(solution)/shard_map/ppermute | solution.py:139
  5.9 9.5 %collective-permute-start.4 = (bf16[16,2048]{1,0:T(8,128)(2,1)S(1)}, bf16[16,2048]{1,0:T(8,128)(2,1)S(1)}, u32[]{:S(2)}, u32[]{:S(2)}) collective-permute-start(bf16[16,2048]{1,0:T(8,128)(2,1)S(1)} %pad_maximum_fusion.refs_0_), channel_id=1, source_target_pairs={{0,10},{2,8},{4,14},{6,12},{8,2},{10,0},{12,6},{14,4},{1,11},{3,9}... | collective-permute-start | bytes 196616 | tf_op jit(solution)/shard_map/ppermute | solution.py:139
  6.3 10.6 %collective-permute-start.3 = (bf16[16,2048]{1,0:T(8,128)(2,1)S(1)}, bf16[16,2048]{1,0:T(8,128)(2,1)S(1)}, u32[]{:S(2)}, u32[]{:S(2)}) collective-permute-start(bf16[16,2048]{1,0:T(8,128)(2,1)S(1)} %pad_maximum_fusion.refs_0_), channel_id=1, source_target_pairs={{0,8},{2,10},{4,12},{6,14},{8,0},{10,2},{12,4},{14,6},{1,9},{3,11}... | collective-permute-start | bytes 196616 | tf_op jit(solution)/shard_map/ppermute | solution.py:139
  8.3 8.6 %collective-permute-start.2 = (bf16[16,2048]{1,0:T(8,128)(2,1)S(1)}, bf16[16,2048]{1,0:T(8,128)(2,1)S(1)}, u32[]{:S(2)}, u32[]{:S(2)}) collective-permute-start(bf16[16,2048]{1,0:T(8,128)(2,1)S(1)} %pad_maximum_fusion.refs_0_), channel_id=1, source_target_pairs={{0,6},{2,4},{4,2},{6,0},{8,14},{10,12},{12,10},{14,8},{1,7},{3,5},... | collective-permute-start | bytes 196616 | tf_op jit(solution)/shard_map/ppermute | solution.py:139
  10.4 6.6 %collective-permute-start.1 = (bf16[16,2048]{1,0:T(8,128)(2,1)S(1)}, bf16[16,2048]{1,0:T(8,128)(2,1)S(1)}, u32[]{:S(2)}, u32[]{:S(2)}) collective-permute-start(bf16[16,2048]{1,0:T(8,128)(2,1)S(1)} %pad_maximum_fusion.refs_0_), channel_id=1, source_target_pairs={{0,4},{2,6},{4,0},{6,2},{8,12},{10,14},{12,8},{14,10},{1,5},{3,7},... | collective-permute-start | bytes 196616 | tf_op jit(solution)/shard_map/ppermute | solution.py:139
  10.9 6.0 %collective-permute-start = (bf16[16,2048]{1,0:T(8,128)(2,1)S(1)}, bf16[16,2048]{1,0:T(8,128)(2,1)S(1)}, u32[]{:S(2)}, u32[]{:S(2)}) collective-permute-start(bf16[16,2048]{1,0:T(8,128)(2,1)S(1)} %pad_maximum_fusion.refs_0_), channel_id=1, source_target_pairs={{0,2},{2,0},{4,6},{6,4},{8,10},{10,8},{12,14},{14,12},{1,3},{3,1},... | collective-permute-start | bytes 196616 | tf_op jit(solution)/shard_map/ppermute | solution.py:139
  18.3 2.6 %collective-permute-start.7 = (f32[64,384]{1,0:T(8,128)S(1)}, f32[64,384]{1,0:T(8,128)S(1)}, u32[]{:S(2)}, u32[]{:S(2)}) collective-permute-start(f32[64,384]{1,0:T(8,128)S(1)} %get-tuple-element.14), channel_id=1, source_target_pairs={{0,1},{1,0},{2,3},{3,2},{4,5},{5,4},{6,7},{7,6},{8,9},{9,8},{10,11... | collective-permute-start | bytes 294920 | tf_op jit(solution)/shard_map/ppermute | solution.py:142
  20.9 5.9 %collective-permute-start.11 = (bf16[16,384]{1,0:T(8,128)(2,1)S(1)}, bf16[16,384]{1,0:T(8,128)(2,1)S(1)}, u32[]{:S(2)}, u32[]{:S(2)}) collective-permute-start(bf16[16,384]{1,0:T(8,128)(2,1)S(1)} %get-tuple-element.15), channel_id=1, source_target_pairs={{0,14},{1,6},{2,12},{3,4},{4,10},{5,2},{6,8},{7,0},{9,7},{8,15},{1... | collective-permute-start | bytes 36872 | tf_op jit(solution)/shard_map/ppermute | solution.py:146
  22.1 4.8 %collective-permute-start.10 = (bf16[16,384]{1,0:T(8,128)(2,1)S(1)}, bf16[16,384]{1,0:T(8,128)(2,1)S(1)}, u32[]{:S(2)}, u32[]{:S(2)}) collective-permute-start(bf16[16,384]{1,0:T(8,128)(2,1)S(1)} %get-tuple-element.16), channel_id=1, source_target_pairs={{0,12},{1,4},{2,14},{3,6},{4,8},{5,0},{6,10},{7,2},{9,5},{8,13},{1... | collective-permute-start | bytes 36872 | tf_op jit(solution)/shard_map/ppermute | solution.py:146
  24.7 4.3 %collective-permute-start.9 = (bf16[16,384]{1,0:T(8,128)(2,1)S(1)}, bf16[16,384]{1,0:T(8,128)(2,1)S(1)}, u32[]{:S(2)}, u32[]{:S(2)}) collective-permute-start(bf16[16,384]{1,0:T(8,128)(2,1)S(1)} %get-tuple-element.17), channel_id=1, source_target_pairs={{0,10},{1,2},{2,8},{3,0},{4,14},{5,6},{6,12},{7,4},{9,3},{8,11},{1... | collective-permute-start | bytes 36872 | tf_op jit(solution)/shard_map/ppermute | solution.py:146
  26.9 3.4 %collective-permute-start.8 = (bf16[16,384]{1,0:T(8,128)(2,1)S(1)}, bf16[16,384]{1,0:T(8,128)(2,1)S(1)}, u32[]{:S(2)}, u32[]{:S(2)}) collective-permute-start(bf16[16,384]{1,0:T(8,128)(2,1)S(1)} %get-tuple-element.18), channel_id=1, source_target_pairs={{0,8},{1,0},{2,10},{3,2},{4,12},{5,4},{6,14},{7,6},{9,1},{8,9},{11... | collective-permute-start | bytes 36872 | tf_op jit(solution)/shard_map/ppermute | solution.py:146

commit v3 on v2

--- a/solution.py
+++ b/solution.py
@@ -41,9 +41,10 @@
     )(*(pltpu.with_memory_space_constraint(w, pltpu.HBM) for w in weights))
 
 
-def mix_kernel(count, half, *refs):
-    blocks = refs[:count]
-    key_basis, value_basis, out_weight, keep, send, partial_sum = refs[count:]
+def mix_kernel(plan, *refs):
+    blocks = [refs[plan.order.index(flip)] for flip in range(plan.count)]
+    key_basis, value_basis, out_weight, keep, send, partial_sum = refs[plan.count :]
+    rows = blocks[0].shape[0]
     width = key_basis.shape[1]
     queries = jnp.concatenate([b[:, :width] for b in blocks], axis=0)
     latent = jnp.concatenate([b[:, width:] for b in blocks], axis=0)
@@ -67,26 +68,23 @@
     partial_sum[...] = lax.dot_general(
         mixed, out_weight[...], NT, preferred_element_type=jnp.float32
     )
-    rows = keep.shape[0]
-    far = own_half(half)
-    keep[...] = partial_sum[pl.ds(pl.multiple_of(far * rows, rows), rows), :]
-    send[...] = partial_sum[pl.ds(pl.multiple_of((1 - far) * rows, rows), rows), :]
-
-
-def own_half(half):
-    taker = lax.axis_index("seq") // half
-    return 1 - jnp.bitwise_xor(taker, lax.axis_index("head"))
-
-
-def mix(half, blocks, key_basis, value_basis, out_weight):
-    rows = sum(b.shape[0] for b in blocks)
-    width, features = key_basis.shape[1], out_weight.shape[0]
-    rank = key_basis.shape[0]
+    taker = lax.axis_index("head") == lax.axis_index("seq") // plan.half
+    for step, flips in enumerate(plan.turns):
+        first, second = (partial_sum[flip * rows : (flip + 1) * rows, :] for flip in flips)
+        part = slice(step * rows, (step + 1) * rows)
+        keep[part, :] = jnp.where(taker, first, second)
+        send[part, :] = jnp.where(taker, second, first)
+
+
+def mix(plan, blocks, key_basis, value_basis, out_weight):
+    rows = blocks[0].shape[0] * plan.count
+    rank, width = key_basis.shape
+    features = out_weight.shape[0]
     vmem = pl.BlockSpec(memory_space=pltpu.VMEM)
     return pl.pallas_call(
-        functools.partial(mix_kernel, len(blocks), half),
+        functools.partial(mix_kernel, plan),
         out_shape=[jax.ShapeDtypeStruct((rows // 2, features), jnp.float32)] * 2,
-        in_specs=[vmem] * (len(blocks) + 3),
+        in_specs=[vmem] * (plan.count + 3),
         out_specs=[vmem] * 2,
         scratch_shapes=[pltpu.VMEM((rows, features), jnp.float32)],
         cost_estimate=pl.CostEstimate(
@@ -96,24 +94,27 @@
         ),
         compiler_params=pltpu.CompilerParams(vmem_limit_bytes=16 * 1024 * 1024),
         name="mix",
-    )(*blocks, key_basis, value_basis, out_weight)
-
-
-def place_kernel(half, *refs):
+    )(*(blocks[flip] for flip in plan.order), key_basis, value_basis, out_weight)
+
+
+def place_kernel(plan, *refs):
     parts, out = refs[:-1], refs[-1]
     features = parts[0].shape[1]
-    mine = lax.rem(lax.axis_index("seq"), half)
-    for step, part in enumerate(parts):
-        column = jnp.bitwise_xor(mine, step) * features
+    seq = lax.axis_index("seq")
+    near = seq // plan.half == lax.axis_index("head")
+    for step, part in zip(plan.landed, parts):
+        low, high = sorted(plan.turns[step])
+        flip = jnp.where(near, low, high - plan.half)
+        column = jnp.bitwise_xor(lax.rem(seq, plan.half), flip) * features
         out[:, pl.ds(pl.multiple_of(column, features), features)] = part[...]
 
 
-def place(parts, half):
+def place(plan, parts):
     rows, features = parts[0].shape
     vmem = pl.BlockSpec(memory_space=pltpu.VMEM)
     return pl.pallas_call(
-        functools.partial(place_kernel, half),
-        out_shape=jax.ShapeDtypeStruct((rows, features * half), parts[0].dtype),
+        functools.partial(place_kernel, plan),
+        out_shape=jax.ShapeDtypeStruct((rows, features * plan.half), parts[0].dtype),
         in_specs=[vmem] * len(parts),
         out_specs=vmem,
         compiler_params=pltpu.CompilerParams(vmem_limit_bytes=1024 * 1024),
@@ -121,36 +122,49 @@
     )(*parts)
 
 
-def back(count, step):
-    half = count // 2
-    pairs = []
-    for s in range(count):
-        taker = s // half
-        pairs.append((2 * s + taker, 2 * (s ^ (step + half)) + taker))
-        pairs.append((2 * s + 1 - taker, 2 * (s ^ step) + taker))
-    return pairs
-
-
-def direct(count, queries, latent, key_basis, value_basis, out_weight):
-    rows, half = queries.shape[0], count // 2
+class Plan:
+    def __init__(self, count):
+        self.count, self.half = count, count // 2
+        if count == 8:
+            self.out, self.again = (3, 2, 1), (3, 2, 1)
+            self.turns = ((7, 2), (5, 3), (4, 0), (6, 1))
+        else:
+            self.out = self.again = tuple(reversed(range(1, self.half)))
+            self.turns = tuple((i + self.half, i) for i in reversed(range(self.half)))
+        sent = (self.half, *self.out, *(flip + self.half for flip in self.again))
+        self.order = (0, *reversed(sent))
+        self.landed = tuple(reversed(range(self.half)))
+
+    def flip(self, flip):
+        return [(i, i ^ flip) for i in range(self.count)]
+
+    def back(self, step):
+        pairs = []
+        for s in range(self.count):
+            taker = s // self.half
+            for core, flip in zip((taker, 1 - taker), self.turns[step]):
+                pairs.append((2 * s + core, 2 * (s ^ flip) + taker))
+        return pairs
+
+
+def direct(plan, queries, latent, key_basis, value_basis, out_weight):
+    rows, half = queries.shape[0], plan.half
     own = jnp.concatenate([queries, latent.T], axis=1)
-    blocks = {0: own}
-    for flip in flips(count):
-        blocks[flip] = lax.ppermute(own, "seq", [(i, i ^ flip) for i in range(count)])
+    across = lax.ppermute(own, "seq", plan.flip(half))
+    blocks = {0: own, half: across}
+    for flip in plan.out:
+        blocks[flip] = lax.ppermute(own, "seq", plan.flip(flip))
+    for flip in plan.again:
+        blocks[flip + half] = lax.ppermute(across, "seq", plan.flip(flip))
     weights = hold(key_basis, value_basis, out_weight)
-    keep, send = mix(half, [blocks[k] for k in range(count)], *weights)
+    keep, send = mix(plan, blocks, *weights)
     other = lax.ppermute(send, "head", [(0, 1), (1, 0)])
     total = (keep + other).astype(jnp.bfloat16)
-    parts = [None] * half
-    for step in reversed(range(half)):
-        parts[step] = lax.ppermute(
-            total[step * rows : (step + 1) * rows], ("seq", "head"), back(count, step)
-        )
-    return place(parts, half)
-
-
-def flips(count):
-    return (4, 5, 7, 6, 3, 1, 2) if count == 8 else tuple(reversed(range(1, count)))
+    parts = [
+        lax.ppermute(total[step * rows : (step + 1) * rows], ("seq", "head"), plan.back(step))
+        for step in plan.landed
+    ]
+    return place(plan, parts)
 
 
 def attend(queries, latent, key_basis, value_basis):
@@ -206,8 +220,8 @@
         P("seq", "head"),
     )
     count = mesh.shape["seq"]
-    pairwise = 2 <= count <= MOST_DIRECT and count & (count - 1) == 0 and mesh.shape["head"] == 2
-    shards = functools.partial(direct, count) if pairwise else gathered
+    pairwise = 4 <= count <= MOST_DIRECT and count & (count - 1) == 0 and mesh.shape["head"] == 2
+    shards = functools.partial(direct, Plan(count)) if pairwise else gathered
     return jax.shard_map(
         shards, mesh=mesh, in_specs=placed, out_specs=P(("groups", "seq"), "head"), check_vma=False
     )

time: 31.1 us -> 28.5 us (0.916)
  waiting for transfers between devices: 8.17 us -> 6.45 us
  starting transfers between devices: 17.6 us -> 16.6 us
    ppermute x11, starting transfers between devices: 16 us -> 14.1 us  [the longest x4 5.69 us: direct(): lax.ppermute(total[step * rows:(step + 1) * rows], ('seq', 'head'), plan....]
    ppermute x11, waiting for transfers between devices: 7.22 us -> 5.5 us  [the longest x4 3.86 us: direct(): lax.ppermute(total[step * rows:(step + 1) * rows], ('seq', 'head'), plan....]
    ppermute x1, starting transfers between devices: 1.62 us -> 2.52 us  [direct(): other = lax.ppermute(send, 'head', [(0, 1), (1, 0)])]
  transfers between devices with their start and end apart: 12 -> 12, of which waited for: 6 -> 6; matrix products, arithmetic and copies ran while one was open for 0% -> 0% of each run, Pallas kernels for 7% -> 8%
where the time goes in v3:
time: 28.5 us; the launch traced here: 28.2 us
  starting transfers between devices  16.6 us (58%)
  waiting for transfers between devices  6.45 us (23%)
  Pallas kernels  4.26 us (15%)
  other arithmetic  0.83 us (3%)
    ppermute x4, starting transfers between devices, direct(): lax.ppermute(total[step * rows:(step + 1) * rows], ('seq', 'head'), plan....  5.69 us
    ppermute x4, waiting for transfers between devices, direct(): lax.ppermute(total[step * rows:(step + 1) * rows], ('seq', 'head'), plan....  3.86 us
    ppermute x1, starting transfers between devices, direct(): across = lax.ppermute(own, 'seq', plan.flip(half))  3.14 us
    ppermute x3, starting transfers between devices, direct(): blocks[flip + half] = lax.ppermute(across, 'seq', plan.flip(flip))  2.65 us
    ppermute x3, starting transfers between devices, direct(): blocks[flip] = lax.ppermute(own, 'seq', plan.flip(flip))  2.65 us
    ppermute x1, starting transfers between devices, direct(): other = lax.ppermute(send, 'head', [(0, 1), (1, 0)])  2.52 us
    pallas_call x1, Pallas kernels, hold(): pl.pallas_call(hold_kernel, out_shape=[jax.ShapeDtypeStruct(w.shape, w.dt...  2.24 us
    ppermute x3, waiting for transfers between devices, direct(): blocks[flip + half] = lax.ppermute(across, 'seq', plan.flip(flip))  1.63 us
  transfers between devices with their start and end apart: 12, of which 6 were waited for; matrix products, arithmetic and copies ran while one was open for 0% of the time, Pallas kernels for 8%

profile of v3, /device:TPU:1, one launch (start us, length us, event | category | flops | bytes accessed | tf_op | source)
XLA Modules:
  0.0 28.2 jit_solution(3775390068235442968)
XLA Ops:
  0.0 0.8 %pad_maximum_fusion.refs_0_ = bf16[16,2048]{1,0:T(8,128)(2,1)S(1)} fusion(bf16[16,512]{1,0:T(8,128)(2,1)} %bitcast.1, bf16[16,1536]{1,0:T(8,128)(2,1)} %param.5), kind=kLoop, calls=%fused_computation.1 | loop fusion | flops 131072 | bytes 131072 | tf_op jit(solution)/shard_map/concatenate | solution.py:152
  0.8 3.1 %collective-permute-start = (bf16[16,2048]{1,0:T(8,128)(2,1)S(1)}, bf16[16,2048]{1,0:T(8,128)(2,1)S(1)}, u32[]{:S(2)}, u32[]{:S(2)}) collective-permute-start(bf16[16,2048]{1,0:T(8,128)(2,1)S(1)} %pad_maximum_fusion.refs_0_), channel_id=1, source_target_pairs={{0,8},{2,10},{4,12},{6,14},{8,0},{10,2},{12,4},{14,6},{1,9},{3,11}... | collective-permute-start | bytes 196616 | tf_op jit(solution)/shard_map/ppermute | solution.py:153
  4.0 2.2 %collective-permute-start.6 = (bf16[16,2048]{1,0:T(8,128)(2,1)S(1)}, bf16[16,2048]{1,0:T(8,128)(2,1)S(1)}, u32[]{:S(2)}, u32[]{:S(2)}) collective-permute-start(bf16[16,2048]{1,0:T(8,128)(2,1)S(1)} %pad_maximum_fusion.refs_0_), channel_id=1, source_target_pairs={{0,6},{2,4},{4,2},{6,0},{8,14},{10,12},{12,10},{14,8},{1,7},{3,5},... | collective-permute-start | bytes 196616 | tf_op jit(solution)/shard_map/ppermute | solution.py:156
  6.2 0.2 collective-permute-start.5
  6.4 0.3 collective-permute-start.4
  6.6 0.0 collective-permute-done.refs_7_
  6.6 2.2 %collective-permute-start.3 = (bf16[16,2048]{1,0:T(8,128)(2,1)S(1)}, bf16[16,2048]{1,0:T(8,128)(2,1)S(1)}, u32[]{:S(2)}, u32[]{:S(2)}) collective-permute-start(bf16[16,2048]{1,0:T(8,128)(2,1)S(1)} %collective-permute-done.refs_7_), channel_id=1, source_target_pairs={{0,6},{2,4},{4,2},{6,0},{8,14},{10,12},{12,10},{14,8},{1,7},{3,5},... | collective-permute-start | bytes 196616 | tf_op jit(solution)/shard_map/ppermute | solution.py:158
  8.8 0.2 collective-permute-start.2
  9.0 0.0 collective-permute-done.6.refs_6_
  9.0 0.3 collective-permute-start.1
  9.3 2.2 %hold.1 = (bf16[512,1536]{1,0:T(8,128)(2,1)S(1)}, bf16[512,1536]{1,0:T(8,128)(2,1)S(1)}, bf16[384,1536]{1,0:T(8,128)(2,1)S(1)}) custom-call(bf16[512,1536]{1,0:T(8,128)(2,1)} %refs_0_.1, bf16[512,1536]{1,0:T(8,128)(2,1)} %refs_1_.1, bf16[384,1536]{1,0:T(8,128)(2,1)} %refs_2_.1), custom_call_target="tpu_custom_call" | custom-call | bytes 8650752 | tf_op jit(solution)/shard_map/hold/pallas_call | solution.py:30
  11.5 0.0 collective-permute-done.5.refs_5_
  11.5 0.0 collective-permute-done.4.refs_4_
  11.5 0.0 collective-permute-done.3.refs_3_
  11.5 0.7 %collective-permute-done.2.refs_2_ = bf16[16,2048]{1,0:T(8,128)(2,1)S(1)} collective-permute-done((bf16[16,2048]{1,0:T(8,128)(2,1)S(1)}, bf16[16,2048]{1,0:T(8,128)(2,1)S(1)}, u32[]{:S(2)}, u32[]{:S(2)}) %collective-permute-start.2) | collective-permute-done | bytes 65568 | tf_op jit(solution)/shard_map/ppermute | solution.py:158
  12.3 0.9 %collective-permute-done.1.refs_1_ = bf16[16,2048]{1,0:T(8,128)(2,1)S(1)} collective-permute-done((bf16[16,2048]{1,0:T(8,128)(2,1)S(1)}, bf16[16,2048]{1,0:T(8,128)(2,1)S(1)}, u32[]{:S(2)}, u32[]{:S(2)}) %collective-permute-start.1) | collective-permute-done | bytes 65568 | tf_op jit(solution)/shard_map/ppermute | solution.py:158
  13.2 1.4 %mix.1 = (f32[64,384]{1,0:T(8,128)S(1)}, f32[64,384]{1,0:T(8,128)S(1)}) custom-call(bf16[16,2048]{1,0:T(8,128)(2,1)S(1)} %pad_maximum_fusion.refs_0_, bf16[16,2048]{1,0:T(8,128)(2,1)S(1)} %collective-permute-done.1.refs_1_, bf16[16,2048]{1,0:T(8,128)(2,1)S(1)} %collective-permute-done.2.refs_2_, bf16[16,2048]{1,0:T(8,128)(2,1)S(1)} %collective-permute-done.3.refs_3_, ...), custom_call_target="tpu_custom_call" | custom-call | flops 654311424 | bytes 4325376 | tf_op jit(solution)/shard_map/mix/pallas_call | solution.py:84
  14.6 2.5 %collective-permute-start.7 = (f32[64,384]{1,0:T(8,128)S(1)}, f32[64,384]{1,0:T(8,128)S(1)}, u32[]{:S(2)}, u32[]{:S(2)}) collective-permute-start(f32[64,384]{1,0:T(8,128)S(1)} %get-tuple-element.14), channel_id=1, source_target_pairs={{0,1},{1,0},{2,3},{3,2},{4,5},{5,4},{6,7},{7,6},{8,9},{9,8},{10,11... | collective-permute-start | bytes 294920 | tf_op jit(solution)/shard_map/ppermute | solution.py:161
  17.1 0.9 %collective-permute-done.7 = f32[64,384]{1,0:T(8,128)S(1)} collective-permute-done((f32[64,384]{1,0:T(8,128)S(1)}, f32[64,384]{1,0:T(8,128)S(1)}, u32[]{:S(2)}, u32[]{:S(2)}) %collective-permute-start.7) | collective-permute-done | bytes 98336 | tf_op jit(solution)/shard_map/ppermute | solution.py:161
  18.1 1.6 %collective-permute-start.11 = (bf16[16,384]{1,0:T(8,128)(2,1)S(1)}, bf16[16,384]{1,0:T(8,128)(2,1)S(1)}, u32[]{:S(2)}, u32[]{:S(2)}) collective-permute-start(bf16[16,384]{1,0:T(8,128)(2,1)S(1)} %get-tuple-element.15), channel_id=1, source_target_pairs={{0,14},{1,4},{2,12},{3,6},{4,10},{5,0},{6,8},{7,2},{9,7},{8,13},{1... | collective-permute-start | bytes 36872 | tf_op jit(solution)/shard_map/ppermute | solution.py:164
  19.7 2.1 %collective-permute-start.10 = (bf16[16,384]{1,0:T(8,128)(2,1)S(1)}, bf16[16,384]{1,0:T(8,128)(2,1)S(1)}, u32[]{:S(2)}, u32[]{:S(2)}) collective-permute-start(bf16[16,384]{1,0:T(8,128)(2,1)S(1)} %get-tuple-element.16), channel_id=1, source_target_pairs={{0,10},{1,6},{2,8},{3,4},{4,14},{5,2},{6,12},{7,0},{9,3},{8,15},{1... | collective-permute-start | bytes 36872 | tf_op jit(solution)/shard_map/ppermute | solution.py:164
  21.8 0.6 %collective-permute-start.9 = (bf16[16,384]{1,0:T(8,128)(2,1)S(1)}, bf16[16,384]{1,0:T(8,128)(2,1)S(1)}, u32[]{:S(2)}, u32[]{:S(2)}) collective-permute-start(bf16[16,384]{1,0:T(8,128)(2,1)S(1)} %get-tuple-element.17), channel_id=1, source_target_pairs={{0,8},{1,0},{2,10},{3,2},{4,12},{5,4},{6,14},{7,6},{9,1},{8,9},{11... | collective-permute-start | bytes 36872 | tf_op jit(solution)/shard_map/ppermute | solution.py:164
  22.4 1.3 %collective-permute-start.8 = (bf16[16,384]{1,0:T(8,128)(2,1)S(1)}, bf16[16,384]{1,0:T(8,128)(2,1)S(1)}, u32[]{:S(2)}, u32[]{:S(2)}) collective-permute-start(bf16[16,384]{1,0:T(8,128)(2,1)S(1)} %get-tuple-element.18), channel_id=1, source_target_pairs={{0,12},{1,2},{2,14},{3,0},{4,8},{5,6},{6,10},{7,4},{9,5},{8,11},{1... | collective-permute-start | bytes 36872 | tf_op jit(solution)/shard_map/ppermute | solution.py:164
  23.8 0.0 collective-permute-done.11.refs_3_
  23.8 0.3 collective-permute-done.10.refs_2_
  24.0 1.2 %collective-permute-done.9.refs_1_ = bf16[16,384]{1,0:T(8,128)(2,1)S(1)} collective-permute-done((bf16[16,384]{1,0:T(8,128)(2,1)S(1)}, bf16[16,384]{1,0:T(8,128)(2,1)S(1)}, u32[]{:S(2)}, u32[]{:S(2)}) %collective-permute-start.9) | collective-permute-done | bytes 12320 | tf_op jit(solution)/shard_map/ppermute | solution.py:164
  25.2 2.4 %collective-permute-done.8.refs_0_ = bf16[16,384]{1,0:T(8,128)(2,1)S(1)} collective-permute-done((bf16[16,384]{1,0:T(8,128)(2,1)S(1)}, bf16[16,384]{1,0:T(8,128)(2,1)S(1)}, u32[]{:S(2)}, u32[]{:S(2)}) %collective-permute-start.8) | collective-permute-done | bytes 12320 | tf_op jit(solution)/shard_map/ppermute | solution.py:164
  27.6 0.6 %place.1 = bf16[16,1536]{1,0:T(8,128)(2,1)} custom-call(bf16[16,384]{1,0:T(8,128)(2,1)S(1)} %collective-permute-done.8.refs_0_, bf16[16,384]{1,0:T(8,128)(2,1)S(1)} %collective-permute-done.9.refs_1_, bf16[16,384]{1,0:T(8,128)(2,1)S(1)} %collective-permute-done.10.refs_2_, bf16[16,384]{1,0:T(8,128)(2,1)S(1)} %collective-permute-done.11.refs_3_), custom_call_target="tpu_custom_call" | custom-call | tf_op jit(solution)/shard_map/place/pallas_call | solution.py:115
  (2 shorter events, 0.0 us)
Async XLA Ops:
  0.8 5.8 %collective-permute-start = (bf16[16,2048]{1,0:T(8,128)(2,1)S(1)}, bf16[16,2048]{1,0:T(8,128)(2,1)S(1)}, u32[]{:S(2)}, u32[]{:S(2)}) collective-permute-start(bf16[16,2048]{1,0:T(8,128)(2,1)S(1)} %pad_maximum_fusion.refs_0_), channel_id=1, source_target_pairs={{0,8},{2,10},{4,12},{6,14},{8,0},{10,2},{12,4},{14,6},{1,9},{3,11}... | collective-permute-start | bytes 196616 | tf_op jit(solution)/shard_map/ppermute | solution.py:153
  4.0 5.0 %collective-permute-start.6 = (bf16[16,2048]{1,0:T(8,128)(2,1)S(1)}, bf16[16,2048]{1,0:T(8,128)(2,1)S(1)}, u32[]{:S(2)}, u32[]{:S(2)}) collective-permute-start(bf16[16,2048]{1,0:T(8,128)(2,1)S(1)} %pad_maximum_fusion.refs_0_), channel_id=1, source_target_pairs={{0,6},{2,4},{4,2},{6,0},{8,14},{10,12},{12,10},{14,8},{1,7},{3,5},... | collective-permute-start | bytes 196616 | tf_op jit(solution)/shard_map/ppermute | solution.py:156
  6.2 5.3 %collective-permute-start.5 = (bf16[16,2048]{1,0:T(8,128)(2,1)S(1)}, bf16[16,2048]{1,0:T(8,128)(2,1)S(1)}, u32[]{:S(2)}, u32[]{:S(2)}) collective-permute-start(bf16[16,2048]{1,0:T(8,128)(2,1)S(1)} %pad_maximum_fusion.refs_0_), channel_id=1, source_target_pairs={{0,4},{2,6},{4,0},{6,2},{8,12},{10,14},{12,8},{14,10},{1,5},{3,7},... | collective-permute-start | bytes 196616 | tf_op jit(solution)/shard_map/ppermute | solution.py:156
  6.4 5.2 %collective-permute-start.4 = (bf16[16,2048]{1,0:T(8,128)(2,1)S(1)}, bf16[16,2048]{1,0:T(8,128)(2,1)S(1)}, u32[]{:S(2)}, u32[]{:S(2)}) collective-permute-start(bf16[16,2048]{1,0:T(8,128)(2,1)S(1)} %pad_maximum_fusion.refs_0_), channel_id=1, source_target_pairs={{0,2},{2,0},{4,6},{6,4},{8,10},{10,8},{12,14},{14,12},{1,3},{3,1},... | collective-permute-start | bytes 196616 | tf_op jit(solution)/shard_map/ppermute | solution.py:156
  6.6 4.9 %collective-permute-start.3 = (bf16[16,2048]{1,0:T(8,128)(2,1)S(1)}, bf16[16,2048]{1,0:T(8,128)(2,1)S(1)}, u32[]{:S(2)}, u32[]{:S(2)}) collective-permute-start(bf16[16,2048]{1,0:T(8,128)(2,1)S(1)} %collective-permute-done.refs_7_), channel_id=1, source_target_pairs={{0,6},{2,4},{4,2},{6,0},{8,14},{10,12},{12,10},{14,8},{1,7},{3,5},... | collective-permute-start | bytes 196616 | tf_op jit(solution)/shard_map/ppermute | solution.py:158
  8.8 3.4 %collective-permute-start.2 = (bf16[16,2048]{1,0:T(8,128)(2,1)S(1)}, bf16[16,2048]{1,0:T(8,128)(2,1)S(1)}, u32[]{:S(2)}, u32[]{:S(2)}) collective-permute-start(bf16[16,2048]{1,0:T(8,128)(2,1)S(1)} %collective-permute-done.refs_7_), channel_id=1, source_target_pairs={{0,4},{2,6},{4,0},{6,2},{8,12},{10,14},{12,8},{14,10},{1,5},{3,7},... | collective-permute-start | bytes 196616 | tf_op jit(solution)/shard_map/ppermute | solution.py:158
  9.0 4.2 %collective-permute-start.1 = (bf16[16,2048]{1,0:T(8,128)(2,1)S(1)}, bf16[16,2048]{1,0:T(8,128)(2,1)S(1)}, u32[]{:S(2)}, u32[]{:S(2)}) collective-permute-start(bf16[16,2048]{1,0:T(8,128)(2,1)S(1)} %collective-permute-done.refs_7_), channel_id=1, source_target_pairs={{0,2},{2,0},{4,6},{6,4},{8,10},{10,8},{12,14},{14,12},{1,3},{3,1},... | collective-permute-start | bytes 196616 | tf_op jit(solution)/shard_map/ppermute | solution.py:158
  14.6 3.5 %collective-permute-start.7 = (f32[64,384]{1,0:T(8,128)S(1)}, f32[64,384]{1,0:T(8,128)S(1)}, u32[]{:S(2)}, u32[]{:S(2)}) collective-permute-start(f32[64,384]{1,0:T(8,128)S(1)} %get-tuple-element.14), channel_id=1, source_target_pairs={{0,1},{1,0},{2,3},{3,2},{4,5},{5,4},{6,7},{7,6},{8,9},{9,8},{10,11... | collective-permute-start | bytes 294920 | tf_op jit(solution)/shard_map/ppermute | solution.py:161
  18.1 5.7 %collective-permute-start.11 = (bf16[16,384]{1,0:T(8,128)(2,1)S(1)}, bf16[16,384]{1,0:T(8,128)(2,1)S(1)}, u32[]{:S(2)}, u32[]{:S(2)}) collective-permute-start(bf16[16,384]{1,0:T(8,128)(2,1)S(1)} %get-tuple-element.15), channel_id=1, source_target_pairs={{0,14},{1,4},{2,12},{3,6},{4,10},{5,0},{6,8},{7,2},{9,7},{8,13},{1... | collective-permute-start | bytes 36872 | tf_op jit(solution)/shard_map/ppermute | solution.py:164
  19.7 4.4 %collective-permute-start.10 = (bf16[16,384]{1,0:T(8,128)(2,1)S(1)}, bf16[16,384]{1,0:T(8,128)(2,1)S(1)}, u32[]{:S(2)}, u32[]{:S(2)}) collective-permute-start(bf16[16,384]{1,0:T(8,128)(2,1)S(1)} %get-tuple-element.16), channel_id=1, source_target_pairs={{0,10},{1,6},{2,8},{3,4},{4,14},{5,2},{6,12},{7,0},{9,3},{8,15},{1... | collective-permute-start | bytes 36872 | tf_op jit(solution)/shard_map/ppermute | solution.py:164
  21.8 3.4 %collective-permute-start.9 = (bf16[16,384]{1,0:T(8,128)(2,1)S(1)}, bf16[16,384]{1,0:T(8,128)(2,1)S(1)}, u32[]{:S(2)}, u32[]{:S(2)}) collective-permute-start(bf16[16,384]{1,0:T(8,128)(2,1)S(1)} %get-tuple-element.17), channel_id=1, source_target_pairs={{0,8},{1,0},{2,10},{3,2},{4,12},{5,4},{6,14},{7,6},{9,1},{8,9},{11... | collective-permute-start | bytes 36872 | tf_op jit(solution)/shard_map/ppermute | solution.py:164
  22.4 5.2 %collective-permute-start.8 = (bf16[16,384]{1,0:T(8,128)(2,1)S(1)}, bf16[16,384]{1,0:T(8,128)(2,1)S(1)}, u32[]{:S(2)}, u32[]{:S(2)}) collective-permute-start(bf16[16,384]{1,0:T(8,128)(2,1)S(1)} %get-tuple-element.18), channel_id=1, source_target_pairs={{0,12},{1,2},{2,14},{3,0},{4,8},{5,6},{6,10},{7,4},{9,5},{8,11},{1... | collective-permute-start | bytes 36872 | tf_op jit(solution)/shard_map/ppermute | solution.py:164

commit v4 on v3

--- a/solution.py
+++ b/solution.py
@@ -13,41 +13,13 @@
 NT = (((1,), (1,)), ((), ()))
 
 
-def hold_kernel(*refs):
-    count = (len(refs) - 1) // 2
-    copies = [
-        pltpu.make_async_copy(source, kept, refs[-1].at[i])
-        for i, (source, kept) in enumerate(zip(refs[:count], refs[count:-1]))
-    ]
-    for copy in copies:
-        copy.start()
-    for copy in copies:
-        copy.wait()
-
-
-def hold(*weights):
-    vmem = pl.BlockSpec(memory_space=pltpu.VMEM)
-    return pl.pallas_call(
-        hold_kernel,
-        out_shape=[jax.ShapeDtypeStruct(w.shape, w.dtype) for w in weights],
-        in_specs=[pl.BlockSpec(memory_space=pltpu.HBM)] * len(weights),
-        out_specs=[vmem] * len(weights),
-        scratch_shapes=[pltpu.SemaphoreType.DMA((len(weights),))],
-        cost_estimate=pl.CostEstimate(
-            flops=0, bytes_accessed=sum(4 * w.size for w in weights), transcendentals=0
-        ),
-        compiler_params=pltpu.CompilerParams(vmem_limit_bytes=1024 * 1024),
-        name="hold",
-    )(*(pltpu.with_memory_space_constraint(w, pltpu.HBM) for w in weights))
-
-
-def mix_kernel(plan, *refs):
-    blocks = [refs[plan.order.index(flip)] for flip in range(plan.count)]
-    key_basis, value_basis, out_weight, keep, send, partial_sum = refs[plan.count :]
-    rows = blocks[0].shape[0]
+def mix_kernel(plan, own, *refs):
+    received = refs[: len(plan.routes)][::-1]
+    key_basis, value_basis, out_weight, keep, send, partial_sum = refs[len(plan.routes) :]
+    rows = own.shape[0]
     width = key_basis.shape[1]
-    queries = jnp.concatenate([b[:, :width] for b in blocks], axis=0)
-    latent = jnp.concatenate([b[:, width:] for b in blocks], axis=0)
+    queries = jnp.concatenate([b[:, :width] for b in (own, *received)], axis=0)
+    latent = jnp.concatenate([b[:, width:] for b in (own, *received)], axis=0)
     scale = 1.0 / math.sqrt(HEAD_DIM)
     heads = [slice(first, first + HEAD_DIM) for first in range(0, width, HEAD_DIM)]
     keys = jnp.dot(latent, key_basis[...], preferred_element_type=jnp.float32).astype(jnp.bfloat16)
@@ -70,21 +42,23 @@
     )
     taker = lax.axis_index("head") == lax.axis_index("seq") // plan.half
     for step, flips in enumerate(plan.turns):
-        first, second = (partial_sum[flip * rows : (flip + 1) * rows, :] for flip in flips)
+        first, second = (
+            partial_sum[at * rows : (at + 1) * rows, :] for at in map(plan.held.index, flips)
+        )
         part = slice(step * rows, (step + 1) * rows)
         keep[part, :] = jnp.where(taker, first, second)
         send[part, :] = jnp.where(taker, second, first)
 
 
-def mix(plan, blocks, key_basis, value_basis, out_weight):
-    rows = blocks[0].shape[0] * plan.count
+def mix(plan, own, received, key_basis, value_basis, out_weight):
+    rows = own.shape[0] * plan.count
     rank, width = key_basis.shape
     features = out_weight.shape[0]
     vmem = pl.BlockSpec(memory_space=pltpu.VMEM)
     return pl.pallas_call(
         functools.partial(mix_kernel, plan),
         out_shape=[jax.ShapeDtypeStruct((rows // 2, features), jnp.float32)] * 2,
-        in_specs=[vmem] * (plan.count + 3),
+        in_specs=[vmem] * (len(received) + 4),
         out_specs=[vmem] * 2,
         scratch_shapes=[pltpu.VMEM((rows, features), jnp.float32)],
         cost_estimate=pl.CostEstimate(
@@ -94,7 +68,7 @@
         ),
         compiler_params=pltpu.CompilerParams(vmem_limit_bytes=16 * 1024 * 1024),
         name="mix",
-    )(*(blocks[flip] for flip in plan.order), key_basis, value_basis, out_weight)
+    )(own, *received[::-1], key_basis, value_basis, out_weight)
 
 
 def place_kernel(plan, *refs):
@@ -122,21 +96,41 @@
     )(*parts)
 
 
+def pack_kernel(block, own):
+    own[...] = block[...]
+
+
+def pack(block, meanwhile):
+    vmem = pl.BlockSpec(memory_space=pltpu.VMEM)
+    return pl.pallas_call(
+        pack_kernel,
+        out_shape=jax.ShapeDtypeStruct(block.shape, block.dtype),
+        in_specs=[vmem],
+        out_specs=vmem,
+        cost_estimate=pl.CostEstimate(
+            flops=4096 * meanwhile, bytes_accessed=0, transcendentals=0
+        ),
+        compiler_params=pltpu.CompilerParams(vmem_limit_bytes=1024 * 1024),
+        name="pack",
+    )(block)
+
+
 class Plan:
     def __init__(self, count):
         self.count, self.half = count, count // 2
         if count == 8:
-            self.out, self.again = (3, 2, 1), (3, 2, 1)
-            self.turns = ((7, 2), (5, 3), (4, 0), (6, 1))
+            self.routes = ((1, (0,)), (6, (0,)), (4, (0,)), (2, (0,)), (4, (1,)), (2, (1,)), (1, (6,)))
+            self.turns = ((5, 3), (6, 0), (7, 2), (4, 1))
         else:
-            self.out = self.again = tuple(reversed(range(1, self.half)))
+            inner = tuple(reversed(range(1, self.half)))
+            self.routes = (
+                (self.half, (0,)),
+                *((flip, (0,)) for flip in inner),
+                *((flip, (self.half,)) for flip in inner),
+            )
             self.turns = tuple((i + self.half, i) for i in reversed(range(self.half)))
-        sent = (self.half, *self.out, *(flip + self.half for flip in self.again))
-        self.order = (0, *reversed(sent))
+        self.held = (0, *(flip ^ block for flip, blocks in self.routes for block in blocks))
         self.landed = tuple(reversed(range(self.half)))
-
-    def flip(self, flip):
-        return [(i, i ^ flip) for i in range(self.count)]
 
     def back(self, step):
         pairs = []
@@ -147,17 +141,25 @@
         return pairs
 
 
+def gather(plan, own):
+    rows = own.shape[0]
+    blocks, received = {0: own}, []
+    for flip, names in plan.routes:
+        sent = [blocks[name] for name in names]
+        sent = sent[0] if len(sent) == 1 else jnp.concatenate(sent, axis=0)
+        received.append(lax.ppermute(sent, "seq", [(i, i ^ flip) for i in range(plan.count)]))
+        for at, name in enumerate(names):
+            blocks[flip ^ name] = received[-1][at * rows : (at + 1) * rows]
+    return received
+
+
 def direct(plan, queries, latent, key_basis, value_basis, out_weight):
-    rows, half = queries.shape[0], plan.half
+    rows = queries.shape[0]
+    weights = key_basis, value_basis, out_weight
     own = jnp.concatenate([queries, latent.T], axis=1)
-    across = lax.ppermute(own, "seq", plan.flip(half))
-    blocks = {0: own, half: across}
-    for flip in plan.out:
-        blocks[flip] = lax.ppermute(own, "seq", plan.flip(flip))
-    for flip in plan.again:
-        blocks[flip + half] = lax.ppermute(across, "seq", plan.flip(flip))
-    weights = hold(key_basis, value_basis, out_weight)
-    keep, send = mix(plan, blocks, *weights)
+    own = pack(own, sum(2 * w.size for w in weights))
+    received = gather(plan, own)
+    keep, send = mix(plan, own, received, *weights)
     other = lax.ppermute(send, "head", [(0, 1), (1, 0)])
     total = (keep + other).astype(jnp.bfloat16)
     parts = [

time: 28.5 us -> 26.7 us (0.937)
  the two profiles are of different devices: /device:TPU:1 before, /device:TPU:0 now
where the time goes in v4:
time: 26.7 us; the launch traced here: 26.5 us
  starting transfers between devices  16.2 us (61%)
  waiting for transfers between devices  7.35 us (28%)
  Pallas kernels  2.02 us (8%)
  other arithmetic  0.83 us (3%)
    ppermute x7, starting transfers between devices, gather(): lax.ppermute(sent, 'seq', [(i, i ^ flip) for i in range(plan.count)])  12.1 us
    ppermute x4, starting transfers between devices, direct(): lax.ppermute(total[step * rows:(step + 1) * rows], ('seq', 'head'), plan....  4 us
    ppermute x7, waiting for transfers between devices, gather(): lax.ppermute(sent, 'seq', [(i, i ^ flip) for i in range(plan.count)])  3.73 us
    ppermute x4, waiting for transfers between devices, direct(): lax.ppermute(total[step * rows:(step + 1) * rows], ('seq', 'head'), plan....  2.33 us
    pallas_call x1, Pallas kernels, mix(): pl.pallas_call(functools.partial(mix_kernel, plan), out_shape=[jax.ShapeD...  1.39 us
    ppermute x1, waiting for transfers between devices, direct(): other = lax.ppermute(send, 'head', [(0, 1), (1, 0)])  1.29 us
    concatenate x1, other arithmetic, direct(): own = jnp.concatenate([queries, latent.T], axis=1)  0.82 us
    pallas_call x1, Pallas kernels, place(): pl.pallas_call(functools.partial(place_kernel, plan), out_shape=jax.Shape...  0.63 us
  transfers between devices with their start and end apart: 12, of which 7 were waited for; matrix products, arithmetic and copies ran while one was open for 0% of the time, Pallas kernels for 0%

profile of v4, /device:TPU:0, one launch (start us, length us, event | category | flops | bytes accessed | tf_op | source)
XLA Modules:
  0.0 26.5 jit_solution(4456415301956285619)
XLA Ops:
  0.0 0.8 %pad_maximum_fusion.block = bf16[16,2048]{1,0:T(8,128)(2,1)S(1)} fusion(bf16[16,512]{1,0:T(8,128)(2,1)} %bitcast.1, bf16[16,1536]{1,0:T(8,128)(2,1)} %param.5), kind=kLoop, calls=%fused_computation.1 | loop fusion | flops 131072 | bytes 131072 | tf_op jit(solution)/shard_map/concatenate | solution.py:159
  0.8 0.0 copy-start
  0.8 0.0 copy-start.1
  0.8 0.0 copy-start.2
  0.9 3.0 %collective-permute-start.2 = (bf16[16,2048]{1,0:T(8,128)(2,1)S(1)}, bf16[16,2048]{1,0:T(8,128)(2,1)S(1)}, u32[]{:S(2)}, u32[]{:S(2)}) collective-permute-start(bf16[16,2048]{1,0:T(8,128)(2,1)S(1)} %pack.1.own), channel_id=1, source_target_pairs={{0,2},{2,0},{4,6},{6,4},{8,10},{10,8},{12,14},{14,12},{1,3},{3,1},... | collective-permute-start | bytes 196616 | tf_op jit(solution)/shard_map/ppermute | solution.py:150
  3.9 3.6 %collective-permute-start = (bf16[16,2048]{1,0:T(8,128)(2,1)S(1)}, bf16[16,2048]{1,0:T(8,128)(2,1)S(1)}, u32[]{:S(2)}, u32[]{:S(2)}) collective-permute-start(bf16[16,2048]{1,0:T(8,128)(2,1)S(1)} %pack.1.own), channel_id=1, source_target_pairs={{0,12},{2,14},{4,8},{6,10},{8,4},{10,6},{12,0},{14,2},{1,13},{3,15... | collective-permute-start | bytes 196616 | tf_op jit(solution)/shard_map/ppermute | solution.py:150
  7.5 0.0 collective-permute-start.6
  7.5 0.8 %collective-permute-start.5 = (bf16[16,2048]{1,0:T(8,128)(2,1)S(1)}, bf16[16,2048]{1,0:T(8,128)(2,1)S(1)}, u32[]{:S(2)}, u32[]{:S(2)}) collective-permute-start(bf16[16,2048]{1,0:T(8,128)(2,1)S(1)} %pack.1.own), channel_id=1, source_target_pairs={{0,4},{2,6},{4,0},{6,2},{8,12},{10,14},{12,8},{14,10},{1,5},{3,7},... | collective-permute-start | bytes 196616 | tf_op jit(solution)/shard_map/ppermute | solution.py:150
  8.2 0.0 collective-permute-done.2.refs_6_
  8.3 2.1 %collective-permute-start.4 = (bf16[16,2048]{1,0:T(8,128)(2,1)S(1)}, bf16[16,2048]{1,0:T(8,128)(2,1)S(1)}, u32[]{:S(2)}, u32[]{:S(2)}) collective-permute-start(bf16[16,2048]{1,0:T(8,128)(2,1)S(1)} %collective-permute-done.2.refs_6_), channel_id=1, source_target_pairs={{0,8},{2,10},{4,12},{6,14},{8,0},{10,2},{12,4},{14,6},{1,9},{3,11}... | collective-permute-start | bytes 196616 | tf_op jit(solution)/shard_map/ppermute | solution.py:150
  10.4 2.0 %collective-permute-start.3 = (bf16[16,2048]{1,0:T(8,128)(2,1)S(1)}, bf16[16,2048]{1,0:T(8,128)(2,1)S(1)}, u32[]{:S(2)}, u32[]{:S(2)}) collective-permute-start(bf16[16,2048]{1,0:T(8,128)(2,1)S(1)} %collective-permute-done.2.refs_6_), channel_id=1, source_target_pairs={{0,4},{2,6},{4,0},{6,2},{8,12},{10,14},{12,8},{14,10},{1,5},{3,7},... | collective-permute-start | bytes 196616 | tf_op jit(solution)/shard_map/ppermute | solution.py:150
  12.4 0.0 collective-permute-done.refs_5_
  12.4 0.5 %collective-permute-start.1 = (bf16[16,2048]{1,0:T(8,128)(2,1)S(1)}, bf16[16,2048]{1,0:T(8,128)(2,1)S(1)}, u32[]{:S(2)}, u32[]{:S(2)}) collective-permute-start(bf16[16,2048]{1,0:T(8,128)(2,1)S(1)} %collective-permute-done.refs_5_), channel_id=1, source_target_pairs={{0,2},{2,0},{4,6},{6,4},{8,10},{10,8},{12,14},{14,12},{1,3},{3,1},... | collective-permute-start | bytes 196616 | tf_op jit(solution)/shard_map/ppermute | solution.py:150
  13.0 1.2 %collective-permute-done.6.refs_4_ = bf16[16,2048]{1,0:T(8,128)(2,1)S(1)} collective-permute-done((bf16[16,2048]{1,0:T(8,128)(2,1)S(1)}, bf16[16,2048]{1,0:T(8,128)(2,1)S(1)}, u32[]{:S(2)}, u32[]{:S(2)}) %collective-permute-start.6) | collective-permute-done | bytes 65568 | tf_op jit(solution)/shard_map/ppermute | solution.py:150
  14.2 0.0 collective-permute-done.5.refs_3_
  14.2 1.5 %collective-permute-done.4.refs_2_ = bf16[16,2048]{1,0:T(8,128)(2,1)S(1)} collective-permute-done((bf16[16,2048]{1,0:T(8,128)(2,1)S(1)}, bf16[16,2048]{1,0:T(8,128)(2,1)S(1)}, u32[]{:S(2)}, u32[]{:S(2)}) %collective-permute-start.4) | collective-permute-done | bytes 65568 | tf_op jit(solution)/shard_map/ppermute | solution.py:150
  15.7 0.0 collective-permute-done.3.refs_1_
  15.7 1.0 %collective-permute-done.1.refs_0_ = bf16[16,2048]{1,0:T(8,128)(2,1)S(1)} collective-permute-done((bf16[16,2048]{1,0:T(8,128)(2,1)S(1)}, bf16[16,2048]{1,0:T(8,128)(2,1)S(1)}, u32[]{:S(2)}, u32[]{:S(2)}) %collective-permute-start.1) | collective-permute-done | bytes 65568 | tf_op jit(solution)/shard_map/ppermute | solution.py:150
  16.7 0.0 copy-done
  16.7 0.0 copy-done.1
  16.7 0.0 copy-done.2
  16.7 1.4 %mix.1 = (f32[64,384]{1,0:T(8,128)S(1)}, f32[64,384]{1,0:T(8,128)S(1)}) custom-call(bf16[16,2048]{1,0:T(8,128)(2,1)S(1)} %pack.1.own, bf16[16,2048]{1,0:T(8,128)(2,1)S(1)} %collective-permute-done.1.refs_0_, bf16[16,2048]{1,0:T(8,128)(2,1)S(1)} %collective-permute-done.3.refs_1_, bf16[16,2048]{1,0:T(8,128)(2,1)S(1)} %collective-permute-done.4.refs_2_, ...), custom_call_target="tpu_custom_call" | custom-call | flops 654311424 | bytes 4325376 | tf_op jit(solution)/shard_map/mix/pallas_call | solution.py:58
  18.1 0.1 collective-permute-start.7
  18.2 1.3 %collective-permute-done.7 = f32[64,384]{1,0:T(8,128)S(1)} collective-permute-done((f32[64,384]{1,0:T(8,128)S(1)}, f32[64,384]{1,0:T(8,128)S(1)}, u32[]{:S(2)}, u32[]{:S(2)}) %collective-permute-start.7) | collective-permute-done | bytes 98336 | tf_op jit(solution)/shard_map/ppermute | solution.py:163
  19.5 0.5 %collective-permute-start.11 = (bf16[16,384]{1,0:T(8,128)(2,1)S(1)}, bf16[16,384]{1,0:T(8,128)(2,1)S(1)}, u32[]{:S(2)}, u32[]{:S(2)}) collective-permute-start(bf16[16,384]{1,0:T(8,128)(2,1)S(1)} %get-tuple-element.9), channel_id=1, source_target_pairs={{0,10},{1,6},{2,8},{3,4},{4,14},{5,2},{6,12},{7,0},{9,3},{8,15},{1... | collective-permute-start | bytes 36872 | tf_op jit(solution)/shard_map/ppermute | solution.py:166
  20.0 1.6 %collective-permute-start.10 = (bf16[16,384]{1,0:T(8,128)(2,1)S(1)}, bf16[16,384]{1,0:T(8,128)(2,1)S(1)}, u32[]{:S(2)}, u32[]{:S(2)}) collective-permute-start(bf16[16,384]{1,0:T(8,128)(2,1)S(1)} %get-tuple-element.10), channel_id=1, source_target_pairs={{0,12},{1,0},{2,14},{3,2},{4,8},{5,4},{6,10},{7,6},{9,5},{8,9},{11... | collective-permute-start | bytes 36872 | tf_op jit(solution)/shard_map/ppermute | solution.py:166
  21.6 1.1 %collective-permute-start.9 = (bf16[16,384]{1,0:T(8,128)(2,1)S(1)}, bf16[16,384]{1,0:T(8,128)(2,1)S(1)}, u32[]{:S(2)}, u32[]{:S(2)}) collective-permute-start(bf16[16,384]{1,0:T(8,128)(2,1)S(1)} %get-tuple-element.11), channel_id=1, source_target_pairs={{0,14},{1,4},{2,12},{3,6},{4,10},{5,0},{6,8},{7,2},{9,7},{8,13},{1... | collective-permute-start | bytes 36872 | tf_op jit(solution)/shard_map/ppermute | solution.py:166
  22.7 0.8 %collective-permute-start.8 = (bf16[16,384]{1,0:T(8,128)(2,1)S(1)}, bf16[16,384]{1,0:T(8,128)(2,1)S(1)}, u32[]{:S(2)}, u32[]{:S(2)}) collective-permute-start(bf16[16,384]{1,0:T(8,128)(2,1)S(1)} %get-tuple-element.12), channel_id=1, source_target_pairs={{0,8},{1,2},{2,10},{3,0},{4,12},{5,6},{6,14},{7,4},{9,1},{8,11},{1... | collective-permute-start | bytes 36872 | tf_op jit(solution)/shard_map/ppermute | solution.py:166
  23.5 0.1 collective-permute-done.11.refs_3_
  23.6 0.0 collective-permute-done.10.refs_2_
  23.6 1.1 %collective-permute-done.9.refs_1_ = bf16[16,384]{1,0:T(8,128)(2,1)S(1)} collective-permute-done((bf16[16,384]{1,0:T(8,128)(2,1)S(1)}, bf16[16,384]{1,0:T(8,128)(2,1)S(1)}, u32[]{:S(2)}, u32[]{:S(2)}) %collective-permute-start.9) | collective-permute-done | bytes 12320 | tf_op jit(solution)/shard_map/ppermute | solution.py:166
  24.7 1.1 %collective-permute-done.8.refs_0_ = bf16[16,384]{1,0:T(8,128)(2,1)S(1)} collective-permute-done((bf16[16,384]{1,0:T(8,128)(2,1)S(1)}, bf16[16,384]{1,0:T(8,128)(2,1)S(1)}, u32[]{:S(2)}, u32[]{:S(2)}) %collective-permute-start.8) | collective-permute-done | bytes 12320 | tf_op jit(solution)/shard_map/ppermute | solution.py:166
  25.8 0.6 %place.1 = bf16[16,1536]{1,0:T(8,128)(2,1)} custom-call(bf16[16,384]{1,0:T(8,128)(2,1)S(1)} %collective-permute-done.8.refs_0_, bf16[16,384]{1,0:T(8,128)(2,1)S(1)} %collective-permute-done.9.refs_1_, bf16[16,384]{1,0:T(8,128)(2,1)S(1)} %collective-permute-done.10.refs_2_, bf16[16,384]{1,0:T(8,128)(2,1)S(1)} %collective-permute-done.11.refs_3_), custom_call_target="tpu_custom_call" | custom-call | tf_op jit(solution)/shard_map/place/pallas_call | solution.py:89
  (3 shorter events, 0.0 us)
Async XLA Ops:
  0.8 15.9 %copy-start = (bf16[512,1536]{1,0:T(8,128)(2,1)S(1)}, bf16[512,1536]{1,0:T(8,128)(2,1)}, u32[]{:S(2)}) copy-start(bf16[512,1536]{1,0:T(8,128)(2,1)} %refs_7_.1) | copy-start | bytes 4718596
  0.8 15.9 %copy-start.1 = (bf16[512,1536]{1,0:T(8,128)(2,1)S(1)}, bf16[512,1536]{1,0:T(8,128)(2,1)}, u32[]{:S(2)}) copy-start(bf16[512,1536]{1,0:T(8,128)(2,1)} %refs_8_.1) | copy-start | bytes 4718596
  0.8 15.9 %copy-start.2 = (bf16[384,1536]{1,0:T(8,128)(2,1)S(1)}, bf16[384,1536]{1,0:T(8,128)(2,1)}, u32[]{:S(2)}) copy-start(bf16[384,1536]{1,0:T(8,128)(2,1)} %refs_9_.1) | copy-start | bytes 3538948
  0.9 7.4 %collective-permute-start.2 = (bf16[16,2048]{1,0:T(8,128)(2,1)S(1)}, bf16[16,2048]{1,0:T(8,128)(2,1)S(1)}, u32[]{:S(2)}, u32[]{:S(2)}) collective-permute-start(bf16[16,2048]{1,0:T(8,128)(2,1)S(1)} %pack.1.own), channel_id=1, source_target_pairs={{0,2},{2,0},{4,6},{6,4},{8,10},{10,8},{12,14},{14,12},{1,3},{3,1},... | collective-permute-start | bytes 196616 | tf_op jit(solution)/shard_map/ppermute | solution.py:150
  3.9 8.6 %collective-permute-start = (bf16[16,2048]{1,0:T(8,128)(2,1)S(1)}, bf16[16,2048]{1,0:T(8,128)(2,1)S(1)}, u32[]{:S(2)}, u32[]{:S(2)}) collective-permute-start(bf16[16,2048]{1,0:T(8,128)(2,1)S(1)} %pack.1.own), channel_id=1, source_target_pairs={{0,12},{2,14},{4,8},{6,10},{8,4},{10,6},{12,0},{14,2},{1,13},{3,15... | collective-permute-start | bytes 196616 | tf_op jit(solution)/shard_map/ppermute | solution.py:150
  7.5 6.7 %collective-permute-start.6 = (bf16[16,2048]{1,0:T(8,128)(2,1)S(1)}, bf16[16,2048]{1,0:T(8,128)(2,1)S(1)}, u32[]{:S(2)}, u32[]{:S(2)}) collective-permute-start(bf16[16,2048]{1,0:T(8,128)(2,1)S(1)} %pack.1.own), channel_id=1, source_target_pairs={{0,8},{2,10},{4,12},{6,14},{8,0},{10,2},{12,4},{14,6},{1,9},{3,11}... | collective-permute-start | bytes 196616 | tf_op jit(solution)/shard_map/ppermute | solution.py:150
  7.5 6.7 %collective-permute-start.5 = (bf16[16,2048]{1,0:T(8,128)(2,1)S(1)}, bf16[16,2048]{1,0:T(8,128)(2,1)S(1)}, u32[]{:S(2)}, u32[]{:S(2)}) collective-permute-start(bf16[16,2048]{1,0:T(8,128)(2,1)S(1)} %pack.1.own), channel_id=1, source_target_pairs={{0,4},{2,6},{4,0},{6,2},{8,12},{10,14},{12,8},{14,10},{1,5},{3,7},... | collective-permute-start | bytes 196616 | tf_op jit(solution)/shard_map/ppermute | solution.py:150
  8.3 7.5 %collective-permute-start.4 = (bf16[16,2048]{1,0:T(8,128)(2,1)S(1)}, bf16[16,2048]{1,0:T(8,128)(2,1)S(1)}, u32[]{:S(2)}, u32[]{:S(2)}) collective-permute-start(bf16[16,2048]{1,0:T(8,128)(2,1)S(1)} %collective-permute-done.2.refs_6_), channel_id=1, source_target_pairs={{0,8},{2,10},{4,12},{6,14},{8,0},{10,2},{12,4},{14,6},{1,9},{3,11}... | collective-permute-start | bytes 196616 | tf_op jit(solution)/shard_map/ppermute | solution.py:150
  10.4 5.3 %collective-permute-start.3 = (bf16[16,2048]{1,0:T(8,128)(2,1)S(1)}, bf16[16,2048]{1,0:T(8,128)(2,1)S(1)}, u32[]{:S(2)}, u32[]{:S(2)}) collective-permute-start(bf16[16,2048]{1,0:T(8,128)(2,1)S(1)} %collective-permute-done.2.refs_6_), channel_id=1, source_target_pairs={{0,4},{2,6},{4,0},{6,2},{8,12},{10,14},{12,8},{14,10},{1,5},{3,7},... | collective-permute-start | bytes 196616 | tf_op jit(solution)/shard_map/ppermute | solution.py:150
  12.4 4.3 %collective-permute-start.1 = (bf16[16,2048]{1,0:T(8,128)(2,1)S(1)}, bf16[16,2048]{1,0:T(8,128)(2,1)S(1)}, u32[]{:S(2)}, u32[]{:S(2)}) collective-permute-start(bf16[16,2048]{1,0:T(8,128)(2,1)S(1)} %collective-permute-done.refs_5_), channel_id=1, source_target_pairs={{0,2},{2,0},{4,6},{6,4},{8,10},{10,8},{12,14},{14,12},{1,3},{3,1},... | collective-permute-start | bytes 196616 | tf_op jit(solution)/shard_map/ppermute | solution.py:150
  18.1 1.4 %collective-permute-start.7 = (f32[64,384]{1,0:T(8,128)S(1)}, f32[64,384]{1,0:T(8,128)S(1)}, u32[]{:S(2)}, u32[]{:S(2)}) collective-permute-start(f32[64,384]{1,0:T(8,128)S(1)} %get-tuple-element.8), channel_id=1, source_target_pairs={{0,1},{1,0},{2,3},{3,2},{4,5},{5,4},{6,7},{7,6},{8,9},{9,8},{10,11... | collective-permute-start | bytes 294920 | tf_op jit(solution)/shard_map/ppermute | solution.py:163
  19.5 4.1 %collective-permute-start.11 = (bf16[16,384]{1,0:T(8,128)(2,1)S(1)}, bf16[16,384]{1,0:T(8,128)(2,1)S(1)}, u32[]{:S(2)}, u32[]{:S(2)}) collective-permute-start(bf16[16,384]{1,0:T(8,128)(2,1)S(1)} %get-tuple-element.9), channel_id=1, source_target_pairs={{0,10},{1,6},{2,8},{3,4},{4,14},{5,2},{6,12},{7,0},{9,3},{8,15},{1... | collective-permute-start | bytes 36872 | tf_op jit(solution)/shard_map/ppermute | solution.py:166
  20.0 3.6 %collective-permute-start.10 = (bf16[16,384]{1,0:T(8,128)(2,1)S(1)}, bf16[16,384]{1,0:T(8,128)(2,1)S(1)}, u32[]{:S(2)}, u32[]{:S(2)}) collective-permute-start(bf16[16,384]{1,0:T(8,128)(2,1)S(1)} %get-tuple-element.10), channel_id=1, source_target_pairs={{0,12},{1,0},{2,14},{3,2},{4,8},{5,4},{6,10},{7,6},{9,5},{8,9},{11... | collective-permute-start | bytes 36872 | tf_op jit(solution)/shard_map/ppermute | solution.py:166
  21.6 3.1 %collective-permute-start.9 = (bf16[16,384]{1,0:T(8,128)(2,1)S(1)}, bf16[16,384]{1,0:T(8,128)(2,1)S(1)}, u32[]{:S(2)}, u32[]{:S(2)}) collective-permute-start(bf16[16,384]{1,0:T(8,128)(2,1)S(1)} %get-tuple-element.11), channel_id=1, source_target_pairs={{0,14},{1,4},{2,12},{3,6},{4,10},{5,0},{6,8},{7,2},{9,7},{8,13},{1... | collective-permute-start | bytes 36872 | tf_op jit(solution)/shard_map/ppermute | solution.py:166
  22.7 3.1 %collective-permute-start.8 = (bf16[16,384]{1,0:T(8,128)(2,1)S(1)}, bf16[16,384]{1,0:T(8,128)(2,1)S(1)}, u32[]{:S(2)}, u32[]{:S(2)}) collective-permute-start(bf16[16,384]{1,0:T(8,128)(2,1)S(1)} %get-tuple-element.12), channel_id=1, source_target_pairs={{0,8},{1,2},{2,10},{3,0},{4,12},{5,6},{6,14},{7,4},{9,1},{8,11},{1... | collective-permute-start | bytes 36872 | tf_op jit(solution)/shard_map/ppermute | solution.py:166

commit v5 on v4

--- a/solution.py
+++ b/solution.py
@@ -11,6 +11,25 @@
 HEAD_DIM = 128
 MOST_DIRECT = 16
 NT = (((1,), (1,)), ((), ()))
+
+
+def turn_kernel(weight, turned):
+    turned[...] = weight[...].T
+
+
+def turn(weight):
+    vmem = pl.BlockSpec(memory_space=pltpu.VMEM)
+    return pl.pallas_call(
+        turn_kernel,
+        out_shape=jax.ShapeDtypeStruct(weight.shape[::-1], weight.dtype),
+        in_specs=[vmem],
+        out_specs=vmem,
+        cost_estimate=pl.CostEstimate(
+            flops=0, bytes_accessed=4 * weight.size, transcendentals=0
+        ),
+        compiler_params=pltpu.CompilerParams(vmem_limit_bytes=8 * 1024 * 1024),
+        name="turn",
+    )(weight)
 
 
 def mix_kernel(plan, own, *refs):
@@ -37,9 +56,7 @@
         for w, c in zip(weights, heads)
     ]
     mixed = jnp.concatenate([(s / t).astype(jnp.bfloat16) for s, t in zip(sums, totals)], axis=1)
-    partial_sum[...] = lax.dot_general(
-        mixed, out_weight[...], NT, preferred_element_type=jnp.float32
-    )
+    partial_sum[...] = jnp.dot(mixed, out_weight[...], preferred_element_type=jnp.float32)
     taker = lax.axis_index("head") == lax.axis_index("seq") // plan.half
     for step, flips in enumerate(plan.turns):
         first, second = (
@@ -53,7 +70,7 @@
 def mix(plan, own, received, key_basis, value_basis, out_weight):
     rows = own.shape[0] * plan.count
     rank, width = key_basis.shape
-    features = out_weight.shape[0]
+    features = out_weight.shape[1]
     vmem = pl.BlockSpec(memory_space=pltpu.VMEM)
     return pl.pallas_call(
         functools.partial(mix_kernel, plan),
@@ -159,7 +176,7 @@
     own = jnp.concatenate([queries, latent.T], axis=1)
     own = pack(own, sum(2 * w.size for w in weights))
     received = gather(plan, own)
-    keep, send = mix(plan, own, received, *weights)
+    keep, send = mix(plan, own, received, key_basis, value_basis, turn(out_weight))
     other = lax.ppermute(send, "head", [(0, 1), (1, 0)])
     total = (keep + other).astype(jnp.bfloat16)
     parts = [

time: 26.7 us -> 26.5 us (level)
  waiting for transfers between devices: 7.35 us -> 6.98 us
    ppermute x7, waiting for transfers between devices: 3.73 us -> 3.37 us  [gather(): lax.ppermute(sent, 'seq', [(i, i ^ flip) for i in range(plan.count)])]
    pallas_call x0 -> x1, Pallas kernels: none -> 0.35 us  [turn(): pl.pallas_call(turn_kernel, out_shape=jax.ShapeDtypeStruct(weight.shape[:...]
  transfers between devices with their start and end apart: 12 -> 12, of which waited for: 7 -> 7; matrix products, arithmetic and copies ran while one was open for 0% -> 0% of each run, Pallas kernels for 0% -> 1%
where the time goes in v5:
time: 26.5 us; the launch traced here: 26.3 us
  starting transfers between devices  16.2 us (61%)
  waiting for transfers between devices  6.98 us (26%)
  Pallas kernels  2.25 us (8%)
  other arithmetic  0.83 us (3%)
    ppermute x7, starting transfers between devices, gather(): lax.ppermute(sent, 'seq', [(i, i ^ flip) for i in range(plan.count)])  12.1 us
    ppermute x4, starting transfers between devices, direct(): lax.ppermute(total[step * rows:(step + 1) * rows], ('seq', 'head'), plan....  4 us
    ppermute x7, waiting for transfers between devices, gather(): lax.ppermute(sent, 'seq', [(i, i ^ flip) for i in range(plan.count)])  3.37 us
    ppermute x4, waiting for transfers between devices, direct(): lax.ppermute(total[step * rows:(step + 1) * rows], ('seq', 'head'), plan....  2.32 us
    ppermute x1, waiting for transfers between devices, direct(): other = lax.ppermute(send, 'head', [(0, 1), (1, 0)])  1.29 us
    pallas_call x1, Pallas kernels, mix(): pl.pallas_call(functools.partial(mix_kernel, plan), out_shape=[jax.ShapeD...  1.26 us
    concatenate x1, other arithmetic, direct(): own = jnp.concatenate([queries, latent.T], axis=1)  0.82 us
    pallas_call x1, Pallas kernels, place(): pl.pallas_call(functools.partial(place_kernel, plan), out_shape=jax.Shape...  0.63 us
  transfers between devices with their start and end apart: 12, of which 7 were waited for; matrix products, arithmetic and copies ran while one was open for 0% of the time, Pallas kernels for 1%

profile of v5, /device:TPU:0, one launch (start us, length us, event | category | flops | bytes accessed | tf_op | source)
XLA Modules:
  0.0 26.3 jit_solution(4988666792689212495)
XLA Ops:
  0.0 0.8 %pad_maximum_fusion.block = bf16[16,2048]{1,0:T(8,128)(2,1)S(1)} fusion(bf16[16,512]{1,0:T(8,128)(2,1)} %bitcast.1, bf16[16,1536]{1,0:T(8,128)(2,1)} %param.5), kind=kLoop, calls=%fused_computation.1 | loop fusion | flops 131072 | bytes 131072 | tf_op jit(solution)/shard_map/concatenate | solution.py:176
  0.8 0.0 copy-start.2
  0.8 0.0 copy-start.1
  0.8 0.0 copy-start
  0.9 3.0 %collective-permute-start.2 = (bf16[16,2048]{1,0:T(8,128)(2,1)S(1)}, bf16[16,2048]{1,0:T(8,128)(2,1)S(1)}, u32[]{:S(2)}, u32[]{:S(2)}) collective-permute-start(bf16[16,2048]{1,0:T(8,128)(2,1)S(1)} %pack.1.own), channel_id=1, source_target_pairs={{0,2},{2,0},{4,6},{6,4},{8,10},{10,8},{12,14},{14,12},{1,3},{3,1},... | collective-permute-start | bytes 196616 | tf_op jit(solution)/shard_map/ppermute | solution.py:167
  3.9 3.6 %collective-permute-start = (bf16[16,2048]{1,0:T(8,128)(2,1)S(1)}, bf16[16,2048]{1,0:T(8,128)(2,1)S(1)}, u32[]{:S(2)}, u32[]{:S(2)}) collective-permute-start(bf16[16,2048]{1,0:T(8,128)(2,1)S(1)} %pack.1.own), channel_id=1, source_target_pairs={{0,12},{2,14},{4,8},{6,10},{8,4},{10,6},{12,0},{14,2},{1,13},{3,15... | collective-permute-start | bytes 196616 | tf_op jit(solution)/shard_map/ppermute | solution.py:167
  7.5 0.0 collective-permute-start.6
  7.5 0.8 %collective-permute-start.5 = (bf16[16,2048]{1,0:T(8,128)(2,1)S(1)}, bf16[16,2048]{1,0:T(8,128)(2,1)S(1)}, u32[]{:S(2)}, u32[]{:S(2)}) collective-permute-start(bf16[16,2048]{1,0:T(8,128)(2,1)S(1)} %pack.1.own), channel_id=1, source_target_pairs={{0,4},{2,6},{4,0},{6,2},{8,12},{10,14},{12,8},{14,10},{1,5},{3,7},... | collective-permute-start | bytes 196616 | tf_op jit(solution)/shard_map/ppermute | solution.py:167
  8.2 0.0 collective-permute-done.2.refs_6_
  8.3 2.1 %collective-permute-start.4 = (bf16[16,2048]{1,0:T(8,128)(2,1)S(1)}, bf16[16,2048]{1,0:T(8,128)(2,1)S(1)}, u32[]{:S(2)}, u32[]{:S(2)}) collective-permute-start(bf16[16,2048]{1,0:T(8,128)(2,1)S(1)} %collective-permute-done.2.refs_6_), channel_id=1, source_target_pairs={{0,8},{2,10},{4,12},{6,14},{8,0},{10,2},{12,4},{14,6},{1,9},{3,11}... | collective-permute-start | bytes 196616 | tf_op jit(solution)/shard_map/ppermute | solution.py:167
  10.4 2.0 %collective-permute-start.3 = (bf16[16,2048]{1,0:T(8,128)(2,1)S(1)}, bf16[16,2048]{1,0:T(8,128)(2,1)S(1)}, u32[]{:S(2)}, u32[]{:S(2)}) collective-permute-start(bf16[16,2048]{1,0:T(8,128)(2,1)S(1)} %collective-permute-done.2.refs_6_), channel_id=1, source_target_pairs={{0,4},{2,6},{4,0},{6,2},{8,12},{10,14},{12,8},{14,10},{1,5},{3,7},... | collective-permute-start | bytes 196616 | tf_op jit(solution)/shard_map/ppermute | solution.py:167
  12.4 0.0 collective-permute-done.refs_5_
  12.4 0.5 %collective-permute-start.1 = (bf16[16,2048]{1,0:T(8,128)(2,1)S(1)}, bf16[16,2048]{1,0:T(8,128)(2,1)S(1)}, u32[]{:S(2)}, u32[]{:S(2)}) collective-permute-start(bf16[16,2048]{1,0:T(8,128)(2,1)S(1)} %collective-permute-done.refs_5_), channel_id=1, source_target_pairs={{0,2},{2,0},{4,6},{6,4},{8,10},{10,8},{12,14},{14,12},{1,3},{3,1},... | collective-permute-start | bytes 196616 | tf_op jit(solution)/shard_map/ppermute | solution.py:167
  13.0 0.0 copy-done.2
  13.0 0.4 %turn.1.refs_9_ = bf16[1536,384]{1,0:T(8,128)(2,1)S(1)} custom-call(bf16[384,1536]{1,0:T(8,128)(2,1)S(1)} %copy-done.2), custom_call_target="tpu_custom_call" | custom-call | bytes 2359296 | tf_op jit(solution)/shard_map/turn/pallas_call | solution.py:22
  13.3 0.9 %collective-permute-done.6.refs_4_ = bf16[16,2048]{1,0:T(8,128)(2,1)S(1)} collective-permute-done((bf16[16,2048]{1,0:T(8,128)(2,1)S(1)}, bf16[16,2048]{1,0:T(8,128)(2,1)S(1)}, u32[]{:S(2)}, u32[]{:S(2)}) %collective-permute-start.6) | collective-permute-done | bytes 65568 | tf_op jit(solution)/shard_map/ppermute | solution.py:167
  14.2 0.0 collective-permute-done.5.refs_3_
  14.2 1.5 %collective-permute-done.4.refs_2_ = bf16[16,2048]{1,0:T(8,128)(2,1)S(1)} collective-permute-done((bf16[16,2048]{1,0:T(8,128)(2,1)S(1)}, bf16[16,2048]{1,0:T(8,128)(2,1)S(1)}, u32[]{:S(2)}, u32[]{:S(2)}) %collective-permute-start.4) | collective-permute-done | bytes 65568 | tf_op jit(solution)/shard_map/ppermute | solution.py:167
  15.7 0.0 collective-permute-done.3.refs_1_
  15.7 1.0 %collective-permute-done.1.refs_0_ = bf16[16,2048]{1,0:T(8,128)(2,1)S(1)} collective-permute-done((bf16[16,2048]{1,0:T(8,128)(2,1)S(1)}, bf16[16,2048]{1,0:T(8,128)(2,1)S(1)}, u32[]{:S(2)}, u32[]{:S(2)}) %collective-permute-start.1) | collective-permute-done | bytes 65568 | tf_op jit(solution)/shard_map/ppermute | solution.py:167
  16.7 0.0 copy-done.1
  16.7 0.0 copy-done
  16.7 1.3 %mix.1 = (f32[64,384]{1,0:T(8,128)S(1)}, f32[64,384]{1,0:T(8,128)S(1)}) custom-call(bf16[16,2048]{1,0:T(8,128)(2,1)S(1)} %pack.1.own, bf16[16,2048]{1,0:T(8,128)(2,1)S(1)} %collective-permute-done.1.refs_0_, bf16[16,2048]{1,0:T(8,128)(2,1)S(1)} %collective-permute-done.3.refs_1_, bf16[16,2048]{1,0:T(8,128)(2,1)S(1)} %collective-permute-done.4.refs_2_, ...), custom_call_target="tpu_custom_call" | custom-call | flops 654311424 | bytes 4325376 | tf_op jit(solution)/shard_map/mix/pallas_call | solution.py:75
  18.0 0.1 collective-permute-start.7
  18.0 1.3 %collective-permute-done.7 = f32[64,384]{1,0:T(8,128)S(1)} collective-permute-done((f32[64,384]{1,0:T(8,128)S(1)}, f32[64,384]{1,0:T(8,128)S(1)}, u32[]{:S(2)}, u32[]{:S(2)}) %collective-permute-start.7) | collective-permute-done | bytes 98336 | tf_op jit(solution)/shard_map/ppermute | solution.py:180
  19.4 0.5 %collective-permute-start.11 = (bf16[16,384]{1,0:T(8,128)(2,1)S(1)}, bf16[16,384]{1,0:T(8,128)(2,1)S(1)}, u32[]{:S(2)}, u32[]{:S(2)}) collective-permute-start(bf16[16,384]{1,0:T(8,128)(2,1)S(1)} %get-tuple-element.9), channel_id=1, source_target_pairs={{0,10},{1,6},{2,8},{3,4},{4,14},{5,2},{6,12},{7,0},{9,3},{8,15},{1... | collective-permute-start | bytes 36872 | tf_op jit(solution)/shard_map/ppermute | solution.py:183
  19.8 1.6 %collective-permute-start.10 = (bf16[16,384]{1,0:T(8,128)(2,1)S(1)}, bf16[16,384]{1,0:T(8,128)(2,1)S(1)}, u32[]{:S(2)}, u32[]{:S(2)}) collective-permute-start(bf16[16,384]{1,0:T(8,128)(2,1)S(1)} %get-tuple-element.10), channel_id=1, source_target_pairs={{0,12},{1,0},{2,14},{3,2},{4,8},{5,4},{6,10},{7,6},{9,5},{8,9},{11... | collective-permute-start | bytes 36872 | tf_op jit(solution)/shard_map/ppermute | solution.py:183
  21.4 1.1 %collective-permute-start.9 = (bf16[16,384]{1,0:T(8,128)(2,1)S(1)}, bf16[16,384]{1,0:T(8,128)(2,1)S(1)}, u32[]{:S(2)}, u32[]{:S(2)}) collective-permute-start(bf16[16,384]{1,0:T(8,128)(2,1)S(1)} %get-tuple-element.11), channel_id=1, source_target_pairs={{0,14},{1,4},{2,12},{3,6},{4,10},{5,0},{6,8},{7,2},{9,7},{8,13},{1... | collective-permute-start | bytes 36872 | tf_op jit(solution)/shard_map/ppermute | solution.py:183
  22.6 0.8 %collective-permute-start.8 = (bf16[16,384]{1,0:T(8,128)(2,1)S(1)}, bf16[16,384]{1,0:T(8,128)(2,1)S(1)}, u32[]{:S(2)}, u32[]{:S(2)}) collective-permute-start(bf16[16,384]{1,0:T(8,128)(2,1)S(1)} %get-tuple-element.12), channel_id=1, source_target_pairs={{0,8},{1,2},{2,10},{3,0},{4,12},{5,6},{6,14},{7,4},{9,1},{8,11},{1... | collective-permute-start | bytes 36872 | tf_op jit(solution)/shard_map/ppermute | solution.py:183
  23.4 0.1 collective-permute-done.11.refs_3_
  23.4 0.0 collective-permute-done.10.refs_2_
  23.4 1.1 %collective-permute-done.9.refs_1_ = bf16[16,384]{1,0:T(8,128)(2,1)S(1)} collective-permute-done((bf16[16,384]{1,0:T(8,128)(2,1)S(1)}, bf16[16,384]{1,0:T(8,128)(2,1)S(1)}, u32[]{:S(2)}, u32[]{:S(2)}) %collective-permute-start.9) | collective-permute-done | bytes 12320 | tf_op jit(solution)/shard_map/ppermute | solution.py:183
  24.6 1.1 %collective-permute-done.8.refs_0_ = bf16[16,384]{1,0:T(8,128)(2,1)S(1)} collective-permute-done((bf16[16,384]{1,0:T(8,128)(2,1)S(1)}, bf16[16,384]{1,0:T(8,128)(2,1)S(1)}, u32[]{:S(2)}, u32[]{:S(2)}) %collective-permute-start.8) | collective-permute-done | bytes 12320 | tf_op jit(solution)/shard_map/ppermute | solution.py:183
  25.7 0.6 %place.1 = bf16[16,1536]{1,0:T(8,128)(2,1)} custom-call(bf16[16,384]{1,0:T(8,128)(2,1)S(1)} %collective-permute-done.8.refs_0_, bf16[16,384]{1,0:T(8,128)(2,1)S(1)} %collective-permute-done.9.refs_1_, bf16[16,384]{1,0:T(8,128)(2,1)S(1)} %collective-permute-done.10.refs_2_, bf16[16,384]{1,0:T(8,128)(2,1)S(1)} %collective-permute-done.11.refs_3_), custom_call_target="tpu_custom_call" | custom-call | tf_op jit(solution)/shard_map/place/pallas_call | solution.py:106
  (3 shorter events, 0.0 us)
Async XLA Ops:
  0.8 12.1 %copy-start.2 = (bf16[384,1536]{1,0:T(8,128)(2,1)S(1)}, bf16[384,1536]{1,0:T(8,128)(2,1)}, u32[]{:S(2)}) copy-start(bf16[384,1536]{1,0:T(8,128)(2,1)} %weight.1) | copy-start | bytes 3538948
  0.8 15.9 %copy-start.1 = (bf16[512,1536]{1,0:T(8,128)(2,1)S(1)}, bf16[512,1536]{1,0:T(8,128)(2,1)}, u32[]{:S(2)}) copy-start(bf16[512,1536]{1,0:T(8,128)(2,1)} %refs_8_.1) | copy-start | bytes 4718596
  0.8 15.8 %copy-start = (bf16[512,1536]{1,0:T(8,128)(2,1)S(1)}, bf16[512,1536]{1,0:T(8,128)(2,1)}, u32[]{:S(2)}) copy-start(bf16[512,1536]{1,0:T(8,128)(2,1)} %refs_7_.1) | copy-start | bytes 4718596
  0.9 7.4 %collective-permute-start.2 = (bf16[16,2048]{1,0:T(8,128)(2,1)S(1)}, bf16[16,2048]{1,0:T(8,128)(2,1)S(1)}, u32[]{:S(2)}, u32[]{:S(2)}) collective-permute-start(bf16[16,2048]{1,0:T(8,128)(2,1)S(1)} %pack.1.own), channel_id=1, source_target_pairs={{0,2},{2,0},{4,6},{6,4},{8,10},{10,8},{12,14},{14,12},{1,3},{3,1},... | collective-permute-start | bytes 196616 | tf_op jit(solution)/shard_map/ppermute | solution.py:167
  3.9 8.6 %collective-permute-start = (bf16[16,2048]{1,0:T(8,128)(2,1)S(1)}, bf16[16,2048]{1,0:T(8,128)(2,1)S(1)}, u32[]{:S(2)}, u32[]{:S(2)}) collective-permute-start(bf16[16,2048]{1,0:T(8,128)(2,1)S(1)} %pack.1.own), channel_id=1, source_target_pairs={{0,12},{2,14},{4,8},{6,10},{8,4},{10,6},{12,0},{14,2},{1,13},{3,15... | collective-permute-start | bytes 196616 | tf_op jit(solution)/shard_map/ppermute | solution.py:167
  7.5 6.7 %collective-permute-start.6 = (bf16[16,2048]{1,0:T(8,128)(2,1)S(1)}, bf16[16,2048]{1,0:T(8,128)(2,1)S(1)}, u32[]{:S(2)}, u32[]{:S(2)}) collective-permute-start(bf16[16,2048]{1,0:T(8,128)(2,1)S(1)} %pack.1.own), channel_id=1, source_target_pairs={{0,8},{2,10},{4,12},{6,14},{8,0},{10,2},{12,4},{14,6},{1,9},{3,11}... | collective-permute-start | bytes 196616 | tf_op jit(solution)/shard_map/ppermute | solution.py:167
  7.5 6.7 %collective-permute-start.5 = (bf16[16,2048]{1,0:T(8,128)(2,1)S(1)}, bf16[16,2048]{1,0:T(8,128)(2,1)S(1)}, u32[]{:S(2)}, u32[]{:S(2)}) collective-permute-start(bf16[16,2048]{1,0:T(8,128)(2,1)S(1)} %pack.1.own), channel_id=1, source_target_pairs={{0,4},{2,6},{4,0},{6,2},{8,12},{10,14},{12,8},{14,10},{1,5},{3,7},... | collective-permute-start | bytes 196616 | tf_op jit(solution)/shard_map/ppermute | solution.py:167
  8.3 7.5 %collective-permute-start.4 = (bf16[16,2048]{1,0:T(8,128)(2,1)S(1)}, bf16[16,2048]{1,0:T(8,128)(2,1)S(1)}, u32[]{:S(2)}, u32[]{:S(2)}) collective-permute-start(bf16[16,2048]{1,0:T(8,128)(2,1)S(1)} %collective-permute-done.2.refs_6_), channel_id=1, source_target_pairs={{0,8},{2,10},{4,12},{6,14},{8,0},{10,2},{12,4},{14,6},{1,9},{3,11}... | collective-permute-start | bytes 196616 | tf_op jit(solution)/shard_map/ppermute | solution.py:167
  10.4 5.3 %collective-permute-start.3 = (bf16[16,2048]{1,0:T(8,128)(2,1)S(1)}, bf16[16,2048]{1,0:T(8,128)(2,1)S(1)}, u32[]{:S(2)}, u32[]{:S(2)}) collective-permute-start(bf16[16,2048]{1,0:T(8,128)(2,1)S(1)} %collective-permute-done.2.refs_6_), channel_id=1, source_target_pairs={{0,4},{2,6},{4,0},{6,2},{8,12},{10,14},{12,8},{14,10},{1,5},{3,7},... | collective-permute-start | bytes 196616 | tf_op jit(solution)/shard_map/ppermute | solution.py:167
  12.4 4.3 %collective-permute-start.1 = (bf16[16,2048]{1,0:T(8,128)(2,1)S(1)}, bf16[16,2048]{1,0:T(8,128)(2,1)S(1)}, u32[]{:S(2)}, u32[]{:S(2)}) collective-permute-start(bf16[16,2048]{1,0:T(8,128)(2,1)S(1)} %collective-permute-done.refs_5_), channel_id=1, source_target_pairs={{0,2},{2,0},{4,6},{6,4},{8,10},{10,8},{12,14},{14,12},{1,3},{3,1},... | collective-permute-start | bytes 196616 | tf_op jit(solution)/shard_map/ppermute | solution.py:167
  18.0 1.4 %collective-permute-start.7 = (f32[64,384]{1,0:T(8,128)S(1)}, f32[64,384]{1,0:T(8,128)S(1)}, u32[]{:S(2)}, u32[]{:S(2)}) collective-permute-start(f32[64,384]{1,0:T(8,128)S(1)} %get-tuple-element.8), channel_id=1, source_target_pairs={{0,1},{1,0},{2,3},{3,2},{4,5},{5,4},{6,7},{7,6},{8,9},{9,8},{10,11... | collective-permute-start | bytes 294920 | tf_op jit(solution)/shard_map/ppermute | solution.py:180
  19.4 4.1 %collective-permute-start.11 = (bf16[16,384]{1,0:T(8,128)(2,1)S(1)}, bf16[16,384]{1,0:T(8,128)(2,1)S(1)}, u32[]{:S(2)}, u32[]{:S(2)}) collective-permute-start(bf16[16,384]{1,0:T(8,128)(2,1)S(1)} %get-tuple-element.9), channel_id=1, source_target_pairs={{0,10},{1,6},{2,8},{3,4},{4,14},{5,2},{6,12},{7,0},{9,3},{8,15},{1... | collective-permute-start | bytes 36872 | tf_op jit(solution)/shard_map/ppermute | solution.py:183
  19.8 3.6 %collective-permute-start.10 = (bf16[16,384]{1,0:T(8,128)(2,1)S(1)}, bf16[16,384]{1,0:T(8,128)(2,1)S(1)}, u32[]{:S(2)}, u32[]{:S(2)}) collective-permute-start(bf16[16,384]{1,0:T(8,128)(2,1)S(1)} %get-tuple-element.10), channel_id=1, source_target_pairs={{0,12},{1,0},{2,14},{3,2},{4,8},{5,4},{6,10},{7,6},{9,5},{8,9},{11... | collective-permute-start | bytes 36872 | tf_op jit(solution)/shard_map/ppermute | solution.py:183
  21.4 3.1 %collective-permute-start.9 = (bf16[16,384]{1,0:T(8,128)(2,1)S(1)}, bf16[16,384]{1,0:T(8,128)(2,1)S(1)}, u32[]{:S(2)}, u32[]{:S(2)}) collective-permute-start(bf16[16,384]{1,0:T(8,128)(2,1)S(1)} %get-tuple-element.11), channel_id=1, source_target_pairs={{0,14},{1,4},{2,12},{3,6},{4,10},{5,0},{6,8},{7,2},{9,7},{8,13},{1... | collective-permute-start | bytes 36872 | tf_op jit(solution)/shard_map/ppermute | solution.py:183
  22.6 3.1 %collective-permute-start.8 = (bf16[16,384]{1,0:T(8,128)(2,1)S(1)}, bf16[16,384]{1,0:T(8,128)(2,1)S(1)}, u32[]{:S(2)}, u32[]{:S(2)}) collective-permute-start(bf16[16,384]{1,0:T(8,128)(2,1)S(1)} %get-tuple-element.12), channel_id=1, source_target_pairs={{0,8},{1,2},{2,10},{3,0},{4,12},{5,6},{6,14},{7,4},{9,1},{8,11},{1... | collective-permute-start | bytes 36872 | tf_op jit(solution)/shard_map/ppermute | solution.py:183

commit v6 on v5

--- a/solution.py
+++ b/solution.py
@@ -9,7 +9,7 @@
 from jax.sharding import PartitionSpec as P
 
 HEAD_DIM = 128
-MOST_DIRECT = 16
+MOST_DIRECT = 8
 NT = (((1,), (1,)), ((), ()))
 
 
@@ -57,14 +57,16 @@
     ]
     mixed = jnp.concatenate([(s / t).astype(jnp.bfloat16) for s, t in zip(sums, totals)], axis=1)
     partial_sum[...] = jnp.dot(mixed, out_weight[...], preferred_element_type=jnp.float32)
-    taker = lax.axis_index("head") == lax.axis_index("seq") // plan.half
-    for step, flips in enumerate(plan.turns):
-        first, second = (
-            partial_sum[at * rows : (at + 1) * rows, :] for at in map(plan.held.index, flips)
-        )
+    core = lax.axis_index("head")
+    for step in range(plan.half):
         part = slice(step * rows, (step + 1) * rows)
-        keep[part, :] = jnp.where(taker, first, second)
-        send[part, :] = jnp.where(taker, second, first)
+        for target, other in ((keep, 0), (send, 1)):
+            at = jnp.where(
+                core == 0,
+                look_up(plan.kept(0, step, other)),
+                look_up(plan.kept(1, step, 1 - other)),
+            )
+            target[part, :] = partial_sum[pl.ds(pl.multiple_of(at * rows, rows), rows), :]
 
 
 def mix(plan, own, received, key_basis, value_basis, out_weight):
@@ -91,12 +93,11 @@
 def place_kernel(plan, *refs):
     parts, out = refs[:-1], refs[-1]
     features = parts[0].shape[1]
-    seq = lax.axis_index("seq")
-    near = seq // plan.half == lax.axis_index("head")
-    for step, part in zip(plan.landed, parts):
-        low, high = sorted(plan.turns[step])
-        flip = jnp.where(near, low, high - plan.half)
-        column = jnp.bitwise_xor(lax.rem(seq, plan.half), flip) * features
+    core = lax.axis_index("head")
+    for step, part in zip(reversed(range(plan.half)), parts):
+        column = features * jnp.where(
+            core == 0, look_up(plan.source(step, 0)), look_up(plan.source(step, 1))
+        )
         out[:, pl.ds(pl.multiple_of(column, features), features)] = part[...]
 
 
@@ -136,38 +137,79 @@
     def __init__(self, count):
         self.count, self.half = count, count // 2
         if count == 8:
-            self.routes = ((1, (0,)), (6, (0,)), (4, (0,)), (2, (0,)), (4, (1,)), (2, (1,)), (1, (6,)))
-            self.turns = ((5, 3), (6, 0), (7, 2), (4, 1))
+            self.routes = (
+                (0, 1, 1),
+                (0, 6, 6),
+                (0, 4, 4),
+                (0, 2, 2),
+                (1, 4, 4),
+                (1, 2, 2),
+                (2, 1, 1),
+            )
+            self.ways = (
+                ((3, 7, 6, 1), (5, 4, 2, 0)),
+                ((0, 6, 5, 3), (1, 2, 4, 7)),
+                ((4, 3, 7, 5), (6, 1, 0, 2)),
+                ((2, 5, 1, 4), (7, 0, 3, 6)),
+                ((5, 4, 3, 7), (1, 2, 6, 0)),
+                ((7, 6, 4, 5), (2, 3, 0, 1)),
+                ((6, 1, 5, 3), (4, 0, 7, 2)),
+                ((3, 7, 1, 6), (0, 5, 2, 4)),
+            )
         else:
-            inner = tuple(reversed(range(1, self.half)))
+            inner = range(1, self.half)
             self.routes = (
-                (self.half, (0,)),
-                *((flip, (0,)) for flip in inner),
-                *((flip, (self.half,)) for flip in inner),
-            )
-            self.turns = tuple((i + self.half, i) for i in reversed(range(self.half)))
-        self.held = (0, *(flip ^ block for flip, blocks in self.routes for block in blocks))
-        self.landed = tuple(reversed(range(self.half)))
+                (0, self.half, self.half),
+                *((0, flip, flip) for flip in inner),
+                *((1, flip, flip) for flip in inner),
+            )
+            steps = range(self.half)
+            self.ways = tuple(
+                tuple(
+                    tuple(s ^ (step + self.half * (core == s // self.half)) for step in steps)
+                    for core in (0, 1)
+                )
+                for s in range(count)
+            )
+
+    def out(self, flips):
+        return [(2 * s + h, 2 * (s ^ flips[h]) + h) for s in range(self.count) for h in (0, 1)]
+
+    def held(self, core):
+        flips = [0]
+        for block, *steps in self.routes:
+            flips.append(flips[block] ^ steps[core])
+        return flips
 
     def back(self, step):
-        pairs = []
-        for s in range(self.count):
-            taker = s // self.half
-            for core, flip in zip((taker, 1 - taker), self.turns[step]):
-                pairs.append((2 * s + core, 2 * (s ^ flip) + taker))
-        return pairs
+        return [
+            (2 * s + h, 2 * self.ways[s][h][step] + s // self.half)
+            for s in range(self.count)
+            for h in (0, 1)
+        ]
+
+    def kept(self, core, step, sender):
+        held = self.held(core)
+        return [held.index(s ^ self.ways[s][sender][step]) for s in range(self.count)]
+
+    def source(self, step, taker):
+        source = [0] * self.count
+        for sender, target in self.back(step):
+            if target % 2 == taker:
+                source[target // 2] = sender // 2 % self.half
+        return source
+
+
+def look_up(values):
+    packed = sum(value << (3 * at) for at, value in enumerate(values))
+    return jnp.bitwise_and(lax.shift_right_logical(packed, 3 * lax.axis_index("seq")), 7)
 
 
 def gather(plan, own):
-    rows = own.shape[0]
-    blocks, received = {0: own}, []
-    for flip, names in plan.routes:
-        sent = [blocks[name] for name in names]
-        sent = sent[0] if len(sent) == 1 else jnp.concatenate(sent, axis=0)
-        received.append(lax.ppermute(sent, "seq", [(i, i ^ flip) for i in range(plan.count)]))
-        for at, name in enumerate(names):
-            blocks[flip ^ name] = received[-1][at * rows : (at + 1) * rows]
-    return received
+    blocks = [own]
+    for block, *flips in plan.routes:
+        blocks.append(lax.ppermute(blocks[block], ("seq", "head"), plan.out(flips)))
+    return blocks[1:]
 
 
 def direct(plan, queries, latent, key_basis, value_basis, out_weight):
@@ -181,7 +223,7 @@
     total = (keep + other).astype(jnp.bfloat16)
     parts = [
         lax.ppermute(total[step * rows : (step + 1) * rows], ("seq", "head"), plan.back(step))
-        for step in plan.landed
+        for step in reversed(range(plan.half))
     ]
     return place(plan, parts)
 

time: 26.5 us -> 25.6 us (0.966)
  the two profiles are of different devices: /device:TPU:0 before, /device:TPU:1 now
where the time goes in v6:
time: 25.6 us; the launch traced here: 25.2 us
  starting transfers between devices  16.4 us (64%)
  waiting for transfers between devices  5.67 us (22%)
  Pallas kernels  2.27 us (9%)
  other arithmetic  0.83 us (3%)
    ppermute x7, starting transfers between devices, gather(): blocks.append(lax.ppermute(blocks[block], ('seq', 'head'), plan.out(flips)))  9.51 us
    ppermute x4, starting transfers between devices, direct(): lax.ppermute(total[step * rows:(step + 1) * rows], ('seq', 'head'), plan....  4.32 us
    ppermute x7, waiting for transfers between devices, gather(): blocks.append(lax.ppermute(blocks[block], ('seq', 'head'), plan.out(flips)))  3.51 us
    ppermute x1, starting transfers between devices, direct(): other = lax.ppermute(send, 'head', [(0, 1), (1, 0)])  2.56 us
    pallas_call x1, Pallas kernels, mix(): pl.pallas_call(functools.partial(mix_kernel, plan), out_shape=[jax.ShapeD...  1.28 us
    ppermute x4, waiting for transfers between devices, direct(): lax.ppermute(total[step * rows:(step + 1) * rows], ('seq', 'head'), plan....  1.21 us
    ppermute x1, waiting for transfers between devices, direct(): other = lax.ppermute(send, 'head', [(0, 1), (1, 0)])  0.94 us
    concatenate x1, other arithmetic, direct(): own = jnp.concatenate([queries, latent.T], axis=1)  0.82 us
  transfers between devices with their start and end apart: 12, of which 6 were waited for; matrix products, arithmetic and copies ran while one was open for 0% of the time, Pallas kernels for 1%

profile of v6, /device:TPU:1, one launch (start us, length us, event | category | flops | bytes accessed | tf_op | source)
XLA Modules:
  0.0 25.2 jit_solution(12507014271576980592)
XLA Ops:
  0.0 0.8 %pad_maximum_fusion.block = bf16[16,2048]{1,0:T(8,128)(2,1)S(1)} fusion(bf16[16,512]{1,0:T(8,128)(2,1)} %bitcast.1, bf16[16,1536]{1,0:T(8,128)(2,1)} %param.5), kind=kLoop, calls=%fused_computation.1 | loop fusion | flops 131072 | bytes 131072 | tf_op jit(solution)/shard_map/concatenate | solution.py:218
  0.8 0.0 copy-start.2
  0.8 0.0 copy-start.1
  0.8 0.0 copy-start
  0.9 2.1 %collective-permute-start.2 = (bf16[16,2048]{1,0:T(8,128)(2,1)S(1)}, bf16[16,2048]{1,0:T(8,128)(2,1)S(1)}, u32[]{:S(2)}, u32[]{:S(2)}) collective-permute-start(bf16[16,2048]{1,0:T(8,128)(2,1)S(1)} %pack.1.own), channel_id=1, source_target_pairs={{0,2},{1,3},{2,0},{3,1},{4,6},{5,7},{6,4},{7,5},{8,10},{9,11},{10,... | collective-permute-start | bytes 196616 | tf_op jit(solution)/shard_map/ppermute | solution.py:211
  3.0 3.3 %collective-permute-start = (bf16[16,2048]{1,0:T(8,128)(2,1)S(1)}, bf16[16,2048]{1,0:T(8,128)(2,1)S(1)}, u32[]{:S(2)}, u32[]{:S(2)}) collective-permute-start(bf16[16,2048]{1,0:T(8,128)(2,1)S(1)} %pack.1.own), channel_id=1, source_target_pairs={{0,12},{1,13},{2,14},{3,15},{4,8},{5,9},{6,10},{7,11},{8,4},{9,5},... | collective-permute-start | bytes 196616 | tf_op jit(solution)/shard_map/ppermute | solution.py:211
  6.3 0.0 collective-permute-start.6
  6.3 0.3 %collective-permute-start.5 = (bf16[16,2048]{1,0:T(8,128)(2,1)S(1)}, bf16[16,2048]{1,0:T(8,128)(2,1)S(1)}, u32[]{:S(2)}, u32[]{:S(2)}) collective-permute-start(bf16[16,2048]{1,0:T(8,128)(2,1)S(1)} %pack.1.own), channel_id=1, source_target_pairs={{0,4},{1,5},{2,6},{3,7},{4,0},{5,1},{6,2},{7,3},{8,12},{9,13},{10,... | collective-permute-start | bytes 196616 | tf_op jit(solution)/shard_map/ppermute | solution.py:211
  6.6 0.0 collective-permute-done.2.refs_6_
  6.6 2.1 %collective-permute-start.4 = (bf16[16,2048]{1,0:T(8,128)(2,1)S(1)}, bf16[16,2048]{1,0:T(8,128)(2,1)S(1)}, u32[]{:S(2)}, u32[]{:S(2)}) collective-permute-start(bf16[16,2048]{1,0:T(8,128)(2,1)S(1)} %collective-permute-done.2.refs_6_), channel_id=1, source_target_pairs={{0,8},{1,9},{2,10},{3,11},{4,12},{5,13},{6,14},{7,15},{8,0},{9,1},... | collective-permute-start | bytes 196616 | tf_op jit(solution)/shard_map/ppermute | solution.py:211
  8.7 1.5 %collective-permute-start.3 = (bf16[16,2048]{1,0:T(8,128)(2,1)S(1)}, bf16[16,2048]{1,0:T(8,128)(2,1)S(1)}, u32[]{:S(2)}, u32[]{:S(2)}) collective-permute-start(bf16[16,2048]{1,0:T(8,128)(2,1)S(1)} %collective-permute-done.2.refs_6_), channel_id=1, source_target_pairs={{0,4},{1,5},{2,6},{3,7},{4,0},{5,1},{6,2},{7,3},{8,12},{9,13},{10,... | collective-permute-start | bytes 196616 | tf_op jit(solution)/shard_map/ppermute | solution.py:211
  10.1 0.0 collective-permute-done.refs_5_
  10.1 0.3 %collective-permute-start.1 = (bf16[16,2048]{1,0:T(8,128)(2,1)S(1)}, bf16[16,2048]{1,0:T(8,128)(2,1)S(1)}, u32[]{:S(2)}, u32[]{:S(2)}) collective-permute-start(bf16[16,2048]{1,0:T(8,128)(2,1)S(1)} %collective-permute-done.refs_5_), channel_id=1, source_target_pairs={{0,2},{1,3},{2,0},{3,1},{4,6},{5,7},{6,4},{7,5},{8,10},{9,11},{10,... | collective-permute-start | bytes 196616 | tf_op jit(solution)/shard_map/ppermute | solution.py:211
  10.4 0.0 copy-done.2
  10.4 0.4 %turn.1.refs_9_ = bf16[1536,384]{1,0:T(8,128)(2,1)S(1)} custom-call(bf16[384,1536]{1,0:T(8,128)(2,1)S(1)} %copy-done.2), custom_call_target="tpu_custom_call" | custom-call | bytes 2359296 | tf_op jit(solution)/shard_map/turn/pallas_call | solution.py:22
  10.7 1.1 %collective-permute-done.6.refs_4_ = bf16[16,2048]{1,0:T(8,128)(2,1)S(1)} collective-permute-done((bf16[16,2048]{1,0:T(8,128)(2,1)S(1)}, bf16[16,2048]{1,0:T(8,128)(2,1)S(1)}, u32[]{:S(2)}, u32[]{:S(2)}) %collective-permute-start.6) | collective-permute-done | bytes 65568 | tf_op jit(solution)/shard_map/ppermute | solution.py:211
  11.8 0.0 collective-permute-done.5.refs_3_
  11.8 2.1 %collective-permute-done.4.refs_2_ = bf16[16,2048]{1,0:T(8,128)(2,1)S(1)} collective-permute-done((bf16[16,2048]{1,0:T(8,128)(2,1)S(1)}, bf16[16,2048]{1,0:T(8,128)(2,1)S(1)}, u32[]{:S(2)}, u32[]{:S(2)}) %collective-permute-start.4) | collective-permute-done | bytes 65568 | tf_op jit(solution)/shard_map/ppermute | solution.py:211
  14.0 0.3 %collective-permute-done.3.refs_1_ = bf16[16,2048]{1,0:T(8,128)(2,1)S(1)} collective-permute-done((bf16[16,2048]{1,0:T(8,128)(2,1)S(1)}, bf16[16,2048]{1,0:T(8,128)(2,1)S(1)}, u32[]{:S(2)}, u32[]{:S(2)}) %collective-permute-start.3) | collective-permute-done | bytes 65568 | tf_op jit(solution)/shard_map/ppermute | solution.py:211
  14.2 0.0 collective-permute-done.1.refs_0_
  14.2 0.0 copy-done.1
  14.3 0.0 copy-done
  14.3 1.3 %mix.1 = (f32[64,384]{1,0:T(8,128)S(1)}, f32[64,384]{1,0:T(8,128)S(1)}) custom-call(bf16[16,2048]{1,0:T(8,128)(2,1)S(1)} %pack.1.own, bf16[16,2048]{1,0:T(8,128)(2,1)S(1)} %collective-permute-done.1.refs_0_, bf16[16,2048]{1,0:T(8,128)(2,1)S(1)} %collective-permute-done.3.refs_1_, bf16[16,2048]{1,0:T(8,128)(2,1)S(1)} %collective-permute-done.4.refs_2_, ...), custom_call_target="tpu_custom_call" | custom-call | flops 654311424 | bytes 4325376 | tf_op jit(solution)/shard_map/mix/pallas_call | solution.py:77
  15.5 2.6 %collective-permute-start.7 = (f32[64,384]{1,0:T(8,128)S(1)}, f32[64,384]{1,0:T(8,128)S(1)}, u32[]{:S(2)}, u32[]{:S(2)}) collective-permute-start(f32[64,384]{1,0:T(8,128)S(1)} %get-tuple-element.8), channel_id=1, source_target_pairs={{0,1},{1,0},{2,3},{3,2},{4,5},{5,4},{6,7},{7,6},{8,9},{9,8},{10,11... | collective-permute-start | bytes 294920 | tf_op jit(solution)/shard_map/ppermute | solution.py:222
  18.1 0.9 %collective-permute-done.7 = f32[64,384]{1,0:T(8,128)S(1)} collective-permute-done((f32[64,384]{1,0:T(8,128)S(1)}, f32[64,384]{1,0:T(8,128)S(1)}, u32[]{:S(2)}, u32[]{:S(2)}) %collective-permute-start.7) | collective-permute-done | bytes 98336 | tf_op jit(solution)/shard_map/ppermute | solution.py:222
  19.1 0.4 %collective-permute-start.11 = (bf16[16,384]{1,0:T(8,128)(2,1)S(1)}, bf16[16,384]{1,0:T(8,128)(2,1)S(1)}, u32[]{:S(2)}, u32[]{:S(2)}) collective-permute-start(bf16[16,384]{1,0:T(8,128)(2,1)S(1)} %get-tuple-element.9), channel_id=1, source_target_pairs={{0,6},{1,10},{2,0},{3,2},{4,8},{5,12},{6,4},{7,14},{8,11},{9,3},{1... | collective-permute-start | bytes 36872 | tf_op jit(solution)/shard_map/ppermute | solution.py:225
  19.5 0.3 %collective-permute-start.10 = (bf16[16,384]{1,0:T(8,128)(2,1)S(1)}, bf16[16,384]{1,0:T(8,128)(2,1)S(1)}, u32[]{:S(2)}, u32[]{:S(2)}) collective-permute-start(bf16[16,384]{1,0:T(8,128)(2,1)S(1)} %get-tuple-element.10), channel_id=1, source_target_pairs={{0,14},{1,8},{2,12},{3,4},{4,6},{5,2},{6,10},{7,0},{8,9},{9,5},{10... | collective-permute-start | bytes 36872 | tf_op jit(solution)/shard_map/ppermute | solution.py:225
  19.8 1.3 %collective-permute-start.9 = (bf16[16,384]{1,0:T(8,128)(2,1)S(1)}, bf16[16,384]{1,0:T(8,128)(2,1)S(1)}, u32[]{:S(2)}, u32[]{:S(2)}) collective-permute-start(bf16[16,384]{1,0:T(8,128)(2,1)S(1)} %get-tuple-element.11), channel_id=1, source_target_pairs={{0,12},{1,4},{2,10},{3,8},{4,14},{5,0},{6,2},{7,6},{8,7},{9,13},{1... | collective-permute-start | bytes 36872 | tf_op jit(solution)/shard_map/ppermute | solution.py:225
  21.1 2.3 %collective-permute-start.8 = (bf16[16,384]{1,0:T(8,128)(2,1)S(1)}, bf16[16,384]{1,0:T(8,128)(2,1)S(1)}, u32[]{:S(2)}, u32[]{:S(2)}) collective-permute-start(bf16[16,384]{1,0:T(8,128)(2,1)S(1)} %get-tuple-element.12), channel_id=1, source_target_pairs={{0,2},{1,0},{2,6},{3,14},{4,10},{5,4},{6,8},{7,12},{8,15},{9,1},{1... | collective-permute-start | bytes 36872 | tf_op jit(solution)/shard_map/ppermute | solution.py:225
  23.4 1.0 %collective-permute-done.11.refs_3_ = bf16[16,384]{1,0:T(8,128)(2,1)S(1)} collective-permute-done((bf16[16,384]{1,0:T(8,128)(2,1)S(1)}, bf16[16,384]{1,0:T(8,128)(2,1)S(1)}, u32[]{:S(2)}, u32[]{:S(2)}) %collective-permute-start.11) | collective-permute-done | bytes 12320 | tf_op jit(solution)/shard_map/ppermute | solution.py:225
  24.4 0.0 collective-permute-done.10.refs_2_
  24.4 0.0 collective-permute-done.9.refs_1_
  24.4 0.2 collective-permute-done.8.refs_0_
  24.6 0.6 %place.1 = bf16[16,1536]{1,0:T(8,128)(2,1)} custom-call(bf16[16,384]{1,0:T(8,128)(2,1)S(1)} %collective-permute-done.8.refs_0_, bf16[16,384]{1,0:T(8,128)(2,1)S(1)} %collective-permute-done.9.refs_1_, bf16[16,384]{1,0:T(8,128)(2,1)S(1)} %collective-permute-done.10.refs_2_, bf16[16,384]{1,0:T(8,128)(2,1)S(1)} %collective-permute-done.11.refs_3_), custom_call_target="tpu_custom_call" | custom-call | tf_op jit(solution)/shard_map/place/pallas_call | solution.py:107
  (3 shorter events, 0.0 us)
Async XLA Ops:
  0.8 9.6 %copy-start.2 = (bf16[384,1536]{1,0:T(8,128)(2,1)S(1)}, bf16[384,1536]{1,0:T(8,128)(2,1)}, u32[]{:S(2)}) copy-start(bf16[384,1536]{1,0:T(8,128)(2,1)} %weight.1) | copy-start | bytes 3538948
  0.8 13.4 %copy-start.1 = (bf16[512,1536]{1,0:T(8,128)(2,1)S(1)}, bf16[512,1536]{1,0:T(8,128)(2,1)}, u32[]{:S(2)}) copy-start(bf16[512,1536]{1,0:T(8,128)(2,1)} %refs_8_.1) | copy-start | bytes 4718596
  0.8 13.4 %copy-start = (bf16[512,1536]{1,0:T(8,128)(2,1)S(1)}, bf16[512,1536]{1,0:T(8,128)(2,1)}, u32[]{:S(2)}) copy-start(bf16[512,1536]{1,0:T(8,128)(2,1)} %refs_7_.1) | copy-start | bytes 4718596
  0.9 5.7 %collective-permute-start.2 = (bf16[16,2048]{1,0:T(8,128)(2,1)S(1)}, bf16[16,2048]{1,0:T(8,128)(2,1)S(1)}, u32[]{:S(2)}, u32[]{:S(2)}) collective-permute-start(bf16[16,2048]{1,0:T(8,128)(2,1)S(1)} %pack.1.own), channel_id=1, source_target_pairs={{0,2},{1,3},{2,0},{3,1},{4,6},{5,7},{6,4},{7,5},{8,10},{9,11},{10,... | collective-permute-start | bytes 196616 | tf_op jit(solution)/shard_map/ppermute | solution.py:211
  3.0 7.2 %collective-permute-start = (bf16[16,2048]{1,0:T(8,128)(2,1)S(1)}, bf16[16,2048]{1,0:T(8,128)(2,1)S(1)}, u32[]{:S(2)}, u32[]{:S(2)}) collective-permute-start(bf16[16,2048]{1,0:T(8,128)(2,1)S(1)} %pack.1.own), channel_id=1, source_target_pairs={{0,12},{1,13},{2,14},{3,15},{4,8},{5,9},{6,10},{7,11},{8,4},{9,5},... | collective-permute-start | bytes 196616 | tf_op jit(solution)/shard_map/ppermute | solution.py:211
  6.3 5.5 %collective-permute-start.6 = (bf16[16,2048]{1,0:T(8,128)(2,1)S(1)}, bf16[16,2048]{1,0:T(8,128)(2,1)S(1)}, u32[]{:S(2)}, u32[]{:S(2)}) collective-permute-start(bf16[16,2048]{1,0:T(8,128)(2,1)S(1)} %pack.1.own), channel_id=1, source_target_pairs={{0,8},{1,9},{2,10},{3,11},{4,12},{5,13},{6,14},{7,15},{8,0},{9,1},... | collective-permute-start | bytes 196616 | tf_op jit(solution)/shard_map/ppermute | solution.py:211
  6.3 5.5 %collective-permute-start.5 = (bf16[16,2048]{1,0:T(8,128)(2,1)S(1)}, bf16[16,2048]{1,0:T(8,128)(2,1)S(1)}, u32[]{:S(2)}, u32[]{:S(2)}) collective-permute-start(bf16[16,2048]{1,0:T(8,128)(2,1)S(1)} %pack.1.own), channel_id=1, source_target_pairs={{0,4},{1,5},{2,6},{3,7},{4,0},{5,1},{6,2},{7,3},{8,12},{9,13},{10,... | collective-permute-start | bytes 196616 | tf_op jit(solution)/shard_map/ppermute | solution.py:211
  6.6 7.4 %collective-permute-start.4 = (bf16[16,2048]{1,0:T(8,128)(2,1)S(1)}, bf16[16,2048]{1,0:T(8,128)(2,1)S(1)}, u32[]{:S(2)}, u32[]{:S(2)}) collective-permute-start(bf16[16,2048]{1,0:T(8,128)(2,1)S(1)} %collective-permute-done.2.refs_6_), channel_id=1, source_target_pairs={{0,8},{1,9},{2,10},{3,11},{4,12},{5,13},{6,14},{7,15},{8,0},{9,1},... | collective-permute-start | bytes 196616 | tf_op jit(solution)/shard_map/ppermute | solution.py:211
  8.7 5.6 %collective-permute-start.3 = (bf16[16,2048]{1,0:T(8,128)(2,1)S(1)}, bf16[16,2048]{1,0:T(8,128)(2,1)S(1)}, u32[]{:S(2)}, u32[]{:S(2)}) collective-permute-start(bf16[16,2048]{1,0:T(8,128)(2,1)S(1)} %collective-permute-done.2.refs_6_), channel_id=1, source_target_pairs={{0,4},{1,5},{2,6},{3,7},{4,0},{5,1},{6,2},{7,3},{8,12},{9,13},{10,... | collective-permute-start | bytes 196616 | tf_op jit(solution)/shard_map/ppermute | solution.py:211
  10.1 4.1 %collective-permute-start.1 = (bf16[16,2048]{1,0:T(8,128)(2,1)S(1)}, bf16[16,2048]{1,0:T(8,128)(2,1)S(1)}, u32[]{:S(2)}, u32[]{:S(2)}) collective-permute-start(bf16[16,2048]{1,0:T(8,128)(2,1)S(1)} %collective-permute-done.refs_5_), channel_id=1, source_target_pairs={{0,2},{1,3},{2,0},{3,1},{4,6},{5,7},{6,4},{7,5},{8,10},{9,11},{10,... | collective-permute-start | bytes 196616 | tf_op jit(solution)/shard_map/ppermute | solution.py:211
  15.5 3.5 %collective-permute-start.7 = (f32[64,384]{1,0:T(8,128)S(1)}, f32[64,384]{1,0:T(8,128)S(1)}, u32[]{:S(2)}, u32[]{:S(2)}) collective-permute-start(f32[64,384]{1,0:T(8,128)S(1)} %get-tuple-element.8), channel_id=1, source_target_pairs={{0,1},{1,0},{2,3},{3,2},{4,5},{5,4},{6,7},{7,6},{8,9},{9,8},{10,11... | collective-permute-start | bytes 294920 | tf_op jit(solution)/shard_map/ppermute | solution.py:222
  19.1 5.3 %collective-permute-start.11 = (bf16[16,384]{1,0:T(8,128)(2,1)S(1)}, bf16[16,384]{1,0:T(8,128)(2,1)S(1)}, u32[]{:S(2)}, u32[]{:S(2)}) collective-permute-start(bf16[16,384]{1,0:T(8,128)(2,1)S(1)} %get-tuple-element.9), channel_id=1, source_target_pairs={{0,6},{1,10},{2,0},{3,2},{4,8},{5,12},{6,4},{7,14},{8,11},{9,3},{1... | collective-permute-start | bytes 36872 | tf_op jit(solution)/shard_map/ppermute | solution.py:225
  19.5 4.9 %collective-permute-start.10 = (bf16[16,384]{1,0:T(8,128)(2,1)S(1)}, bf16[16,384]{1,0:T(8,128)(2,1)S(1)}, u32[]{:S(2)}, u32[]{:S(2)}) collective-permute-start(bf16[16,384]{1,0:T(8,128)(2,1)S(1)} %get-tuple-element.10), channel_id=1, source_target_pairs={{0,14},{1,8},{2,12},{3,4},{4,6},{5,2},{6,10},{7,0},{8,9},{9,5},{10... | collective-permute-start | bytes 36872 | tf_op jit(solution)/shard_map/ppermute | solution.py:225
  19.8 4.6 %collective-permute-start.9 = (bf16[16,384]{1,0:T(8,128)(2,1)S(1)}, bf16[16,384]{1,0:T(8,128)(2,1)S(1)}, u32[]{:S(2)}, u32[]{:S(2)}) collective-permute-start(bf16[16,384]{1,0:T(8,128)(2,1)S(1)} %get-tuple-element.11), channel_id=1, source_target_pairs={{0,12},{1,4},{2,10},{3,8},{4,14},{5,0},{6,2},{7,6},{8,7},{9,13},{1... | collective-permute-start | bytes 36872 | tf_op jit(solution)/shard_map/ppermute | solution.py:225
  21.1 3.5 %collective-permute-start.8 = (bf16[16,384]{1,0:T(8,128)(2,1)S(1)}, bf16[16,384]{1,0:T(8,128)(2,1)S(1)}, u32[]{:S(2)}, u32[]{:S(2)}) collective-permute-start(bf16[16,384]{1,0:T(8,128)(2,1)S(1)} %get-tuple-element.12), channel_id=1, source_target_pairs={{0,2},{1,0},{2,6},{3,14},{4,10},{5,4},{6,8},{7,12},{8,15},{9,1},{1... | collective-permute-start | bytes 36872 | tf_op jit(solution)/shard_map/ppermute | solution.py:225

commit v7 on v6

--- a/solution.py
+++ b/solution.py
@@ -41,10 +41,10 @@
     latent = jnp.concatenate([b[:, width:] for b in (own, *received)], axis=0)
     scale = 1.0 / math.sqrt(HEAD_DIM)
     heads = [slice(first, first + HEAD_DIM) for first in range(0, width, HEAD_DIM)]
-    keys = jnp.dot(latent, key_basis[...], preferred_element_type=jnp.float32).astype(jnp.bfloat16)
     values = jnp.dot(latent, value_basis[...], preferred_element_type=jnp.float32).astype(
         jnp.bfloat16
     )
+    keys = jnp.dot(latent, key_basis[...], preferred_element_type=jnp.float32).astype(jnp.bfloat16)
     scores = [
         lax.dot_general(queries[:, c], keys[:, c], NT, preferred_element_type=jnp.float32) * scale
         for c in heads
@@ -138,23 +138,23 @@
         self.count, self.half = count, count // 2
         if count == 8:
             self.routes = (
-                (0, 1, 1),
-                (0, 6, 6),
-                (0, 4, 4),
-                (0, 2, 2),
-                (1, 4, 4),
-                (1, 2, 2),
-                (2, 1, 1),
+                (0, 2, 1),
+                (0, 1, 4),
+                (0, 6, 2),
+                (0, 4, 7),
+                (2, 2, 2),
+                (2, 4, 1),
+                (3, 1, 1),
             )
             self.ways = (
-                ((3, 7, 6, 1), (5, 4, 2, 0)),
-                ((0, 6, 5, 3), (1, 2, 4, 7)),
-                ((4, 3, 7, 5), (6, 1, 0, 2)),
-                ((2, 5, 1, 4), (7, 0, 3, 6)),
-                ((5, 4, 3, 7), (1, 2, 6, 0)),
-                ((7, 6, 4, 5), (2, 3, 0, 1)),
-                ((6, 1, 5, 3), (4, 0, 7, 2)),
-                ((3, 7, 1, 6), (0, 5, 2, 4)),
+                ((2, 6, 7, 1), (3, 5, 4, 0)),
+                ((4, 2, 3, 7), (5, 0, 1, 6)),
+                ((6, 1, 5, 3), (7, 4, 0, 2)),
+                ((0, 7, 6, 5), (1, 3, 2, 4)),
+                ((7, 4, 5, 6), (2, 1, 3, 0)),
+                ((5, 7, 4, 3), (6, 2, 0, 1)),
+                ((4, 0, 6, 5), (1, 3, 7, 2)),
+                ((3, 5, 1, 7), (0, 6, 2, 4)),
             )
         else:
             inner = range(1, self.half)

time: 25.6 us -> 25.5 us (level)
  starting transfers between devices: 16.4 us -> 16.1 us
  waiting for transfers between devices: 5.67 us -> 5.95 us
    ppermute x7, starting transfers between devices: 9.51 us -> 8.17 us  [gather(): blocks.append(lax.ppermute(blocks[block], ('seq', 'head'), plan.out(flips)))]
    ppermute x1, starting transfers between devices: 2.56 us -> 3.69 us  [direct(): other = lax.ppermute(send, 'head', [(0, 1), (1, 0)])]
  transfers between devices with their start and end apart: 12 -> 12, of which waited for: 6 -> 5; matrix products, arithmetic and copies ran while one was open for 0% -> 0% of each run, Pallas kernels for 1% -> 1%
where the time goes in v7:
time: 25.5 us; the launch traced here: 25.2 us
  starting transfers between devices  16.1 us (63%)
  waiting for transfers between devices  5.95 us (23%)
  Pallas kernels  2.27 us (9%)
  other arithmetic  0.83 us (3%)
    ppermute x7, starting transfers between devices, gather(): blocks.append(lax.ppermute(blocks[block], ('seq', 'head'), plan.out(flips)))  8.17 us
    ppermute x4, starting transfers between devices, direct(): lax.ppermute(total[step * rows:(step + 1) * rows], ('seq', 'head'), plan....  4.24 us
    ppermute x7, waiting for transfers between devices, gather(): blocks.append(lax.ppermute(blocks[block], ('seq', 'head'), plan.out(flips)))  3.72 us
    ppermute x1, starting transfers between devices, direct(): other = lax.ppermute(send, 'head', [(0, 1), (1, 0)])  3.69 us
    ppermute x4, waiting for transfers between devices, direct(): lax.ppermute(total[step * rows:(step + 1) * rows], ('seq', 'head'), plan....  1.29 us
    pallas_call x1, Pallas kernels, mix(): pl.pallas_call(functools.partial(mix_kernel, plan), out_shape=[jax.ShapeD...  1.28 us
    ppermute x1, waiting for transfers between devices, direct(): other = lax.ppermute(send, 'head', [(0, 1), (1, 0)])  0.94 us
    concatenate x1, other arithmetic, direct(): own = jnp.concatenate([queries, latent.T], axis=1)  0.82 us
  transfers between devices with their start and end apart: 12, of which 5 were waited for; matrix products, arithmetic and copies ran while one was open for 0% of the time, Pallas kernels for 1%

profile of v7, /device:TPU:1, one launch (start us, length us, event | category | flops | bytes accessed | tf_op | source)
XLA Modules:
  0.0 25.2 jit_solution(15478804587117878138)
XLA Ops:
  0.0 0.8 %pad_maximum_fusion.block = bf16[16,2048]{1,0:T(8,128)(2,1)S(1)} fusion(bf16[16,512]{1,0:T(8,128)(2,1)} %bitcast.1, bf16[16,1536]{1,0:T(8,128)(2,1)} %param.5), kind=kLoop, calls=%fused_computation.1 | loop fusion | flops 131072 | bytes 131072 | tf_op jit(solution)/shard_map/concatenate | solution.py:218
  0.8 0.0 copy-start.2
  0.8 0.0 copy-start.1
  0.8 0.0 copy-start
  0.9 3.2 %collective-permute-start.2 = (bf16[16,2048]{1,0:T(8,128)(2,1)S(1)}, bf16[16,2048]{1,0:T(8,128)(2,1)S(1)}, u32[]{:S(2)}, u32[]{:S(2)}) collective-permute-start(bf16[16,2048]{1,0:T(8,128)(2,1)S(1)} %pack.1.own), channel_id=1, source_target_pairs={{0,2},{1,9},{2,0},{3,11},{4,6},{5,13},{6,4},{7,15},{8,10},{9,1},{1... | collective-permute-start | bytes 196616 | tf_op jit(solution)/shard_map/ppermute | solution.py:211
  4.1 1.3 %collective-permute-start = (bf16[16,2048]{1,0:T(8,128)(2,1)S(1)}, bf16[16,2048]{1,0:T(8,128)(2,1)S(1)}, u32[]{:S(2)}, u32[]{:S(2)}) collective-permute-start(bf16[16,2048]{1,0:T(8,128)(2,1)S(1)} %pack.1.own), channel_id=1, source_target_pairs={{0,12},{1,5},{2,14},{3,7},{4,8},{5,1},{6,10},{7,3},{8,4},{9,13},{1... | collective-permute-start | bytes 196616 | tf_op jit(solution)/shard_map/ppermute | solution.py:211
  5.4 1.2 %collective-permute-start.6 = (bf16[16,2048]{1,0:T(8,128)(2,1)S(1)}, bf16[16,2048]{1,0:T(8,128)(2,1)S(1)}, u32[]{:S(2)}, u32[]{:S(2)}) collective-permute-start(bf16[16,2048]{1,0:T(8,128)(2,1)S(1)} %pack.1.own), channel_id=1, source_target_pairs={{0,4},{1,3},{2,6},{3,1},{4,0},{5,7},{6,2},{7,5},{8,12},{9,11},{10,... | collective-permute-start | bytes 196616 | tf_op jit(solution)/shard_map/ppermute | solution.py:211
  6.6 0.0 collective-permute-start.5
  6.6 0.0 collective-permute-done.2.refs_5_
  6.6 0.6 %collective-permute-start.4 = (bf16[16,2048]{1,0:T(8,128)(2,1)S(1)}, bf16[16,2048]{1,0:T(8,128)(2,1)S(1)}, u32[]{:S(2)}, u32[]{:S(2)}) collective-permute-start(bf16[16,2048]{1,0:T(8,128)(2,1)S(1)} %collective-permute-done.2.refs_5_), channel_id=1, source_target_pairs={{0,4},{1,5},{2,6},{3,7},{4,0},{5,1},{6,2},{7,3},{8,12},{9,13},{10,... | collective-permute-start | bytes 196616 | tf_op jit(solution)/shard_map/ppermute | solution.py:211
  7.2 1.8 %collective-permute-start.3 = (bf16[16,2048]{1,0:T(8,128)(2,1)S(1)}, bf16[16,2048]{1,0:T(8,128)(2,1)S(1)}, u32[]{:S(2)}, u32[]{:S(2)}) collective-permute-start(bf16[16,2048]{1,0:T(8,128)(2,1)S(1)} %collective-permute-done.2.refs_5_), channel_id=1, source_target_pairs={{0,8},{1,3},{2,10},{3,1},{4,12},{5,7},{6,14},{7,5},{8,0},{9,11},{1... | collective-permute-start | bytes 196616 | tf_op jit(solution)/shard_map/ppermute | solution.py:211
  9.0 0.0 collective-permute-done.refs_4_
  9.0 0.0 collective-permute-start.1
  9.0 0.0 copy-done.2
  9.0 0.4 %turn.1.refs_9_ = bf16[1536,384]{1,0:T(8,128)(2,1)S(1)} custom-call(bf16[384,1536]{1,0:T(8,128)(2,1)S(1)} %copy-done.2), custom_call_target="tpu_custom_call" | custom-call | bytes 2359296 | tf_op jit(solution)/shard_map/turn/pallas_call | solution.py:22
  9.4 0.0 collective-permute-done.6.refs_6_
  9.4 3.2 %collective-permute-done.5.refs_3_ = bf16[16,2048]{1,0:T(8,128)(2,1)S(1)} collective-permute-done((bf16[16,2048]{1,0:T(8,128)(2,1)S(1)}, bf16[16,2048]{1,0:T(8,128)(2,1)S(1)}, u32[]{:S(2)}, u32[]{:S(2)}) %collective-permute-start.5) | collective-permute-done | bytes 65568 | tf_op jit(solution)/shard_map/ppermute | solution.py:211
  12.6 0.0 collective-permute-done.4.refs_2_
  12.6 0.0 collective-permute-done.3.refs_1_
  12.7 0.5 %collective-permute-done.1.refs_0_ = bf16[16,2048]{1,0:T(8,128)(2,1)S(1)} collective-permute-done((bf16[16,2048]{1,0:T(8,128)(2,1)S(1)}, bf16[16,2048]{1,0:T(8,128)(2,1)S(1)}, u32[]{:S(2)}, u32[]{:S(2)}) %collective-permute-start.1) | collective-permute-done | bytes 65568 | tf_op jit(solution)/shard_map/ppermute | solution.py:211
  13.1 0.0 copy-done.1
  13.1 0.0 copy-done
  13.1 1.3 %mix.1 = (f32[64,384]{1,0:T(8,128)S(1)}, f32[64,384]{1,0:T(8,128)S(1)}) custom-call(bf16[16,2048]{1,0:T(8,128)(2,1)S(1)} %pack.1.own, bf16[16,2048]{1,0:T(8,128)(2,1)S(1)} %collective-permute-done.1.refs_0_, bf16[16,2048]{1,0:T(8,128)(2,1)S(1)} %collective-permute-done.3.refs_1_, bf16[16,2048]{1,0:T(8,128)(2,1)S(1)} %collective-permute-done.4.refs_2_, ...), custom_call_target="tpu_custom_call" | custom-call | flops 654311424 | bytes 4325376 | tf_op jit(solution)/shard_map/mix/pallas_call | solution.py:77
  14.4 3.7 %collective-permute-start.7 = (f32[64,384]{1,0:T(8,128)S(1)}, f32[64,384]{1,0:T(8,128)S(1)}, u32[]{:S(2)}, u32[]{:S(2)}) collective-permute-start(f32[64,384]{1,0:T(8,128)S(1)} %get-tuple-element.8), channel_id=1, source_target_pairs={{0,1},{1,0},{2,3},{3,2},{4,5},{5,4},{6,7},{7,6},{8,9},{9,8},{10,11... | collective-permute-start | bytes 294920 | tf_op jit(solution)/shard_map/ppermute | solution.py:222
  18.1 0.9 %collective-permute-done.7 = f32[64,384]{1,0:T(8,128)S(1)} collective-permute-done((f32[64,384]{1,0:T(8,128)S(1)}, f32[64,384]{1,0:T(8,128)S(1)}, u32[]{:S(2)}, u32[]{:S(2)}) %collective-permute-start.7) | collective-permute-done | bytes 98336 | tf_op jit(solution)/shard_map/ppermute | solution.py:222
  19.1 0.2 collective-permute-start.11
  19.3 0.8 %collective-permute-start.10 = (bf16[16,384]{1,0:T(8,128)(2,1)S(1)}, bf16[16,384]{1,0:T(8,128)(2,1)S(1)}, u32[]{:S(2)}, u32[]{:S(2)}) collective-permute-start(bf16[16,384]{1,0:T(8,128)(2,1)S(1)} %get-tuple-element.10), channel_id=1, source_target_pairs={{0,12},{1,10},{2,4},{3,0},{4,2},{5,8},{6,14},{7,6},{8,9},{9,3},{10... | collective-permute-start | bytes 36872 | tf_op jit(solution)/shard_map/ppermute | solution.py:225
  20.1 1.0 %collective-permute-start.9 = (bf16[16,384]{1,0:T(8,128)(2,1)S(1)}, bf16[16,384]{1,0:T(8,128)(2,1)S(1)}, u32[]{:S(2)}, u32[]{:S(2)}) collective-permute-start(bf16[16,384]{1,0:T(8,128)(2,1)S(1)} %get-tuple-element.11), channel_id=1, source_target_pairs={{0,14},{1,8},{2,6},{3,2},{4,10},{5,0},{6,12},{7,4},{8,11},{9,7},{1... | collective-permute-start | bytes 36872 | tf_op jit(solution)/shard_map/ppermute | solution.py:225
  21.2 2.2 %collective-permute-start.8 = (bf16[16,384]{1,0:T(8,128)(2,1)S(1)}, bf16[16,384]{1,0:T(8,128)(2,1)S(1)}, u32[]{:S(2)}, u32[]{:S(2)}) collective-permute-start(bf16[16,384]{1,0:T(8,128)(2,1)S(1)} %get-tuple-element.12), channel_id=1, source_target_pairs={{0,2},{1,0},{2,14},{3,12},{4,6},{5,4},{6,10},{7,8},{8,13},{9,1},{1... | collective-permute-start | bytes 36872 | tf_op jit(solution)/shard_map/ppermute | solution.py:225
  23.3 1.2 %collective-permute-done.11.refs_3_ = bf16[16,384]{1,0:T(8,128)(2,1)S(1)} collective-permute-done((bf16[16,384]{1,0:T(8,128)(2,1)S(1)}, bf16[16,384]{1,0:T(8,128)(2,1)S(1)}, u32[]{:S(2)}, u32[]{:S(2)}) %collective-permute-start.11) | collective-permute-done | bytes 12320 | tf_op jit(solution)/shard_map/ppermute | solution.py:225
  24.5 0.0 collective-permute-done.10.refs_2_
  24.5 0.0 collective-permute-done.9.refs_1_
  24.6 0.1 collective-permute-done.8.refs_0_
  24.6 0.6 %place.1 = bf16[16,1536]{1,0:T(8,128)(2,1)} custom-call(bf16[16,384]{1,0:T(8,128)(2,1)S(1)} %collective-permute-done.8.refs_0_, bf16[16,384]{1,0:T(8,128)(2,1)S(1)} %collective-permute-done.9.refs_1_, bf16[16,384]{1,0:T(8,128)(2,1)S(1)} %collective-permute-done.10.refs_2_, bf16[16,384]{1,0:T(8,128)(2,1)S(1)} %collective-permute-done.11.refs_3_), custom_call_target="tpu_custom_call" | custom-call | tf_op jit(solution)/shard_map/place/pallas_call | solution.py:107
  (3 shorter events, 0.0 us)
Async XLA Ops:
  0.8 8.2 %copy-start.2 = (bf16[384,1536]{1,0:T(8,128)(2,1)S(1)}, bf16[384,1536]{1,0:T(8,128)(2,1)}, u32[]{:S(2)}) copy-start(bf16[384,1536]{1,0:T(8,128)(2,1)} %weight.1) | copy-start | bytes 3538948
  0.8 12.3 %copy-start.1 = (bf16[512,1536]{1,0:T(8,128)(2,1)S(1)}, bf16[512,1536]{1,0:T(8,128)(2,1)}, u32[]{:S(2)}) copy-start(bf16[512,1536]{1,0:T(8,128)(2,1)} %refs_8_.1) | copy-start | bytes 4718596
  0.8 12.3 %copy-start = (bf16[512,1536]{1,0:T(8,128)(2,1)S(1)}, bf16[512,1536]{1,0:T(8,128)(2,1)}, u32[]{:S(2)}) copy-start(bf16[512,1536]{1,0:T(8,128)(2,1)} %refs_7_.1) | copy-start | bytes 4718596
  0.9 5.7 %collective-permute-start.2 = (bf16[16,2048]{1,0:T(8,128)(2,1)S(1)}, bf16[16,2048]{1,0:T(8,128)(2,1)S(1)}, u32[]{:S(2)}, u32[]{:S(2)}) collective-permute-start(bf16[16,2048]{1,0:T(8,128)(2,1)S(1)} %pack.1.own), channel_id=1, source_target_pairs={{0,2},{1,9},{2,0},{3,11},{4,6},{5,13},{6,4},{7,15},{8,10},{9,1},{1... | collective-permute-start | bytes 196616 | tf_op jit(solution)/shard_map/ppermute | solution.py:211
  4.1 4.9 %collective-permute-start = (bf16[16,2048]{1,0:T(8,128)(2,1)S(1)}, bf16[16,2048]{1,0:T(8,128)(2,1)S(1)}, u32[]{:S(2)}, u32[]{:S(2)}) collective-permute-start(bf16[16,2048]{1,0:T(8,128)(2,1)S(1)} %pack.1.own), channel_id=1, source_target_pairs={{0,12},{1,5},{2,14},{3,7},{4,8},{5,1},{6,10},{7,3},{8,4},{9,13},{1... | collective-permute-start | bytes 196616 | tf_op jit(solution)/shard_map/ppermute | solution.py:211
  5.4 4.0 %collective-permute-start.6 = (bf16[16,2048]{1,0:T(8,128)(2,1)S(1)}, bf16[16,2048]{1,0:T(8,128)(2,1)S(1)}, u32[]{:S(2)}, u32[]{:S(2)}) collective-permute-start(bf16[16,2048]{1,0:T(8,128)(2,1)S(1)} %pack.1.own), channel_id=1, source_target_pairs={{0,4},{1,3},{2,6},{3,1},{4,0},{5,7},{6,2},{7,5},{8,12},{9,11},{10,... | collective-permute-start | bytes 196616 | tf_op jit(solution)/shard_map/ppermute | solution.py:211
  6.6 6.1 %collective-permute-start.5 = (bf16[16,2048]{1,0:T(8,128)(2,1)S(1)}, bf16[16,2048]{1,0:T(8,128)(2,1)S(1)}, u32[]{:S(2)}, u32[]{:S(2)}) collective-permute-start(bf16[16,2048]{1,0:T(8,128)(2,1)S(1)} %pack.1.own), channel_id=1, source_target_pairs={{0,8},{1,15},{2,10},{3,13},{4,12},{5,11},{6,14},{7,9},{8,0},{9,7},... | collective-permute-start | bytes 196616 | tf_op jit(solution)/shard_map/ppermute | solution.py:211
  6.6 6.1 %collective-permute-start.4 = (bf16[16,2048]{1,0:T(8,128)(2,1)S(1)}, bf16[16,2048]{1,0:T(8,128)(2,1)S(1)}, u32[]{:S(2)}, u32[]{:S(2)}) collective-permute-start(bf16[16,2048]{1,0:T(8,128)(2,1)S(1)} %collective-permute-done.2.refs_5_), channel_id=1, source_target_pairs={{0,4},{1,5},{2,6},{3,7},{4,0},{5,1},{6,2},{7,3},{8,12},{9,13},{10,... | collective-permute-start | bytes 196616 | tf_op jit(solution)/shard_map/ppermute | solution.py:211
  7.2 5.5 %collective-permute-start.3 = (bf16[16,2048]{1,0:T(8,128)(2,1)S(1)}, bf16[16,2048]{1,0:T(8,128)(2,1)S(1)}, u32[]{:S(2)}, u32[]{:S(2)}) collective-permute-start(bf16[16,2048]{1,0:T(8,128)(2,1)S(1)} %collective-permute-done.2.refs_5_), channel_id=1, source_target_pairs={{0,8},{1,3},{2,10},{3,1},{4,12},{5,7},{6,14},{7,5},{8,0},{9,11},{1... | collective-permute-start | bytes 196616 | tf_op jit(solution)/shard_map/ppermute | solution.py:211
  9.0 4.1 %collective-permute-start.1 = (bf16[16,2048]{1,0:T(8,128)(2,1)S(1)}, bf16[16,2048]{1,0:T(8,128)(2,1)S(1)}, u32[]{:S(2)}, u32[]{:S(2)}) collective-permute-start(bf16[16,2048]{1,0:T(8,128)(2,1)S(1)} %collective-permute-done.refs_4_), channel_id=1, source_target_pairs={{0,2},{1,3},{2,0},{3,1},{4,6},{5,7},{6,4},{7,5},{8,10},{9,11},{10,... | collective-permute-start | bytes 196616 | tf_op jit(solution)/shard_map/ppermute | solution.py:211
  14.4 4.6 %collective-permute-start.7 = (f32[64,384]{1,0:T(8,128)S(1)}, f32[64,384]{1,0:T(8,128)S(1)}, u32[]{:S(2)}, u32[]{:S(2)}) collective-permute-start(f32[64,384]{1,0:T(8,128)S(1)} %get-tuple-element.8), channel_id=1, source_target_pairs={{0,1},{1,0},{2,3},{3,2},{4,5},{5,4},{6,7},{7,6},{8,9},{9,8},{10,11... | collective-permute-start | bytes 294920 | tf_op jit(solution)/shard_map/ppermute | solution.py:222
  19.1 5.5 %collective-permute-start.11 = (bf16[16,384]{1,0:T(8,128)(2,1)S(1)}, bf16[16,384]{1,0:T(8,128)(2,1)S(1)}, u32[]{:S(2)}, u32[]{:S(2)}) collective-permute-start(bf16[16,384]{1,0:T(8,128)(2,1)S(1)} %get-tuple-element.9), channel_id=1, source_target_pairs={{0,4},{1,6},{2,8},{3,10},{4,12},{5,14},{6,0},{7,2},{8,15},{9,5},{1... | collective-permute-start | bytes 36872 | tf_op jit(solution)/shard_map/ppermute | solution.py:225
  19.3 5.2 %collective-permute-start.10 = (bf16[16,384]{1,0:T(8,128)(2,1)S(1)}, bf16[16,384]{1,0:T(8,128)(2,1)S(1)}, u32[]{:S(2)}, u32[]{:S(2)}) collective-permute-start(bf16[16,384]{1,0:T(8,128)(2,1)S(1)} %get-tuple-element.10), channel_id=1, source_target_pairs={{0,12},{1,10},{2,4},{3,0},{4,2},{5,8},{6,14},{7,6},{8,9},{9,3},{10... | collective-permute-start | bytes 36872 | tf_op jit(solution)/shard_map/ppermute | solution.py:225
  20.1 4.4 %collective-permute-start.9 = (bf16[16,384]{1,0:T(8,128)(2,1)S(1)}, bf16[16,384]{1,0:T(8,128)(2,1)S(1)}, u32[]{:S(2)}, u32[]{:S(2)}) collective-permute-start(bf16[16,384]{1,0:T(8,128)(2,1)S(1)} %get-tuple-element.11), channel_id=1, source_target_pairs={{0,14},{1,8},{2,6},{3,2},{4,10},{5,0},{6,12},{7,4},{8,11},{9,7},{1... | collective-permute-start | bytes 36872 | tf_op jit(solution)/shard_map/ppermute | solution.py:225
  21.2 3.4 %collective-permute-start.8 = (bf16[16,384]{1,0:T(8,128)(2,1)S(1)}, bf16[16,384]{1,0:T(8,128)(2,1)S(1)}, u32[]{:S(2)}, u32[]{:S(2)}) collective-permute-start(bf16[16,384]{1,0:T(8,128)(2,1)S(1)} %get-tuple-element.12), channel_id=1, source_target_pairs={{0,2},{1,0},{2,14},{3,12},{4,6},{5,4},{6,10},{7,8},{8,13},{9,1},{1... | collective-permute-start | bytes 36872 | tf_op jit(solution)/shard_map/ppermute | solution.py:225

commit v8 on v6

--- a/solution.py
+++ b/solution.py
@@ -66,7 +66,9 @@
                 look_up(plan.kept(0, step, other)),
                 look_up(plan.kept(1, step, 1 - other)),
             )
-            target[part, :] = partial_sum[pl.ds(pl.multiple_of(at * rows, rows), rows), :]
+            target[part, :] = partial_sum[pl.ds(pl.multiple_of(at * rows, rows), rows), :].astype(
+                target.dtype
+            )
 
 
 def mix(plan, own, received, key_basis, value_basis, out_weight):
@@ -76,7 +78,10 @@
     vmem = pl.BlockSpec(memory_space=pltpu.VMEM)
     return pl.pallas_call(
         functools.partial(mix_kernel, plan),
-        out_shape=[jax.ShapeDtypeStruct((rows // 2, features), jnp.float32)] * 2,
+        out_shape=[
+            jax.ShapeDtypeStruct((rows // 2, features), kind)
+            for kind in (jnp.float32, jnp.bfloat16)
+        ],
         in_specs=[vmem] * (len(received) + 4),
         out_specs=[vmem] * 2,
         scratch_shapes=[pltpu.VMEM((rows, features), jnp.float32)],

time: 25.6 us -> 25.5 us (level)
  no operation moved by 1% of the time
where the time goes in v8:
time: 25.5 us; the launch traced here: 25.2 us
  starting transfers between devices  16.4 us (64%)
  waiting for transfers between devices  5.6 us (22%)
  Pallas kernels  2.27 us (9%)
  other arithmetic  0.84 us (3%)
    ppermute x7, starting transfers between devices, gather(): blocks.append(lax.ppermute(blocks[block], ('seq', 'head'), plan.out(flips)))  9.51 us
    ppermute x4, starting transfers between devices, direct(): lax.ppermute(total[step * rows:(step + 1) * rows], ('seq', 'head'), plan....  4.31 us
    ppermute x7, waiting for transfers between devices, gather(): blocks.append(lax.ppermute(blocks[block], ('seq', 'head'), plan.out(flips)))  3.51 us
    ppermute x1, starting transfers between devices, direct(): other = lax.ppermute(send, 'head', [(0, 1), (1, 0)])  2.56 us
    pallas_call x1, Pallas kernels, mix(): pl.pallas_call(functools.partial(mix_kernel, plan), out_shape=[jax.ShapeD...  1.28 us
    ppermute x4, waiting for transfers between devices, direct(): lax.ppermute(total[step * rows:(step + 1) * rows], ('seq', 'head'), plan....  1.21 us
    ppermute x1, waiting for transfers between devices, direct(): other = lax.ppermute(send, 'head', [(0, 1), (1, 0)])  0.88 us
    concatenate x1, other arithmetic, direct(): own = jnp.concatenate([queries, latent.T], axis=1)  0.82 us
  transfers between devices with their start and end apart: 12, of which 6 were waited for; matrix products, arithmetic and copies ran while one was open for 0% of the time, Pallas kernels for 1%

profile of v8, /device:TPU:1, one launch (start us, length us, event | category | flops | bytes accessed | tf_op | source)
XLA Modules:
  0.0 25.2 jit_solution(3624557503738773120)
XLA Ops:
  0.0 0.8 %pad_maximum_fusion.block = bf16[16,2048]{1,0:T(8,128)(2,1)S(1)} fusion(bf16[16,512]{1,0:T(8,128)(2,1)} %bitcast.1, bf16[16,1536]{1,0:T(8,128)(2,1)} %param.5), kind=kLoop, calls=%fused_computation.1 | loop fusion | flops 131072 | bytes 131072 | tf_op jit(solution)/shard_map/concatenate | solution.py:223
  0.8 0.0 copy-start.2
  0.8 0.0 copy-start.1
  0.8 0.0 copy-start
  0.9 2.1 %collective-permute-start.2 = (bf16[16,2048]{1,0:T(8,128)(2,1)S(1)}, bf16[16,2048]{1,0:T(8,128)(2,1)S(1)}, u32[]{:S(2)}, u32[]{:S(2)}) collective-permute-start(bf16[16,2048]{1,0:T(8,128)(2,1)S(1)} %pack.1.own), channel_id=1, source_target_pairs={{0,2},{1,3},{2,0},{3,1},{4,6},{5,7},{6,4},{7,5},{8,10},{9,11},{10,... | collective-permute-start | bytes 196616 | tf_op jit(solution)/shard_map/ppermute | solution.py:216
  3.0 3.3 %collective-permute-start = (bf16[16,2048]{1,0:T(8,128)(2,1)S(1)}, bf16[16,2048]{1,0:T(8,128)(2,1)S(1)}, u32[]{:S(2)}, u32[]{:S(2)}) collective-permute-start(bf16[16,2048]{1,0:T(8,128)(2,1)S(1)} %pack.1.own), channel_id=1, source_target_pairs={{0,12},{1,13},{2,14},{3,15},{4,8},{5,9},{6,10},{7,11},{8,4},{9,5},... | collective-permute-start | bytes 196616 | tf_op jit(solution)/shard_map/ppermute | solution.py:216
  6.3 0.0 collective-permute-start.6
  6.3 0.3 %collective-permute-start.5 = (bf16[16,2048]{1,0:T(8,128)(2,1)S(1)}, bf16[16,2048]{1,0:T(8,128)(2,1)S(1)}, u32[]{:S(2)}, u32[]{:S(2)}) collective-permute-start(bf16[16,2048]{1,0:T(8,128)(2,1)S(1)} %pack.1.own), channel_id=1, source_target_pairs={{0,4},{1,5},{2,6},{3,7},{4,0},{5,1},{6,2},{7,3},{8,12},{9,13},{10,... | collective-permute-start | bytes 196616 | tf_op jit(solution)/shard_map/ppermute | solution.py:216
  6.6 0.0 collective-permute-done.2.refs_6_
  6.6 2.1 %collective-permute-start.4 = (bf16[16,2048]{1,0:T(8,128)(2,1)S(1)}, bf16[16,2048]{1,0:T(8,128)(2,1)S(1)}, u32[]{:S(2)}, u32[]{:S(2)}) collective-permute-start(bf16[16,2048]{1,0:T(8,128)(2,1)S(1)} %collective-permute-done.2.refs_6_), channel_id=1, source_target_pairs={{0,8},{1,9},{2,10},{3,11},{4,12},{5,13},{6,14},{7,15},{8,0},{9,1},... | collective-permute-start | bytes 196616 | tf_op jit(solution)/shard_map/ppermute | solution.py:216
  8.7 1.5 %collective-permute-start.3 = (bf16[16,2048]{1,0:T(8,128)(2,1)S(1)}, bf16[16,2048]{1,0:T(8,128)(2,1)S(1)}, u32[]{:S(2)}, u32[]{:S(2)}) collective-permute-start(bf16[16,2048]{1,0:T(8,128)(2,1)S(1)} %collective-permute-done.2.refs_6_), channel_id=1, source_target_pairs={{0,4},{1,5},{2,6},{3,7},{4,0},{5,1},{6,2},{7,3},{8,12},{9,13},{10,... | collective-permute-start | bytes 196616 | tf_op jit(solution)/shard_map/ppermute | solution.py:216
  10.1 0.0 collective-permute-done.refs_5_
  10.1 0.3 %collective-permute-start.1 = (bf16[16,2048]{1,0:T(8,128)(2,1)S(1)}, bf16[16,2048]{1,0:T(8,128)(2,1)S(1)}, u32[]{:S(2)}, u32[]{:S(2)}) collective-permute-start(bf16[16,2048]{1,0:T(8,128)(2,1)S(1)} %collective-permute-done.refs_5_), channel_id=1, source_target_pairs={{0,2},{1,3},{2,0},{3,1},{4,6},{5,7},{6,4},{7,5},{8,10},{9,11},{10,... | collective-permute-start | bytes 196616 | tf_op jit(solution)/shard_map/ppermute | solution.py:216
  10.4 0.0 copy-done.2
  10.4 0.4 %turn.1.refs_9_ = bf16[1536,384]{1,0:T(8,128)(2,1)S(1)} custom-call(bf16[384,1536]{1,0:T(8,128)(2,1)S(1)} %copy-done.2), custom_call_target="tpu_custom_call" | custom-call | bytes 2359296 | tf_op jit(solution)/shard_map/turn/pallas_call | solution.py:22
  10.7 1.1 %collective-permute-done.6.refs_4_ = bf16[16,2048]{1,0:T(8,128)(2,1)S(1)} collective-permute-done((bf16[16,2048]{1,0:T(8,128)(2,1)S(1)}, bf16[16,2048]{1,0:T(8,128)(2,1)S(1)}, u32[]{:S(2)}, u32[]{:S(2)}) %collective-permute-start.6) | collective-permute-done | bytes 65568 | tf_op jit(solution)/shard_map/ppermute | solution.py:216
  11.8 0.0 collective-permute-done.5.refs_3_
  11.8 2.1 %collective-permute-done.4.refs_2_ = bf16[16,2048]{1,0:T(8,128)(2,1)S(1)} collective-permute-done((bf16[16,2048]{1,0:T(8,128)(2,1)S(1)}, bf16[16,2048]{1,0:T(8,128)(2,1)S(1)}, u32[]{:S(2)}, u32[]{:S(2)}) %collective-permute-start.4) | collective-permute-done | bytes 65568 | tf_op jit(solution)/shard_map/ppermute | solution.py:216
  14.0 0.3 %collective-permute-done.3.refs_1_ = bf16[16,2048]{1,0:T(8,128)(2,1)S(1)} collective-permute-done((bf16[16,2048]{1,0:T(8,128)(2,1)S(1)}, bf16[16,2048]{1,0:T(8,128)(2,1)S(1)}, u32[]{:S(2)}, u32[]{:S(2)}) %collective-permute-start.3) | collective-permute-done | bytes 65568 | tf_op jit(solution)/shard_map/ppermute | solution.py:216
  14.2 0.0 collective-permute-done.1.refs_0_
  14.2 0.0 copy-done.1
  14.3 0.0 copy-done
  14.3 1.3 %mix.1 = (f32[64,384]{1,0:T(8,128)S(1)}, bf16[64,384]{1,0:T(8,128)(2,1)S(1)}) custom-call(bf16[16,2048]{1,0:T(8,128)(2,1)S(1)} %pack.1.own, bf16[16,2048]{1,0:T(8,128)(2,1)S(1)} %collective-permute-done.1.refs_0_, bf16[16,2048]{1,0:T(8,128)(2,1)S(1)} %collective-permute-done.3.refs_1_, bf16[16,2048]{1,0:T(8,128)(2,1)S(1)} %collective-permute-done.4.refs_2_, ...), custom_call_target="tpu_custom_call" | custom-call | flops 654311424 | bytes 4325376 | tf_op jit(solution)/shard_map/mix/pallas_call | solution.py:79
  15.5 2.6 %collective-permute-start.7 = (bf16[64,384]{1,0:T(8,128)(2,1)S(1)}, bf16[64,384]{1,0:T(8,128)(2,1)S(1)}, u32[]{:S(2)}, u32[]{:S(2)}) collective-permute-start(bf16[64,384]{1,0:T(8,128)(2,1)S(1)} %get-tuple-element.8), channel_id=1, source_target_pairs={{0,1},{1,0},{2,3},{3,2},{4,5},{5,4},{6,7},{7,6},{8,9},{9,8},{10,11... | collective-permute-start | bytes 147464 | tf_op jit(solution)/shard_map/ppermute | solution.py:227
  18.1 0.9 %collective-permute-done.7 = bf16[64,384]{1,0:T(8,128)(2,1)S(1)} collective-permute-done((bf16[64,384]{1,0:T(8,128)(2,1)S(1)}, bf16[64,384]{1,0:T(8,128)(2,1)S(1)}, u32[]{:S(2)}, u32[]{:S(2)}) %collective-permute-start.7) | collective-permute-done | bytes 49184 | tf_op jit(solution)/shard_map/ppermute | solution.py:227
  19.0 0.4 %collective-permute-start.11 = (bf16[16,384]{1,0:T(8,128)(2,1)S(1)}, bf16[16,384]{1,0:T(8,128)(2,1)S(1)}, u32[]{:S(2)}, u32[]{:S(2)}) collective-permute-start(bf16[16,384]{1,0:T(8,128)(2,1)S(1)} %get-tuple-element.9), channel_id=1, source_target_pairs={{0,6},{1,10},{2,0},{3,2},{4,8},{5,12},{6,4},{7,14},{8,11},{9,3},{1... | collective-permute-start | bytes 36872 | tf_op jit(solution)/shard_map/ppermute | solution.py:230
  19.4 0.3 %collective-permute-start.10 = (bf16[16,384]{1,0:T(8,128)(2,1)S(1)}, bf16[16,384]{1,0:T(8,128)(2,1)S(1)}, u32[]{:S(2)}, u32[]{:S(2)}) collective-permute-start(bf16[16,384]{1,0:T(8,128)(2,1)S(1)} %get-tuple-element.10), channel_id=1, source_target_pairs={{0,14},{1,8},{2,12},{3,4},{4,6},{5,2},{6,10},{7,0},{8,9},{9,5},{10... | collective-permute-start | bytes 36872 | tf_op jit(solution)/shard_map/ppermute | solution.py:230
  19.8 1.3 %collective-permute-start.9 = (bf16[16,384]{1,0:T(8,128)(2,1)S(1)}, bf16[16,384]{1,0:T(8,128)(2,1)S(1)}, u32[]{:S(2)}, u32[]{:S(2)}) collective-permute-start(bf16[16,384]{1,0:T(8,128)(2,1)S(1)} %get-tuple-element.11), channel_id=1, source_target_pairs={{0,12},{1,4},{2,10},{3,8},{4,14},{5,0},{6,2},{7,6},{8,7},{9,13},{1... | collective-permute-start | bytes 36872 | tf_op jit(solution)/shard_map/ppermute | solution.py:230
  21.1 2.3 %collective-permute-start.8 = (bf16[16,384]{1,0:T(8,128)(2,1)S(1)}, bf16[16,384]{1,0:T(8,128)(2,1)S(1)}, u32[]{:S(2)}, u32[]{:S(2)}) collective-permute-start(bf16[16,384]{1,0:T(8,128)(2,1)S(1)} %get-tuple-element.12), channel_id=1, source_target_pairs={{0,2},{1,0},{2,6},{3,14},{4,10},{5,4},{6,8},{7,12},{8,15},{9,1},{1... | collective-permute-start | bytes 36872 | tf_op jit(solution)/shard_map/ppermute | solution.py:230
  23.3 1.0 %collective-permute-done.11.refs_3_ = bf16[16,384]{1,0:T(8,128)(2,1)S(1)} collective-permute-done((bf16[16,384]{1,0:T(8,128)(2,1)S(1)}, bf16[16,384]{1,0:T(8,128)(2,1)S(1)}, u32[]{:S(2)}, u32[]{:S(2)}) %collective-permute-start.11) | collective-permute-done | bytes 12320 | tf_op jit(solution)/shard_map/ppermute | solution.py:230
  24.3 0.0 collective-permute-done.10.refs_2_
  24.3 0.0 collective-permute-done.9.refs_1_
  24.3 0.2 collective-permute-done.8.refs_0_
  24.5 0.6 %place.1 = bf16[16,1536]{1,0:T(8,128)(2,1)} custom-call(bf16[16,384]{1,0:T(8,128)(2,1)S(1)} %collective-permute-done.8.refs_0_, bf16[16,384]{1,0:T(8,128)(2,1)S(1)} %collective-permute-done.9.refs_1_, bf16[16,384]{1,0:T(8,128)(2,1)S(1)} %collective-permute-done.10.refs_2_, bf16[16,384]{1,0:T(8,128)(2,1)S(1)} %collective-permute-done.11.refs_3_), custom_call_target="tpu_custom_call" | custom-call | tf_op jit(solution)/shard_map/place/pallas_call | solution.py:112
  (3 shorter events, 0.0 us)
Async XLA Ops:
  0.8 9.6 %copy-start.2 = (bf16[384,1536]{1,0:T(8,128)(2,1)S(1)}, bf16[384,1536]{1,0:T(8,128)(2,1)}, u32[]{:S(2)}) copy-start(bf16[384,1536]{1,0:T(8,128)(2,1)} %weight.1) | copy-start | bytes 3538948
  0.8 13.4 %copy-start.1 = (bf16[512,1536]{1,0:T(8,128)(2,1)S(1)}, bf16[512,1536]{1,0:T(8,128)(2,1)}, u32[]{:S(2)}) copy-start(bf16[512,1536]{1,0:T(8,128)(2,1)} %refs_8_.1) | copy-start | bytes 4718596
  0.8 13.4 %copy-start = (bf16[512,1536]{1,0:T(8,128)(2,1)S(1)}, bf16[512,1536]{1,0:T(8,128)(2,1)}, u32[]{:S(2)}) copy-start(bf16[512,1536]{1,0:T(8,128)(2,1)} %refs_7_.1) | copy-start | bytes 4718596
  0.9 5.7 %collective-permute-start.2 = (bf16[16,2048]{1,0:T(8,128)(2,1)S(1)}, bf16[16,2048]{1,0:T(8,128)(2,1)S(1)}, u32[]{:S(2)}, u32[]{:S(2)}) collective-permute-start(bf16[16,2048]{1,0:T(8,128)(2,1)S(1)} %pack.1.own), channel_id=1, source_target_pairs={{0,2},{1,3},{2,0},{3,1},{4,6},{5,7},{6,4},{7,5},{8,10},{9,11},{10,... | collective-permute-start | bytes 196616 | tf_op jit(solution)/shard_map/ppermute | solution.py:216
  3.0 7.2 %collective-permute-start = (bf16[16,2048]{1,0:T(8,128)(2,1)S(1)}, bf16[16,2048]{1,0:T(8,128)(2,1)S(1)}, u32[]{:S(2)}, u32[]{:S(2)}) collective-permute-start(bf16[16,2048]{1,0:T(8,128)(2,1)S(1)} %pack.1.own), channel_id=1, source_target_pairs={{0,12},{1,13},{2,14},{3,15},{4,8},{5,9},{6,10},{7,11},{8,4},{9,5},... | collective-permute-start | bytes 196616 | tf_op jit(solution)/shard_map/ppermute | solution.py:216
  6.3 5.5 %collective-permute-start.6 = (bf16[16,2048]{1,0:T(8,128)(2,1)S(1)}, bf16[16,2048]{1,0:T(8,128)(2,1)S(1)}, u32[]{:S(2)}, u32[]{:S(2)}) collective-permute-start(bf16[16,2048]{1,0:T(8,128)(2,1)S(1)} %pack.1.own), channel_id=1, source_target_pairs={{0,8},{1,9},{2,10},{3,11},{4,12},{5,13},{6,14},{7,15},{8,0},{9,1},... | collective-permute-start | bytes 196616 | tf_op jit(solution)/shard_map/ppermute | solution.py:216
  6.3 5.5 %collective-permute-start.5 = (bf16[16,2048]{1,0:T(8,128)(2,1)S(1)}, bf16[16,2048]{1,0:T(8,128)(2,1)S(1)}, u32[]{:S(2)}, u32[]{:S(2)}) collective-permute-start(bf16[16,2048]{1,0:T(8,128)(2,1)S(1)} %pack.1.own), channel_id=1, source_target_pairs={{0,4},{1,5},{2,6},{3,7},{4,0},{5,1},{6,2},{7,3},{8,12},{9,13},{10,... | collective-permute-start | bytes 196616 | tf_op jit(solution)/shard_map/ppermute | solution.py:216
  6.6 7.4 %collective-permute-start.4 = (bf16[16,2048]{1,0:T(8,128)(2,1)S(1)}, bf16[16,2048]{1,0:T(8,128)(2,1)S(1)}, u32[]{:S(2)}, u32[]{:S(2)}) collective-permute-start(bf16[16,2048]{1,0:T(8,128)(2,1)S(1)} %collective-permute-done.2.refs_6_), channel_id=1, source_target_pairs={{0,8},{1,9},{2,10},{3,11},{4,12},{5,13},{6,14},{7,15},{8,0},{9,1},... | collective-permute-start | bytes 196616 | tf_op jit(solution)/shard_map/ppermute | solution.py:216
  8.7 5.6 %collective-permute-start.3 = (bf16[16,2048]{1,0:T(8,128)(2,1)S(1)}, bf16[16,2048]{1,0:T(8,128)(2,1)S(1)}, u32[]{:S(2)}, u32[]{:S(2)}) collective-permute-start(bf16[16,2048]{1,0:T(8,128)(2,1)S(1)} %collective-permute-done.2.refs_6_), channel_id=1, source_target_pairs={{0,4},{1,5},{2,6},{3,7},{4,0},{5,1},{6,2},{7,3},{8,12},{9,13},{10,... | collective-permute-start | bytes 196616 | tf_op jit(solution)/shard_map/ppermute | solution.py:216
  10.1 4.1 %collective-permute-start.1 = (bf16[16,2048]{1,0:T(8,128)(2,1)S(1)}, bf16[16,2048]{1,0:T(8,128)(2,1)S(1)}, u32[]{:S(2)}, u32[]{:S(2)}) collective-permute-start(bf16[16,2048]{1,0:T(8,128)(2,1)S(1)} %collective-permute-done.refs_5_), channel_id=1, source_target_pairs={{0,2},{1,3},{2,0},{3,1},{4,6},{5,7},{6,4},{7,5},{8,10},{9,11},{10,... | collective-permute-start | bytes 196616 | tf_op jit(solution)/shard_map/ppermute | solution.py:216
  15.5 3.4 %collective-permute-start.7 = (bf16[64,384]{1,0:T(8,128)(2,1)S(1)}, bf16[64,384]{1,0:T(8,128)(2,1)S(1)}, u32[]{:S(2)}, u32[]{:S(2)}) collective-permute-start(bf16[64,384]{1,0:T(8,128)(2,1)S(1)} %get-tuple-element.8), channel_id=1, source_target_pairs={{0,1},{1,0},{2,3},{3,2},{4,5},{5,4},{6,7},{7,6},{8,9},{9,8},{10,11... | collective-permute-start | bytes 147464 | tf_op jit(solution)/shard_map/ppermute | solution.py:227
  19.0 5.3 %collective-permute-start.11 = (bf16[16,384]{1,0:T(8,128)(2,1)S(1)}, bf16[16,384]{1,0:T(8,128)(2,1)S(1)}, u32[]{:S(2)}, u32[]{:S(2)}) collective-permute-start(bf16[16,384]{1,0:T(8,128)(2,1)S(1)} %get-tuple-element.9), channel_id=1, source_target_pairs={{0,6},{1,10},{2,0},{3,2},{4,8},{5,12},{6,4},{7,14},{8,11},{9,3},{1... | collective-permute-start | bytes 36872 | tf_op jit(solution)/shard_map/ppermute | solution.py:230
  19.4 4.9 %collective-permute-start.10 = (bf16[16,384]{1,0:T(8,128)(2,1)S(1)}, bf16[16,384]{1,0:T(8,128)(2,1)S(1)}, u32[]{:S(2)}, u32[]{:S(2)}) collective-permute-start(bf16[16,384]{1,0:T(8,128)(2,1)S(1)} %get-tuple-element.10), channel_id=1, source_target_pairs={{0,14},{1,8},{2,12},{3,4},{4,6},{5,2},{6,10},{7,0},{8,9},{9,5},{10... | collective-permute-start | bytes 36872 | tf_op jit(solution)/shard_map/ppermute | solution.py:230
  19.8 4.6 %collective-permute-start.9 = (bf16[16,384]{1,0:T(8,128)(2,1)S(1)}, bf16[16,384]{1,0:T(8,128)(2,1)S(1)}, u32[]{:S(2)}, u32[]{:S(2)}) collective-permute-start(bf16[16,384]{1,0:T(8,128)(2,1)S(1)} %get-tuple-element.11), channel_id=1, source_target_pairs={{0,12},{1,4},{2,10},{3,8},{4,14},{5,0},{6,2},{7,6},{8,7},{9,13},{1... | collective-permute-start | bytes 36872 | tf_op jit(solution)/shard_map/ppermute | solution.py:230
  21.1 3.5 %collective-permute-start.8 = (bf16[16,384]{1,0:T(8,128)(2,1)S(1)}, bf16[16,384]{1,0:T(8,128)(2,1)S(1)}, u32[]{:S(2)}, u32[]{:S(2)}) collective-permute-start(bf16[16,384]{1,0:T(8,128)(2,1)S(1)} %get-tuple-element.12), channel_id=1, source_target_pairs={{0,2},{1,0},{2,6},{3,14},{4,10},{5,4},{6,8},{7,12},{8,15},{9,1},{1... | collective-permute-start | bytes 36872 | tf_op jit(solution)/shard_map/ppermute | solution.py:230

commit v9 on v6

--- a/solution.py
+++ b/solution.py
@@ -147,14 +147,14 @@
                 (2, 1, 1),
             )
             self.ways = (
-                ((3, 7, 6, 1), (5, 4, 2, 0)),
-                ((0, 6, 5, 3), (1, 2, 4, 7)),
-                ((4, 3, 7, 5), (6, 1, 0, 2)),
-                ((2, 5, 1, 4), (7, 0, 3, 6)),
-                ((5, 4, 3, 7), (1, 2, 6, 0)),
-                ((7, 6, 4, 5), (2, 3, 0, 1)),
-                ((6, 1, 5, 3), (4, 0, 7, 2)),
-                ((3, 7, 1, 6), (0, 5, 2, 4)),
+                ((4, 7, 6, 2), (3, 5, 1, 0)),
+                ((5, 4, 3, 7), (1, 0, 2, 6)),
+                ((7, 1, 5, 3), (6, 2, 0, 4)),
+                ((0, 6, 4, 5), (2, 3, 7, 1)),
+                ((4, 1, 7, 5), (6, 2, 3, 0)),
+                ((5, 7, 2, 3), (0, 6, 4, 1)),
+                ((7, 4, 0, 6), (1, 3, 5, 2)),
+                ((3, 5, 6, 7), (2, 0, 1, 4)),
             )
         else:
             inner = range(1, self.half)

time: 25.6 us -> 25.6 us (level)
  waiting for transfers between devices: 5.67 us -> 6.21 us
  starting transfers between devices: 16.4 us -> 15.9 us
    ppermute x4, waiting for transfers between devices: 1.21 us -> 1.76 us  [direct(): lax.ppermute(total[step * rows:(step + 1) * rows], ('seq', 'head'), plan....]
    ppermute x4, starting transfers between devices: 4.32 us -> 3.86 us  [direct(): lax.ppermute(total[step * rows:(step + 1) * rows], ('seq', 'head'), plan....]
  transfers between devices with their start and end apart: 12 -> 12, of which waited for: 6 -> 8; matrix products, arithmetic and copies ran while one was open for 0% -> 0% of each run, Pallas kernels for 1% -> 1%
where the time goes in v9:
time: 25.6 us; the launch traced here: 25.3 us
  starting transfers between devices  15.9 us (62%)
  waiting for transfers between devices  6.21 us (24%)
  Pallas kernels  2.27 us (9%)
  other arithmetic  0.83 us (3%)
    ppermute x7, starting transfers between devices, gather(): blocks.append(lax.ppermute(blocks[block], ('seq', 'head'), plan.out(flips)))  9.51 us
    ppermute x4, starting transfers between devices, direct(): lax.ppermute(total[step * rows:(step + 1) * rows], ('seq', 'head'), plan....  3.86 us
    ppermute x7, waiting for transfers between devices, gather(): blocks.append(lax.ppermute(blocks[block], ('seq', 'head'), plan.out(flips)))  3.51 us
    ppermute x1, starting transfers between devices, direct(): other = lax.ppermute(send, 'head', [(0, 1), (1, 0)])  2.56 us
    ppermute x4, waiting for transfers between devices, direct(): lax.ppermute(total[step * rows:(step + 1) * rows], ('seq', 'head'), plan....  1.76 us
    pallas_call x1, Pallas kernels, mix(): pl.pallas_call(functools.partial(mix_kernel, plan), out_shape=[jax.ShapeD...  1.28 us
    ppermute x1, waiting for transfers between devices, direct(): other = lax.ppermute(send, 'head', [(0, 1), (1, 0)])  0.94 us
    concatenate x1, other arithmetic, direct(): own = jnp.concatenate([queries, latent.T], axis=1)  0.82 us
  transfers between devices with their start and end apart: 12, of which 8 were waited for; matrix products, arithmetic and copies ran while one was open for 0% of the time, Pallas kernels for 1%

profile of v9, /device:TPU:1, one launch (start us, length us, event | category | flops | bytes accessed | tf_op | source)
XLA Modules:
  0.0 25.3 jit_solution(9963841723696561055)
XLA Ops:
  0.0 0.8 %pad_maximum_fusion.block = bf16[16,2048]{1,0:T(8,128)(2,1)S(1)} fusion(bf16[16,512]{1,0:T(8,128)(2,1)} %bitcast.1, bf16[16,1536]{1,0:T(8,128)(2,1)} %param.5), kind=kLoop, calls=%fused_computation.1 | loop fusion | flops 131072 | bytes 131072 | tf_op jit(solution)/shard_map/concatenate | solution.py:218
  0.8 0.0 copy-start.2
  0.8 0.0 copy-start.1
  0.8 0.0 copy-start
  0.9 2.1 %collective-permute-start.2 = (bf16[16,2048]{1,0:T(8,128)(2,1)S(1)}, bf16[16,2048]{1,0:T(8,128)(2,1)S(1)}, u32[]{:S(2)}, u32[]{:S(2)}) collective-permute-start(bf16[16,2048]{1,0:T(8,128)(2,1)S(1)} %pack.1.own), channel_id=1, source_target_pairs={{0,2},{1,3},{2,0},{3,1},{4,6},{5,7},{6,4},{7,5},{8,10},{9,11},{10,... | collective-permute-start | bytes 196616 | tf_op jit(solution)/shard_map/ppermute | solution.py:211
  3.0 3.3 %collective-permute-start = (bf16[16,2048]{1,0:T(8,128)(2,1)S(1)}, bf16[16,2048]{1,0:T(8,128)(2,1)S(1)}, u32[]{:S(2)}, u32[]{:S(2)}) collective-permute-start(bf16[16,2048]{1,0:T(8,128)(2,1)S(1)} %pack.1.own), channel_id=1, source_target_pairs={{0,12},{1,13},{2,14},{3,15},{4,8},{5,9},{6,10},{7,11},{8,4},{9,5},... | collective-permute-start | bytes 196616 | tf_op jit(solution)/shard_map/ppermute | solution.py:211
  6.3 0.0 collective-permute-start.6
  6.3 0.3 %collective-permute-start.5 = (bf16[16,2048]{1,0:T(8,128)(2,1)S(1)}, bf16[16,2048]{1,0:T(8,128)(2,1)S(1)}, u32[]{:S(2)}, u32[]{:S(2)}) collective-permute-start(bf16[16,2048]{1,0:T(8,128)(2,1)S(1)} %pack.1.own), channel_id=1, source_target_pairs={{0,4},{1,5},{2,6},{3,7},{4,0},{5,1},{6,2},{7,3},{8,12},{9,13},{10,... | collective-permute-start | bytes 196616 | tf_op jit(solution)/shard_map/ppermute | solution.py:211
  6.6 0.0 collective-permute-done.2.refs_6_
  6.6 2.1 %collective-permute-start.4 = (bf16[16,2048]{1,0:T(8,128)(2,1)S(1)}, bf16[16,2048]{1,0:T(8,128)(2,1)S(1)}, u32[]{:S(2)}, u32[]{:S(2)}) collective-permute-start(bf16[16,2048]{1,0:T(8,128)(2,1)S(1)} %collective-permute-done.2.refs_6_), channel_id=1, source_target_pairs={{0,8},{1,9},{2,10},{3,11},{4,12},{5,13},{6,14},{7,15},{8,0},{9,1},... | collective-permute-start | bytes 196616 | tf_op jit(solution)/shard_map/ppermute | solution.py:211
  8.7 1.5 %collective-permute-start.3 = (bf16[16,2048]{1,0:T(8,128)(2,1)S(1)}, bf16[16,2048]{1,0:T(8,128)(2,1)S(1)}, u32[]{:S(2)}, u32[]{:S(2)}) collective-permute-start(bf16[16,2048]{1,0:T(8,128)(2,1)S(1)} %collective-permute-done.2.refs_6_), channel_id=1, source_target_pairs={{0,4},{1,5},{2,6},{3,7},{4,0},{5,1},{6,2},{7,3},{8,12},{9,13},{10,... | collective-permute-start | bytes 196616 | tf_op jit(solution)/shard_map/ppermute | solution.py:211
  10.1 0.0 collective-permute-done.refs_5_
  10.1 0.3 %collective-permute-start.1 = (bf16[16,2048]{1,0:T(8,128)(2,1)S(1)}, bf16[16,2048]{1,0:T(8,128)(2,1)S(1)}, u32[]{:S(2)}, u32[]{:S(2)}) collective-permute-start(bf16[16,2048]{1,0:T(8,128)(2,1)S(1)} %collective-permute-done.refs_5_), channel_id=1, source_target_pairs={{0,2},{1,3},{2,0},{3,1},{4,6},{5,7},{6,4},{7,5},{8,10},{9,11},{10,... | collective-permute-start | bytes 196616 | tf_op jit(solution)/shard_map/ppermute | solution.py:211
  10.4 0.0 copy-done.2
  10.4 0.4 %turn.1.refs_9_ = bf16[1536,384]{1,0:T(8,128)(2,1)S(1)} custom-call(bf16[384,1536]{1,0:T(8,128)(2,1)S(1)} %copy-done.2), custom_call_target="tpu_custom_call" | custom-call | bytes 2359296 | tf_op jit(solution)/shard_map/turn/pallas_call | solution.py:22
  10.7 1.1 %collective-permute-done.6.refs_4_ = bf16[16,2048]{1,0:T(8,128)(2,1)S(1)} collective-permute-done((bf16[16,2048]{1,0:T(8,128)(2,1)S(1)}, bf16[16,2048]{1,0:T(8,128)(2,1)S(1)}, u32[]{:S(2)}, u32[]{:S(2)}) %collective-permute-start.6) | collective-permute-done | bytes 65568 | tf_op jit(solution)/shard_map/ppermute | solution.py:211
  11.8 0.0 collective-permute-done.5.refs_3_
  11.8 2.1 %collective-permute-done.4.refs_2_ = bf16[16,2048]{1,0:T(8,128)(2,1)S(1)} collective-permute-done((bf16[16,2048]{1,0:T(8,128)(2,1)S(1)}, bf16[16,2048]{1,0:T(8,128)(2,1)S(1)}, u32[]{:S(2)}, u32[]{:S(2)}) %collective-permute-start.4) | collective-permute-done | bytes 65568 | tf_op jit(solution)/shard_map/ppermute | solution.py:211
  14.0 0.3 %collective-permute-done.3.refs_1_ = bf16[16,2048]{1,0:T(8,128)(2,1)S(1)} collective-permute-done((bf16[16,2048]{1,0:T(8,128)(2,1)S(1)}, bf16[16,2048]{1,0:T(8,128)(2,1)S(1)}, u32[]{:S(2)}, u32[]{:S(2)}) %collective-permute-start.3) | collective-permute-done | bytes 65568 | tf_op jit(solution)/shard_map/ppermute | solution.py:211
  14.2 0.0 collective-permute-done.1.refs_0_
  14.2 0.0 copy-done.1
  14.3 0.0 copy-done
  14.3 1.3 %mix.1 = (f32[64,384]{1,0:T(8,128)S(1)}, f32[64,384]{1,0:T(8,128)S(1)}) custom-call(bf16[16,2048]{1,0:T(8,128)(2,1)S(1)} %pack.1.own, bf16[16,2048]{1,0:T(8,128)(2,1)S(1)} %collective-permute-done.1.refs_0_, bf16[16,2048]{1,0:T(8,128)(2,1)S(1)} %collective-permute-done.3.refs_1_, bf16[16,2048]{1,0:T(8,128)(2,1)S(1)} %collective-permute-done.4.refs_2_, ...), custom_call_target="tpu_custom_call" | custom-call | flops 654311424 | bytes 4325376 | tf_op jit(solution)/shard_map/mix/pallas_call | solution.py:77
  15.5 2.6 %collective-permute-start.7 = (f32[64,384]{1,0:T(8,128)S(1)}, f32[64,384]{1,0:T(8,128)S(1)}, u32[]{:S(2)}, u32[]{:S(2)}) collective-permute-start(f32[64,384]{1,0:T(8,128)S(1)} %get-tuple-element.8), channel_id=1, source_target_pairs={{0,1},{1,0},{2,3},{3,2},{4,5},{5,4},{6,7},{7,6},{8,9},{9,8},{10,11... | collective-permute-start | bytes 294920 | tf_op jit(solution)/shard_map/ppermute | solution.py:222
  18.1 0.9 %collective-permute-done.7 = f32[64,384]{1,0:T(8,128)S(1)} collective-permute-done((f32[64,384]{1,0:T(8,128)S(1)}, f32[64,384]{1,0:T(8,128)S(1)}, u32[]{:S(2)}, u32[]{:S(2)}) %collective-permute-start.7) | collective-permute-done | bytes 98336 | tf_op jit(solution)/shard_map/ppermute | solution.py:222
  19.1 0.1 collective-permute-start.11
  19.2 0.5 %collective-permute-start.10 = (bf16[16,384]{1,0:T(8,128)(2,1)S(1)}, bf16[16,384]{1,0:T(8,128)(2,1)S(1)}, u32[]{:S(2)}, u32[]{:S(2)}) collective-permute-start(bf16[16,384]{1,0:T(8,128)(2,1)S(1)} %get-tuple-element.10), channel_id=1, source_target_pairs={{0,14},{1,10},{2,8},{3,0},{4,2},{5,4},{6,12},{7,6},{8,3},{9,5},{10... | collective-permute-start | bytes 36872 | tf_op jit(solution)/shard_map/ppermute | solution.py:225
  19.7 1.5 %collective-permute-start.9 = (bf16[16,384]{1,0:T(8,128)(2,1)S(1)}, bf16[16,384]{1,0:T(8,128)(2,1)S(1)}, u32[]{:S(2)}, u32[]{:S(2)}) collective-permute-start(bf16[16,384]{1,0:T(8,128)(2,1)S(1)} %get-tuple-element.11), channel_id=1, source_target_pairs={{0,12},{1,2},{2,6},{3,4},{4,10},{5,0},{6,8},{7,14},{8,15},{9,7},{1... | collective-permute-start | bytes 36872 | tf_op jit(solution)/shard_map/ppermute | solution.py:225
  21.2 1.8 %collective-permute-start.8 = (bf16[16,384]{1,0:T(8,128)(2,1)S(1)}, bf16[16,384]{1,0:T(8,128)(2,1)S(1)}, u32[]{:S(2)}, u32[]{:S(2)}) collective-permute-start(bf16[16,384]{1,0:T(8,128)(2,1)S(1)} %get-tuple-element.12), channel_id=1, source_target_pairs={{0,4},{1,0},{2,14},{3,12},{4,6},{5,8},{6,10},{7,2},{8,11},{9,1},{1... | collective-permute-start | bytes 36872 | tf_op jit(solution)/shard_map/ppermute | solution.py:225
  22.9 0.6 %collective-permute-done.11.refs_3_ = bf16[16,384]{1,0:T(8,128)(2,1)S(1)} collective-permute-done((bf16[16,384]{1,0:T(8,128)(2,1)S(1)}, bf16[16,384]{1,0:T(8,128)(2,1)S(1)}, u32[]{:S(2)}, u32[]{:S(2)}) %collective-permute-start.11) | collective-permute-done | bytes 12320 | tf_op jit(solution)/shard_map/ppermute | solution.py:225
  23.5 0.9 %collective-permute-done.10.refs_2_ = bf16[16,384]{1,0:T(8,128)(2,1)S(1)} collective-permute-done((bf16[16,384]{1,0:T(8,128)(2,1)S(1)}, bf16[16,384]{1,0:T(8,128)(2,1)S(1)}, u32[]{:S(2)}, u32[]{:S(2)}) %collective-permute-start.10) | collective-permute-done | bytes 12320 | tf_op jit(solution)/shard_map/ppermute | solution.py:225
  24.5 0.1 collective-permute-done.9.refs_1_
  24.6 0.1 collective-permute-done.8.refs_0_
  24.7 0.6 %place.1 = bf16[16,1536]{1,0:T(8,128)(2,1)} custom-call(bf16[16,384]{1,0:T(8,128)(2,1)S(1)} %collective-permute-done.8.refs_0_, bf16[16,384]{1,0:T(8,128)(2,1)S(1)} %collective-permute-done.9.refs_1_, bf16[16,384]{1,0:T(8,128)(2,1)S(1)} %collective-permute-done.10.refs_2_, bf16[16,384]{1,0:T(8,128)(2,1)S(1)} %collective-permute-done.11.refs_3_), custom_call_target="tpu_custom_call" | custom-call | tf_op jit(solution)/shard_map/place/pallas_call | solution.py:107
  (3 shorter events, 0.0 us)
Async XLA Ops:
  0.8 9.6 %copy-start.2 = (bf16[384,1536]{1,0:T(8,128)(2,1)S(1)}, bf16[384,1536]{1,0:T(8,128)(2,1)}, u32[]{:S(2)}) copy-start(bf16[384,1536]{1,0:T(8,128)(2,1)} %weight.1) | copy-start | bytes 3538948
  0.8 13.4 %copy-start.1 = (bf16[512,1536]{1,0:T(8,128)(2,1)S(1)}, bf16[512,1536]{1,0:T(8,128)(2,1)}, u32[]{:S(2)}) copy-start(bf16[512,1536]{1,0:T(8,128)(2,1)} %refs_8_.1) | copy-start | bytes 4718596
  0.8 13.4 %copy-start = (bf16[512,1536]{1,0:T(8,128)(2,1)S(1)}, bf16[512,1536]{1,0:T(8,128)(2,1)}, u32[]{:S(2)}) copy-start(bf16[512,1536]{1,0:T(8,128)(2,1)} %refs_7_.1) | copy-start | bytes 4718596
  0.9 5.7 %collective-permute-start.2 = (bf16[16,2048]{1,0:T(8,128)(2,1)S(1)}, bf16[16,2048]{1,0:T(8,128)(2,1)S(1)}, u32[]{:S(2)}, u32[]{:S(2)}) collective-permute-start(bf16[16,2048]{1,0:T(8,128)(2,1)S(1)} %pack.1.own), channel_id=1, source_target_pairs={{0,2},{1,3},{2,0},{3,1},{4,6},{5,7},{6,4},{7,5},{8,10},{9,11},{10,... | collective-permute-start | bytes 196616 | tf_op jit(solution)/shard_map/ppermute | solution.py:211
  3.0 7.2 %collective-permute-start = (bf16[16,2048]{1,0:T(8,128)(2,1)S(1)}, bf16[16,2048]{1,0:T(8,128)(2,1)S(1)}, u32[]{:S(2)}, u32[]{:S(2)}) collective-permute-start(bf16[16,2048]{1,0:T(8,128)(2,1)S(1)} %pack.1.own), channel_id=1, source_target_pairs={{0,12},{1,13},{2,14},{3,15},{4,8},{5,9},{6,10},{7,11},{8,4},{9,5},... | collective-permute-start | bytes 196616 | tf_op jit(solution)/shard_map/ppermute | solution.py:211
  6.3 5.5 %collective-permute-start.6 = (bf16[16,2048]{1,0:T(8,128)(2,1)S(1)}, bf16[16,2048]{1,0:T(8,128)(2,1)S(1)}, u32[]{:S(2)}, u32[]{:S(2)}) collective-permute-start(bf16[16,2048]{1,0:T(8,128)(2,1)S(1)} %pack.1.own), channel_id=1, source_target_pairs={{0,8},{1,9},{2,10},{3,11},{4,12},{5,13},{6,14},{7,15},{8,0},{9,1},... | collective-permute-start | bytes 196616 | tf_op jit(solution)/shard_map/ppermute | solution.py:211
  6.3 5.5 %collective-permute-start.5 = (bf16[16,2048]{1,0:T(8,128)(2,1)S(1)}, bf16[16,2048]{1,0:T(8,128)(2,1)S(1)}, u32[]{:S(2)}, u32[]{:S(2)}) collective-permute-start(bf16[16,2048]{1,0:T(8,128)(2,1)S(1)} %pack.1.own), channel_id=1, source_target_pairs={{0,4},{1,5},{2,6},{3,7},{4,0},{5,1},{6,2},{7,3},{8,12},{9,13},{10,... | collective-permute-start | bytes 196616 | tf_op jit(solution)/shard_map/ppermute | solution.py:211
  6.6 7.4 %collective-permute-start.4 = (bf16[16,2048]{1,0:T(8,128)(2,1)S(1)}, bf16[16,2048]{1,0:T(8,128)(2,1)S(1)}, u32[]{:S(2)}, u32[]{:S(2)}) collective-permute-start(bf16[16,2048]{1,0:T(8,128)(2,1)S(1)} %collective-permute-done.2.refs_6_), channel_id=1, source_target_pairs={{0,8},{1,9},{2,10},{3,11},{4,12},{5,13},{6,14},{7,15},{8,0},{9,1},... | collective-permute-start | bytes 196616 | tf_op jit(solution)/shard_map/ppermute | solution.py:211
  8.7 5.6 %collective-permute-start.3 = (bf16[16,2048]{1,0:T(8,128)(2,1)S(1)}, bf16[16,2048]{1,0:T(8,128)(2,1)S(1)}, u32[]{:S(2)}, u32[]{:S(2)}) collective-permute-start(bf16[16,2048]{1,0:T(8,128)(2,1)S(1)} %collective-permute-done.2.refs_6_), channel_id=1, source_target_pairs={{0,4},{1,5},{2,6},{3,7},{4,0},{5,1},{6,2},{7,3},{8,12},{9,13},{10,... | collective-permute-start | bytes 196616 | tf_op jit(solution)/shard_map/ppermute | solution.py:211
  10.1 4.1 %collective-permute-start.1 = (bf16[16,2048]{1,0:T(8,128)(2,1)S(1)}, bf16[16,2048]{1,0:T(8,128)(2,1)S(1)}, u32[]{:S(2)}, u32[]{:S(2)}) collective-permute-start(bf16[16,2048]{1,0:T(8,128)(2,1)S(1)} %collective-permute-done.refs_5_), channel_id=1, source_target_pairs={{0,2},{1,3},{2,0},{3,1},{4,6},{5,7},{6,4},{7,5},{8,10},{9,11},{10,... | collective-permute-start | bytes 196616 | tf_op jit(solution)/shard_map/ppermute | solution.py:211
  15.5 3.5 %collective-permute-start.7 = (f32[64,384]{1,0:T(8,128)S(1)}, f32[64,384]{1,0:T(8,128)S(1)}, u32[]{:S(2)}, u32[]{:S(2)}) collective-permute-start(f32[64,384]{1,0:T(8,128)S(1)} %get-tuple-element.8), channel_id=1, source_target_pairs={{0,1},{1,0},{2,3},{3,2},{4,5},{5,4},{6,7},{7,6},{8,9},{9,8},{10,11... | collective-permute-start | bytes 294920 | tf_op jit(solution)/shard_map/ppermute | solution.py:222
  19.1 4.5 %collective-permute-start.11 = (bf16[16,384]{1,0:T(8,128)(2,1)S(1)}, bf16[16,384]{1,0:T(8,128)(2,1)S(1)}, u32[]{:S(2)}, u32[]{:S(2)}) collective-permute-start(bf16[16,384]{1,0:T(8,128)(2,1)S(1)} %get-tuple-element.9), channel_id=1, source_target_pairs={{0,8},{1,6},{2,10},{3,2},{4,14},{5,12},{6,0},{7,4},{8,9},{9,13},{1... | collective-permute-start | bytes 36872 | tf_op jit(solution)/shard_map/ppermute | solution.py:225
  19.2 5.3 %collective-permute-start.10 = (bf16[16,384]{1,0:T(8,128)(2,1)S(1)}, bf16[16,384]{1,0:T(8,128)(2,1)S(1)}, u32[]{:S(2)}, u32[]{:S(2)}) collective-permute-start(bf16[16,384]{1,0:T(8,128)(2,1)S(1)} %get-tuple-element.10), channel_id=1, source_target_pairs={{0,14},{1,10},{2,8},{3,0},{4,2},{5,4},{6,12},{7,6},{8,3},{9,5},{10... | collective-permute-start | bytes 36872 | tf_op jit(solution)/shard_map/ppermute | solution.py:225
  19.7 4.9 %collective-permute-start.9 = (bf16[16,384]{1,0:T(8,128)(2,1)S(1)}, bf16[16,384]{1,0:T(8,128)(2,1)S(1)}, u32[]{:S(2)}, u32[]{:S(2)}) collective-permute-start(bf16[16,384]{1,0:T(8,128)(2,1)S(1)} %get-tuple-element.11), channel_id=1, source_target_pairs={{0,12},{1,2},{2,6},{3,4},{4,10},{5,0},{6,8},{7,14},{8,15},{9,7},{1... | collective-permute-start | bytes 36872 | tf_op jit(solution)/shard_map/ppermute | solution.py:225
  21.2 3.6 %collective-permute-start.8 = (bf16[16,384]{1,0:T(8,128)(2,1)S(1)}, bf16[16,384]{1,0:T(8,128)(2,1)S(1)}, u32[]{:S(2)}, u32[]{:S(2)}) collective-permute-start(bf16[16,384]{1,0:T(8,128)(2,1)S(1)} %get-tuple-element.12), channel_id=1, source_target_pairs={{0,4},{1,0},{2,14},{3,12},{4,6},{5,8},{6,10},{7,2},{8,11},{9,1},{1... | collective-permute-start | bytes 36872 | tf_op jit(solution)/shard_map/ppermute | solution.py:225
